TPU v7x, 256 devices: a whole 4x4x8 slice. The times are simulated.
256 devices in a mesh: expert: 64 (over x_hi, z, y), tensor: 4 (over x_lo, core).
Axes of the slice: x: 4 (x_hi: 2, x_lo: 2; x = x_hi * 2 + x_lo), y: 4, z: 8, core: 2. Of those that a mesh axis runs over, the one named last changes fastest.
Arguments:
- tokens: bfloat16 [16384, 3584], P(('expert', 'tensor')), may hold values from -6 to 6
- expert_ids: int32 [16384, 2], P(('expert', 'tensor')), may hold values from 0 to 63, all different within a row; in each aligned block of 256 rows (0 to 255, 256 to 511, ...) at most 10 rows name the same one
- gate_codes: int32 [16384, 2], P(('expert', 'tensor')), may hold values from 1 to 1023
- dense_up: bfloat16 [3584, 2560], P('expert', 'tensor'), may hold values from -0.09375 to 0.09375
- dense_down: bfloat16 [2560, 3584], P('tensor', 'expert'), may hold values from -0.125 to 0.125
- expert_in: bfloat16 [64, 3584, 2560], P('expert', None, 'tensor'), may hold values from -0.09375 to 0.09375
- expert_out: bfloat16 [64, 2560, 3584], P('expert', 'tensor'), may hold values from -0.125 to 0.125
Outputs:
- layer_out: bfloat16 [16384, 3584], P(('expert', 'tensor'))
Inputs may be any that keep to these rules, and one draw needn't show every extreme that they name: `expert_ids`: the two ids of a token differ. In each aligned block of 256 rows no expert is named by more than 10 rows, and in some block one expert is named by exactly 10 rows. Every expert is named somewhere.
All inputs are finite; a program needn't handle non-finite values.
Results may differ from a plain program's by a relative error of at most 0.014.
Values may be sent and summed in bfloat16 or wider, within the bound.
No kernel may reach another device: no remote copies, remote signals or barrier semaphores. Data moves between devices by JAX's collectives and lax.ppermute only.
A program may use at most 192 MiB of HBM per device.

v0:
```python
import jax
import jax.numpy as jnp
from jax import lax
from jax.sharding import PartitionSpec as P


def local(tokens, expert_ids, gate_codes, dense_up, dense_down, expert_in, expert_out):
    f32 = jnp.float32
    width = tokens.shape[1]
    place = lax.axis_index("tensor")
    rows_own = tokens.shape[0]
    grouped, group_ids, group_codes = (
        lax.all_gather(tokens, "tensor", axis=0, tiled=True),
        lax.all_gather(expert_ids, "tensor", axis=0, tiled=True),
        lax.all_gather(gate_codes, "tensor", axis=0, tiled=True),
    )
    group_len = grouped.shape[0]
    experts_all = lax.axis_size("expert") * expert_in.shape[0]
    capacity = 5 * group_len // (2 * experts_all)
    dense_pre = jnp.dot(
        grouped, lax.all_gather(dense_up, "expert", axis=0, tiled=True), preferred_element_type=f32
    )
    dense_hidden = jax.nn.silu(dense_pre).astype(jnp.bfloat16)
    dense_part = jnp.dot(
        dense_hidden,
        lax.all_gather(dense_down, "expert", axis=1, tiled=True),
        preferred_element_type=f32,
    )
    pairs = group_ids.reshape(-1).astype(jnp.int32)
    onehot = (pairs[:, None] == jnp.arange(experts_all, dtype=jnp.int32)[None, :]).astype(jnp.int32)
    before = jnp.cumsum(onehot, axis=0) - onehot
    slot = jnp.sum(before * onehot, axis=1)
    target = pairs * capacity + slot
    placed = jnp.arange(experts_all * capacity, dtype=jnp.int32)[:, None] == target[None, :]
    placed = placed.reshape(experts_all * capacity, group_len, 2).any(axis=2).astype(jnp.bfloat16)
    codes = group_codes.astype(f32)
    gates = codes / jnp.sum(codes, axis=1, keepdims=True)
    w_first = expert_in[0]
    w_second = expert_out[0]
    outgoing = jnp.dot(placed, grouped, preferred_element_type=f32).astype(jnp.bfloat16)
    outgoing = outgoing.reshape(experts_all, capacity, width)
    received = lax.all_to_all(outgoing, "expert", split_axis=0, concat_axis=0, tiled=True)
    sources = received.shape[0]
    count = received.shape[1]
    flat = received.reshape(sources * count, width)
    hidden = jax.nn.silu(jnp.dot(flat, w_first, preferred_element_type=f32)).astype(jnp.bfloat16)
    result = jnp.dot(hidden, w_second, preferred_element_type=f32).astype(jnp.bfloat16)
    returned = lax.all_to_all(
        result.reshape(sources, count, width), "expert", split_axis=0, concat_axis=0, tiled=True
    )
    picked = returned.reshape(experts_all * capacity, width)[target].astype(f32)
    picked = picked.reshape(group_len, 2, width)
    total = dense_part + jnp.sum(gates[:, :, None] * picked, axis=1)
    summed_all = lax.psum(total.astype(jnp.bfloat16), "tensor").astype(jnp.float32)
    mine = lax.dynamic_slice_in_dim(summed_all, place * rows_own, rows_own, 0)
    return (tokens.astype(f32) + mine).astype(jnp.bfloat16)


def solution(mesh):
    return jax.shard_map(
        local,
        mesh=mesh,
        in_specs=(
            P(("expert", "tensor"), None),
            P(("expert", "tensor"), None),
            P(("expert", "tensor"), None),
            P("expert", "tensor"),
            P("tensor", "expert"),
            P("expert", None, "tensor"),
            P("expert", "tensor", None),
        ),
        out_specs=P(("expert", "tensor"), None),
        check_vma=False,
    )
```

profile of v0, /device:TPU:1, one launch (start us, length us, event | category | flops | bytes accessed | tf_op | source)
XLA Modules:
  0.0 593.7 jit_solution(13936904945216202189)
XLA Ops:
  7.4 0.0 all-gather.6.cloned.1.call-start
  7.4 0.7 all-gather.6.cloned.1.call-update
  8.1 8.3 %all-gather.1 = s32[4,64,2]{1,2,0:T(2,128)S(1)} all-gather(s32[1,64,2]{1,2,0:T(2,128)} %bitcast.46), channel_id=1, replica_groups=mesh['expert'=64,'tensor'=4] {'tensor'}, dimensions={0}, use_global_device_ids=true | all-gather | bytes 2560 | tf_op jit(solution)/shard_map/all_gather | solution.py:14
  16.4 0.1 copy.41
  16.5 0.1 copy.40
  16.7 0.1 copy.42
  16.8 1.2 reduce-window.6
  18.0 0.2 slice_reduce_fusion
  18.2 0.1 eq.40
  18.4 0.1 fusion.10
  18.5 0.1 reduce_sum.33
  18.7 0.1 copy.44
  18.7 0.1 reshape.104
  18.8 0.2 fusion.6
  19.1 24.7 %all-gather.6.cloned.1.call-done = bf16[256,3584]{1,0:T(8,128)(2,1)} async-done(((bf16[64,3584]{1,0:T(8,128)(2,1)}), bf16[256,3584]{1,0:T(8,128)(2,1)}) %all-gather.6.cloned.1.call-update) | async-done | bytes 1835024 | tf_op jit(solution)/shard_map/all_gather | solution.py:13
  43.7 5.0 convolution_convert_fusion.1
  48.7 7.7 %reshape.82 = bf16[64,10,3584]{2,1,0:T(8,128)(2,1)} reshape(bf16[640,3584]{1,0:T(8,128)(2,1)} %convolution_convert_fusion.1) | data formatting | bytes 9175040 | tf_op jit(solution)/shard_map/reshape | solution.py:41
  56.5 12.5 %all-to-all-start = ((bf16[64,10,3584]{2,1,0:T(8,128)(2,1)}), bf16[64,10,3584]{2,1,0:T(8,128)(2,1)}, u32[]{:S(2)}, u32[]{:S(2)}) async-start(bf16[64,10,3584]{2,1,0:T(8,128)(2,1)} %reshape.82), calls=%async_computation | async-start | bytes 14680064 | tf_op jit(solution)/shard_map/all_to_all | solution.py:42
  69.0 0.0 all-gather.10.cloned.1.call-start
  69.1 0.5 all-gather.10.cloned.1.call-update
  69.6 178.6 %all-to-all-done = bf16[64,10,3584]{2,1,0:T(8,128)(2,1)} async-done(((bf16[64,10,3584]{2,1,0:T(8,128)(2,1)}), bf16[64,10,3584]{2,1,0:T(8,128)(2,1)}, u32[]{:S(2)}, u32[]{:S(2)}) %all-to-all-start) | async-done | bytes 4587552 | tf_op jit(solution)/shard_map/all_to_all | solution.py:42
  248.2 8.0 %reshape.83 = bf16[640,3584]{1,0:T(8,128)(2,1)} reshape(bf16[64,10,3584]{2,1,0:T(8,128)(2,1)} %all-to-all-done) | data formatting | bytes 9175040 | tf_op jit(solution)/shard_map/reshape | solution.py:45
  256.2 7.5 %multiply_convert_fusion = bf16[640,640]{1,0:T(8,128)(2,1)S(1)} fusion(bf16[640,3584]{1,0:T(8,128)(2,1)} %reshape.83, bf16[1,3584,640]{2,1,0:T(8,128)(2,1)} %param.12), kind=kOutput, calls=%fused_computation.9 | convolution fusion | flops 2938060800 | bytes 9994240 | tf_op jit(solution)/shard_map/dot_general | solution.py:46
  263.7 7.7 %convolution_convert_fusion = bf16[640,3584]{1,0:T(8,128)(2,1)} fusion(bf16[640,640]{1,0:T(8,128)(2,1)S(1)} %multiply_convert_fusion, bf16[1,640,3584]{2,1,0:T(8,128)(2,1)} %param.13), kind=kOutput, calls=%fused_computation.2 | convolution fusion | flops 2938306560 | bytes 9994240 | tf_op jit(solution)/shard_map/dot_general | solution.py:47
  271.5 7.8 %reshape.84 = bf16[64,10,3584]{2,1,0:T(8,128)(2,1)} reshape(bf16[640,3584]{1,0:T(8,128)(2,1)} %convolution_convert_fusion) | data formatting | bytes 9175040 | tf_op jit(solution)/shard_map/reshape | solution.py:49
  279.3 0.0 copy-start.2
  279.3 13.6 %all-to-all-start.1 = ((bf16[64,10,3584]{2,1,0:T(8,128)(2,1)}), bf16[64,10,3584]{2,1,0:T(8,128)(2,1)}, u32[]{:S(2)}, u32[]{:S(2)}) async-start(bf16[64,10,3584]{2,1,0:T(8,128)(2,1)} %reshape.84), calls=%async_computation.1 | async-start | bytes 14680064 | tf_op jit(solution)/shard_map/all_to_all | solution.py:48
  292.9 0.0 all-gather.8.cloned.1.call-start
  292.9 0.5 all-gather.8.cloned.1.call-update
  293.5 0.0 all-reduce.2.cloned.1.call-start
  293.5 0.1 copy.45
  293.6 0.1 mul.48
  293.8 0.0 copy-done.2
  293.8 17.3 %all-gather = s32[4,64,2]{1,2,0:T(2,128)S(1)} all-gather(s32[1,64,2]{1,2,0:T(2,128)S(1)} %bitcast.47), channel_id=1, replica_groups=mesh['expert'=64,'tensor'=4] {'tensor'}, dimensions={0}, use_global_device_ids=true | all-gather | bytes 2560 | tf_op jit(solution)/shard_map/all_gather | solution.py:15
  311.1 0.1 reshape.99
  311.2 0.1 reshape.102
  311.3 0.1 copy.38
  311.5 160.8 %all-to-all-done.1 = bf16[64,10,3584]{2,1,0:T(8,128)(2,1)} async-done(((bf16[64,10,3584]{2,1,0:T(8,128)(2,1)}), bf16[64,10,3584]{2,1,0:T(8,128)(2,1)}, u32[]{:S(2)}, u32[]{:S(2)}) %all-to-all-start.1) | async-done | bytes 4587552 | tf_op jit(solution)/shard_map/all_to_all | solution.py:48
  472.3 8.0 %reshape.85 = bf16[640,3584]{1,0:T(8,128)(2,1)} reshape(bf16[64,10,3584]{2,1,0:T(8,128)(2,1)} %all-to-all-done.1) | data formatting | bytes 9175040 | tf_op jit(solution)/shard_map/reshape | solution.py:51
  480.2 10.8 %gather_fusion = bf16[512,3584]{1,0:T(8,128)(2,1)} fusion(bf16[640,3584]{1,0:T(8,128)(2,1)} %reshape.85, s32[1024]{0:T(1024)S(1)} %pad_clamp_fusion), kind=kCustom, calls=%fused_computation | custom fusion | bytes 7342080 | tf_op jit(solution)/shard_map/gather | solution.py:51
  491.0 8.6 %reshape.86 = f32[256,2,3584]{2,1,0:T(2,128)} reshape(bf16[512,3584]{1,0:T(8,128)(2,1)} %gather_fusion) | data formatting | bytes 11010048 | tf_op jit(solution)/shard_map/convert_element_type | solution.py:51
  499.7 13.7 %multiply_reduce_fusion = f32[256,3584]{1,0:T(8,128)} fusion(f32[256,2,3584]{2,1,0:T(2,128)} %reshape.86, f32[256,2]{1,0:T(8,128)S(1)} %copy.38), kind=kLoop, calls=%fused_computation.1 | loop fusion | flops 2752512 | bytes 11012096 | tf_op jit(solution)/shard_map/reduce_sum | solution.py:53
  513.4 0.0 copy-done
  513.4 9.1 %fusion = bf16[256,3584]{1,0:T(8,128)(2,1)} fusion(f32[256,3584]{1,0:T(8,128)} %multiply_reduce_fusion, bf16[640,3584]{0,1:T(8,128)(2,1)} %all-gather.10.cloned.1.call-done, bf16[256,3584]{1,0:T(8,128)(2,1)S(1)} %copy-done, bf16[3584,640]{1,0:T(8,128)(2,1)} %all-gather.8.cloned.1.call-done), kind=kOutput, calls=%fused_computation.5 | convolution fusion | flops 2351464448 | bytes 16515072 | tf_op jit(solution)/shard_map/dot_general | solution.py:24
  522.5 0.0 all-reduce.2.cloned.1.call-update
  522.5 61.8 %all-reduce.2.cloned.1.call-done = bf16[256,3584]{1,0:T(8,128)(2,1)} async-done(((bf16[256,3584]{1,0:T(8,128)(2,1)}), bf16[256,3584]{1,0:T(8,128)(2,1)}) %all-reduce.2.cloned.1.call-update) | async-done | bytes 1835024 | tf_op jit(solution)/shard_map/psum | solution.py:54
  584.3 0.0 copy-done.1
  584.3 1.9 add_convert_fusion
  (15 shorter events, 0.1 us)
Async XLA Ops:
  7.4 36.4 %all-gather.6.cloned.1.call-start = ((), (), s32[]{:S(2)}) async-start(), calls=%async_computation.2 | async-start | bytes 2293760 | tf_op jit(solution)/shard_map/all_gather | solution.py:13
  56.5 191.8 %all-to-all-start = ((bf16[64,10,3584]{2,1,0:T(8,128)(2,1)}), bf16[64,10,3584]{2,1,0:T(8,128)(2,1)}, u32[]{:S(2)}, u32[]{:S(2)}) async-start(bf16[64,10,3584]{2,1,0:T(8,128)(2,1)} %reshape.82), calls=%async_computation | async-start | bytes 14680064 | tf_op jit(solution)/shard_map/all_to_all | solution.py:42
  69.0 444.4 %all-gather.10.cloned.1.call-start = ((), (), s32[]{:S(2)}) async-start(), calls=%async_computation.4 | async-start | bytes 4659200 | tf_op jit(solution)/shard_map/all_gather | solution.py:26
  279.3 14.5 %copy-start.2 = (s32[64,2]{0,1:T(2,128)S(1)}, s32[64,2]{0,1:T(2,128)}, u32[]{:S(2)}) copy-start(s32[64,2]{0,1:T(2,128)} %param.9) | copy-start | bytes 1540
  279.3 193.0 %all-to-all-start.1 = ((bf16[64,10,3584]{2,1,0:T(8,128)(2,1)}), bf16[64,10,3584]{2,1,0:T(8,128)(2,1)}, u32[]{:S(2)}, u32[]{:S(2)}) async-start(bf16[64,10,3584]{2,1,0:T(8,128)(2,1)} %reshape.84), calls=%async_computation.1 | async-start | bytes 14680064 | tf_op jit(solution)/shard_map/all_to_all | solution.py:48
  292.9 220.5 %all-gather.8.cloned.1.call-start = ((), (), s32[]{:S(2)}) async-start(), calls=%async_computation.3 | async-start | bytes 4659200 | tf_op jit(solution)/shard_map/all_gather | solution.py:21
  293.5 290.9 %all-reduce.2.cloned.1.call-start = ((), (), s32[]{:S(2)}) async-start(), calls=%async_computation.5 | async-start | bytes 3670016 | tf_op jit(solution)/shard_map/psum | solution.py:54
  499.7 13.7 %copy-start = (bf16[256,3584]{1,0:T(8,128)(2,1)S(1)}, bf16[256,3584]{1,0:T(8,128)(2,1)}, u32[]{:S(2)}) copy-start(bf16[256,3584]{1,0:T(8,128)(2,1)} %all-gather.6.cloned.1.call-done) | copy-start | bytes 5505028
  513.4 71.0 %copy-start.1 = (bf16[64,3584]{1,0:T(8,128)(2,1)S(1)}, bf16[64,3584]{1,0:T(8,128)(2,1)}, u32[]{:S(2)}) copy-start(bf16[64,3584]{1,0:T(8,128)(2,1)} %param.7) | copy-start | bytes 1376260
Sparse Core Ops, SparseCore 0:
  10.0 33.7 all-gather.5
  522.6 61.6 all-reduce.1
Sparse Core Ops, SparseCore 1:
  73.1 182.5 all-gather.9
  296.9 179.6 all-gather.7
where the time goes:
time: 595 us; the launch traced here: 594 us
  waiting for transfers between devices  428 us (72%)
  local copies, waits for them, and re-layouts  52.5 us (9%)
  matrix products  29.3 us (5%)
  starting transfers between devices  26.3 us (4%)
  blocking collectives  25.6 us (4%)
  other arithmetic  17.3 us (3%)
  between operations  15 us (3%)
    all_to_all x1, waiting for transfers between devices, local(): lax.all_to_all(outgoing, 'expert', split_axis=0, concat_axis=0, tiled=True)  179 us
    all_to_all x1, waiting for transfers between devices, local(): lax.all_to_all(result.reshape(sources, count, width), 'expert', split_axi...  161 us
    psum x1, waiting for transfers between devices, local(): lax.psum(total.astype(jnp.bfloat16), 'tensor').astype(jnp.float32)  61.8 us
    all_gather x1, waiting for transfers between devices, local(): lax.all_gather(tokens, 'tensor', axis=0, tiled=True)  24.7 us
    all_gather x1, blocking collectives, local(): lax.all_gather(gate_codes, 'tensor', axis=0, tiled=True)  17.3 us
    reduce_sum x1, other arithmetic, local(): total = dense_part + jnp.sum(gates[:, :, None] * picked, axis=1)  13.7 us
    all_to_all x1, starting transfers between devices, local(): lax.all_to_all(result.reshape(sources, count, width), 'expert', split_axi...  13.6 us
    all_to_all x1, starting transfers between devices, local(): lax.all_to_all(outgoing, 'expert', split_axis=0, concat_axis=0, tiled=True)  12.5 us
  transfers between devices with their start and end apart: 6, of which 4 were waited for; matrix products, arithmetic and copies ran while one was open for 13% of the time, Pallas kernels for 0%

commit v1 on v0

v1 whole, which is shorter than its diff:
```python
import functools

import jax
import jax.numpy as jnp
from jax import lax
from jax.experimental import pallas as pl
from jax.experimental.pallas import tpu as pltpu
from jax.sharding import PartitionSpec as P

F32 = jnp.float32
BF16 = jnp.bfloat16
CORE = [(0, 1), (1, 0), (2, 3), (3, 2)]
NEXT = [(0, 2), (2, 0), (1, 3), (3, 1)]
META = 16
MAIN = 8
VMEM = 48 * 1024 * 1024


def dot(a, b, dims=((1,), (0,))):
    return lax.dot_general(a, b, (dims, ((), ())), preferred_element_type=F32)


def silu(v):
    return v / (1.0 + jnp.exp(-v))


def dispatch_kernel(n_experts, capacity, x_ref, first_ref, second_ref, plan_ref):
    blocks, rows_all, _ = x_ref.shape
    rows = rows_all - META
    group = blocks * rows
    meta = x_ref[0, rows:, :group].astype(F32)
    for b in range(1, blocks):
        meta = meta + x_ref[b, rows:, :group].astype(F32)
    ids = [meta[k : k + 1].astype(jnp.int32) for k in range(2)]
    codes = [meta[2 + k : 3 + k] * 32.0 + meta[4 + k : 5 + k] for k in range(2)]
    names = lax.broadcasted_iota(jnp.int32, (n_experts, group), 0)
    hits = [(names == ids[k]).astype(F32) for k in range(2)]
    earlier = (
        lax.broadcasted_iota(jnp.int32, (group, group), 0)
        < lax.broadcasted_iota(jnp.int32, (group, group), 1)
    )
    before = dot((hits[0] + hits[1]).astype(BF16), earlier.astype(F32).astype(BF16))
    slots = [jnp.sum(hits[k] * before, axis=0, keepdims=True).astype(jnp.int32) for k in range(2)]
    tail = capacity - MAIN
    in_main = [slots[k] < MAIN for k in range(2)]
    spot_main = [ids[k] * MAIN + slots[k] for k in range(2)]
    spot_tail = [ids[k] * tail + slots[k] - MAIN for k in range(2)]
    tokens = jnp.concatenate([x_ref[b, :rows, :] for b in range(blocks)], axis=0)

    def placed(count, spots):
        at = lax.broadcasted_iota(jnp.int32, (count, group), 0)
        hit = jnp.where((at == spots[0]) | (at == spots[1]), 1.0, 0.0)
        return dot(hit.astype(BF16), tokens).astype(BF16)

    first_ref[...] = placed(
        n_experts * MAIN, [jnp.where(in_main[k], spot_main[k], -1) for k in range(2)]
    )
    second_ref[...] = placed(
        n_experts * tail, [jnp.where(in_main[k], -1, spot_tail[k]) for k in range(2)]
    )
    whole = codes[0] + codes[1]
    for k in range(2):
        row = jnp.where(in_main[k], spot_main[k], n_experts * MAIN + spot_tail[k])
        plan_ref[k : k + 1, :] = row.astype(F32)
        plan_ref[2 + k : 3 + k, :] = codes[k] / whole
    plan_ref[4:8, :] = jnp.zeros((4, group), F32)


def dispatch(x, n_experts, capacity):
    blocks, rows_all, width = x.shape
    group = blocks * (rows_all - META)
    return pl.pallas_call(
        functools.partial(dispatch_kernel, n_experts, capacity),
        out_shape=(
            jax.ShapeDtypeStruct((n_experts * MAIN, width), BF16),
            jax.ShapeDtypeStruct((n_experts * (capacity - MAIN), width), BF16),
            jax.ShapeDtypeStruct((8, group), F32),
        ),
        compiler_params=pltpu.CompilerParams(vmem_limit_bytes=VMEM),
        name="dispatch",
    )(x)


def combine_kernel(first_ref, second_ref, plan_ref, out_ref):
    plan = plan_ref[...]
    group = plan.shape[1]
    total = jnp.zeros((group, first_ref.shape[1]), F32)
    start = 0
    for ref in (first_ref, second_ref):
        count = ref.shape[0]
        at = lax.broadcasted_iota(jnp.int32, (count, group), 0) + start
        gate = jnp.zeros((count, group), F32)
        for k in range(2):
            row = plan[k : k + 1].astype(jnp.int32)
            gate = gate + jnp.where(at == row, plan[2 + k : 3 + k], 0.0)
        high = gate.astype(BF16)
        low = (gate - high.astype(F32)).astype(BF16)
        values = ref[...]
        total = total + dot(high, values, ((0,), (0,))) + dot(low, values, ((0,), (0,)))
        start += count
    out_ref[...] = total.astype(BF16)


def combine(first, second, plan):
    return pl.pallas_call(
        combine_kernel,
        out_shape=jax.ShapeDtypeStruct((plan.shape[1], first.shape[1]), BF16),
        compiler_params=pltpu.CompilerParams(vmem_limit_bytes=VMEM),
        name="combine",
    )(first, second, plan)


def block_of(place, step):
    shift = jnp.where(step == 1, 2, jnp.where(step == 2, 1, step))
    return place ^ shift


def experts_kernel(place_ref, x0, x1, x2, x3, up_ref, down_ref, out_ref, pre, hidden):
    step = pl.program_id(0)
    for i, x in enumerate((x0, x1, x2, x3)):

        @pl.when(step == i)
        def _():
            part = dot(x[...], up_ref[...])
            if i == 0:
                pre[...] = part
            elif i < 3:
                pre[...] += part
            else:
                hidden[...] = silu(pre[...] + part).astype(BF16)

    @pl.when(step >= 4)
    def _():
        out_ref[0] = dot(hidden[...], down_ref[...]).astype(BF16)


def experts(place, xs, up, down):
    rows, width = xs[0].shape
    units = up.shape[1]
    whole = pl.BlockSpec((rows, width), lambda i, p: (0, 0))
    return pl.pallas_call(
        experts_kernel,
        grid_spec=pltpu.PrefetchScalarGridSpec(
            num_scalar_prefetch=1,
            grid=(8,),
            in_specs=[whole] * 4
            + [
                pl.BlockSpec((width, units), lambda i, p: (block_of(p[0], jnp.minimum(i, 3)), 0)),
                pl.BlockSpec((units, width), lambda i, p: (0, block_of(p[0], jnp.maximum(i - 4, 0)))),
            ],
            out_specs=pl.BlockSpec((1, rows, width), lambda i, p: (jnp.maximum(i - 4, 0), 0, 0)),
            scratch_shapes=[pltpu.VMEM((rows, units), F32), pltpu.VMEM((rows, units), BF16)],
        ),
        out_shape=jax.ShapeDtypeStruct((4, rows, width), BF16),
        compiler_params=pltpu.CompilerParams(vmem_limit_bytes=VMEM),
        cost_estimate=pl.CostEstimate(
            flops=16 * rows * width * units, bytes_accessed=32 * rows * width, transcendentals=rows * units
        ),
        name="experts",
    )(place, *xs, up, down)


def dense_kernel(parts, x0, x1, x2, x3, up_ref, down_ref, out_ref, pre, hidden):
    step = pl.program_id(0)

    @pl.when(step < parts)
    def _():
        x = jnp.concatenate([x0[...], x1[...], x2[...], x3[...]], axis=0)
        up = up_ref[...].reshape(x.shape[1], up_ref.shape[-1])
        part = dot(x, up)

        @pl.when(step == 0)
        def _():
            pre[...] = part

        @pl.when(step > 0)
        def _():
            pre[...] += part

    @pl.when(step == parts - 1)
    def _():
        hidden[...] = silu(pre[...]).astype(BF16)

    @pl.when(step >= parts)
    def _():
        out = dot(hidden[...], down_ref[...], ((1,), (1,))).astype(BF16)
        out_ref[...] = out.reshape(out_ref.shape)


def dense(xs, up, down):
    rows, width = xs[0].shape
    outer, parts, inner, units = up.shape
    column = outer * inner
    tile = width // 4
    x_spec = pl.BlockSpec((rows, column), lambda i: (0, jnp.minimum(i, parts - 1)))
    return pl.pallas_call(
        functools.partial(dense_kernel, parts),
        grid=(parts + 4,),
        in_specs=[x_spec] * 4
        + [
            pl.BlockSpec((outer, None, inner, units), lambda i: (0, jnp.minimum(i, parts - 1), 0, 0)),
            pl.BlockSpec((tile, units), lambda i: (jnp.maximum(i - parts, 0), 0)),
        ],
        out_specs=pl.BlockSpec((4, rows, tile), lambda i: (0, 0, jnp.maximum(i - parts, 0))),
        out_shape=jax.ShapeDtypeStruct((4, rows, width), BF16),
        scratch_shapes=[pltpu.VMEM((4 * rows, units), F32), pltpu.VMEM((4 * rows, units), BF16)],
        compiler_params=pltpu.CompilerParams(vmem_limit_bytes=VMEM),
        cost_estimate=pl.CostEstimate(
            flops=16 * rows * width * units, bytes_accessed=4 * width * units, transcendentals=4 * rows * units
        ),
        name="dense",
    )(*xs, up, down)


def spread(x):
    other = lax.ppermute(x, "tensor", CORE)
    near = lax.ppermute(x, "tensor", NEXT)
    far = lax.ppermute(near, "tensor", CORE)
    return x, near, other, far


def fold(parts):
    got = lax.ppermute(parts[2:], "tensor", CORE)
    rest = (parts[1].astype(F32) + got[1].astype(F32)).astype(BF16)
    last = lax.ppermute(rest, "tensor", NEXT)
    return parts[0].astype(F32) + got[0].astype(F32), last


N_X, N_Z, N_Y = 2, 8, 4


def expert_at(x, z, y):
    return (x * N_Z + z) * N_Y + y


def lines(axis):
    xs, zs, ys = range(N_X), range(N_Z), range(N_Y)
    if axis == "z":
        return [[expert_at(x, z, y) for z in zs] for x in xs for y in ys]
    return [[expert_at(x, z, y) for y in ys] for x in xs for z in zs]


def gather_dense(dense_up, dense_down):
    index = lax.axis_index("expert")
    rows, units = dense_up.shape
    both = jnp.concatenate([dense_up, dense_down.T], axis=0)
    swap = [(expert_at(x, z, y), expert_at(1 - x, z, y)) for x in range(N_X) for z in range(N_Z) for y in range(N_Y)]
    mate = lax.ppermute(both, "expert", swap)
    low = index < N_Z * N_Y
    pair = jnp.stack([jnp.where(low, both, mate), jnp.where(low, mate, both)])
    up, down = pair[:, :rows], pair[:, rows:]
    turns = [up]
    for shift in range(1, N_Y):
        turns.append(
            lax.ppermute(
                up,
                "expert",
                [
                    (expert_at(x, z, (y + shift) % N_Y), expert_at(x, z, y))
                    for x in range(N_X)
                    for z in range(N_Z)
                    for y in range(N_Y)
                ],
            )
        )
    turns = jnp.stack(turns + turns[:-1])
    start = lax.rem(N_Y - lax.rem(index, N_Y), N_Y)
    up = lax.dynamic_slice_in_dim(turns, start, N_Y, 0)
    up = up.transpose(1, 0, 2, 3).reshape(N_X * N_Y * rows, units)
    up = lax.all_gather(up, "expert", axis=0, tiled=True, axis_index_groups=lines("z"))
    up = up.reshape(N_Z, N_X, N_Y * rows, units)
    down = down.reshape(N_X * rows, units)
    down = lax.all_gather(down, "expert", axis=0, tiled=True, axis_index_groups=lines("z"))
    down = lax.all_gather(down, "expert", axis=0, tiled=True, axis_index_groups=lines("y"))
    down = down.reshape(N_Y, N_Z, N_X, rows, units).transpose(2, 1, 0, 3, 4).reshape(-1, units)
    return up, down


def local(tokens, expert_ids, gate_codes, dense_up, dense_down, expert_in, expert_out):
    rows_own, width = tokens.shape
    place = lax.axis_index("tensor")
    n_tensor = lax.axis_size("tensor")
    group = rows_own * n_tensor
    n_experts = lax.axis_size("expert") * expert_in.shape[0]
    capacity = 5 * group // (2 * n_experts)
    part = width // n_tensor

    ids, codes = expert_ids.astype(jnp.int32).T, gate_codes.astype(jnp.int32).T
    meta = jnp.concatenate([ids, codes // 32, codes % 32, jnp.zeros((META - 6, rows_own), jnp.int32)])
    owner = jnp.arange(group, dtype=jnp.int32)[None, :] // rows_own
    meta = jnp.where(owner == place, jnp.tile(meta, (1, n_tensor)), 0).astype(BF16)
    meta = jnp.pad(meta, ((0, 0), (0, part - group)))
    columns = tokens.reshape(rows_own, n_tensor, part).transpose(1, 0, 2)
    sent = jnp.concatenate([columns, jnp.broadcast_to(meta, (n_tensor,) + meta.shape)], axis=1)
    grouped = lax.all_to_all(sent, "tensor", split_axis=0, concat_axis=0, tiled=True)

    up_all, down_all = gather_dense(dense_up, dense_down)

    first, second, plan = dispatch(grouped, n_experts, capacity)
    first = lax.all_to_all(
        first.reshape(n_experts, MAIN, part), "expert", split_axis=0, concat_axis=0, tiled=True
    )
    second = lax.all_to_all(
        second.reshape(n_experts, capacity - MAIN, part), "expert", split_axis=0, concat_axis=0, tiled=True
    )
    received = jnp.concatenate([first.reshape(-1, part), second.reshape(-1, part)], axis=0)
    result = experts(place.reshape(1), spread(received), expert_in[0], expert_out[0])
    term, last = fold(result)
    result = (term + last.astype(F32)).astype(BF16)
    cut = n_experts * MAIN
    first = lax.all_to_all(
        result[:cut].reshape(n_experts, MAIN, part), "expert", split_axis=0, concat_axis=0, tiled=True
    )
    second = lax.all_to_all(
        result[cut:].reshape(n_experts, capacity - MAIN, part), "expert", split_axis=0, concat_axis=0, tiled=True
    )
    routed = combine(first.reshape(-1, part), second.reshape(-1, part), plan)

    dense_parts = dense(spread(tokens), up_all, down_all)
    dense_term, dense_last = fold(dense_parts)

    routed = lax.all_to_all(
        routed.reshape(n_tensor, rows_own, part), "tensor", split_axis=0, concat_axis=0, tiled=True
    )
    routed = routed.transpose(1, 0, 2).reshape(rows_own, width)
    total = tokens.astype(F32) + dense_term + dense_last.astype(F32) + routed.astype(F32)
    return total.astype(BF16)


def solution(mesh):
    return jax.shard_map(
        local,
        mesh=mesh,
        in_specs=(
            P(("expert", "tensor"), None),
            P(("expert", "tensor"), None),
            P(("expert", "tensor"), None),
            P("expert", "tensor"),
            P("tensor", "expert"),
            P("expert", None, "tensor"),
            P("expert", "tensor", None),
        ),
        out_specs=P(("expert", "tensor"), None),
        check_vma=False,
    )
```

time: 595 us -> 294 us (0.49)
  waiting for transfers between devices: 428 us -> 144 us
  local copies, waits for them, and re-layouts: 52.5 us -> 19.5 us
  matrix products: 29.3 us -> 0 us
  Pallas kernels: 0 us -> 23.6 us
  starting transfers between devices: 26.3 us -> 47.4 us
  blocking collectives: 25.6 us -> 37.6 us
  other arithmetic: 17.3 us -> 7.69 us
    all_to_all x2 -> x4, waiting for transfers between devices: 339 us -> 16.7 us  [the longest x1 10.9 us: local(): lax.all_to_all(result[cut:].reshape(n_experts, capacity - MAIN, part), 'e...]
    ppermute x0 -> x14, waiting for transfers between devices: none -> 87.6 us  [the longest x2 36.2 us: fold(): last = lax.ppermute(rest, 'tensor', NEXT)]
    psum x1 -> x0, waiting for transfers between devices: 61.8 us -> none  [local(): lax.psum(total.astype(jnp.bfloat16), 'tensor').astype(jnp.float32)]
    all_to_all x0 -> x2, blocking collectives: none -> 37.6 us  [the longest x1 21.7 us: local(): lax.all_to_all(second.reshape(n_experts, capacity - MAIN, part), 'expert'...]
    dot_general x4 -> x0, matrix products: 29.3 us -> none  [the longest x1 9.07 us: local(): jnp.dot(dense_hidden, lax.all_gather(dense_down, 'expert', axis=1, tiled=...]
    reshape x4 -> x6, local copies, waits for them, and re-layouts: 31.5 us -> 3.02 us  [the longest x1 1.03 us: local(): routed = combine(first.reshape(-1, part), second.reshape(-1, part), plan)]
    all_gather x2 -> x0, blocking collectives: 25.6 us -> none  [the longest x1 17.3 us: local(): lax.all_gather(gate_codes, 'tensor', axis=0, tiled=True)]
    pallas_call x0 -> x4, Pallas kernels: none -> 23.6 us  [the longest x1 12.9 us: experts(): pl.pallas_call(experts_kernel, grid_spec=pltpu.PrefetchScalarGridSpec(num...]
  transfers between devices with their start and end apart: 6 -> 21, of which waited for: 4 -> 12; matrix products, arithmetic and copies ran while one was open for 13% -> 5% of each run, Pallas kernels for 0% -> 8%
where the time goes in v1:
time: 294 us; the launch traced here: 293 us
  waiting for transfers between devices  144 us (49%)
  starting transfers between devices  47.4 us (16%)
  blocking collectives  37.6 us (13%)
  Pallas kernels  23.6 us (8%)
  local copies, waits for them, and re-layouts  19.5 us (7%)
  between operations  13.4 us (5%)
  other arithmetic  7.69 us (3%)
    all_gather x2, waiting for transfers between devices, gather_dense(): lax.all_gather(down, 'expert', axis=0, tiled=True, axis_index_groups=line...  39.7 us
    ppermute x2, waiting for transfers between devices, fold(): last = lax.ppermute(rest, 'tensor', NEXT)  36.2 us
    ppermute x3, waiting for transfers between devices, gather_dense(): lax.ppermute(up, 'expert', [(expert_at(x, z, (y + shift) % N_Y), expert_a...  22 us
    all_to_all x1, blocking collectives, local(): lax.all_to_all(second.reshape(n_experts, capacity - MAIN, part), 'expert'...  21.7 us
    ppermute x2, waiting for transfers between devices, spread(): near = lax.ppermute(x, 'tensor', NEXT)  20.4 us
    all_to_all x1, blocking collectives, local(): lax.all_to_all(sent, 'tensor', split_axis=0, concat_axis=0, tiled=True)  15.9 us
    pallas_call x1, Pallas kernels, experts(): pl.pallas_call(experts_kernel, grid_spec=pltpu.PrefetchScalarGridSpec(num...  12.9 us
    all_to_all x1, waiting for transfers between devices, local(): lax.all_to_all(result[cut:].reshape(n_experts, capacity - MAIN, part), 'e...  10.9 us
  transfers between devices with their start and end apart: 21, of which 12 were waited for; matrix products, arithmetic and copies ran while one was open for 5% of the time, Pallas kernels for 8%

profile of v1, /device:TPU:1, one launch (start us, length us, event | category | flops | bytes accessed | tf_op | source)
XLA Modules:
  0.0 293.3 jit_solution(4803335166513618098)
XLA Ops:
  6.5 1.0 pad_maximum_fusion.3
  7.5 3.7 %collective-permute-start.3 = (bf16[112,640]{1,0:T(8,128)(2,1)S(1)}, bf16[112,640]{1,0:T(8,128)(2,1)S(1)}, u32[]{:S(2)}, u32[]{:S(2)}) collective-permute-start(bf16[112,640]{1,0:T(8,128)(2,1)S(1)} %pad_maximum_fusion.3), channel_id=1, source_target_pairs={{0,128},{4,132},{8,136},{12,140},{16,144},{20,148},{24,152},{28,15... | collective-permute-start | bytes 430088 | tf_op jit(solution)/shard_map/ppermute | solution.py:248
  11.2 2.5 collective-permute-done.3
  13.7 1.0 select_bitcast_fusion.1
  15.4 39.7 %all-gather.6.cloned.1.call-done = bf16[896,640]{1,0:T(8,128)(2,1)} async-done(((bf16[112,640]{1,0:T(8,128)(2,1)}), bf16[896,640]{1,0:T(8,128)(2,1)}) %all-gather.6.cloned.1.call-update) | async-done | bytes 1146896 | tf_op jit(solution)/shard_map/all_gather | solution.py:273
  55.6 15.9 %all_to_all.30.x_ref = bf16[4,80,896]{2,1,0:T(8,128)(2,1)S(1)} all-to-all(bf16[4,80,896]{2,1,0:T(8,128)(2,1)S(1)} %pad_maximum_fusion.1), channel_id=1, replica_groups=mesh['expert'=64,'tensor'=4] {'tensor'}, dimensions={0} | all-to-all | bytes 1146880 | tf_op jit(solution)/shard_map/all_to_all | solution.py:295
  71.5 1.6 dispatch.1
  73.2 21.7 %all_to_all.31 = bf16[64,2,896]{2,1,0:T(2,128)(2,1)S(1)} all-to-all(bf16[64,2,896]{2,1,0:T(2,128)(2,1)S(1)} %reshape.117), channel_id=1, replica_groups=mesh['expert'=64,'tensor'=4] {'expert'}, dimensions={0} | all-to-all | bytes 458752 | tf_op jit(solution)/shard_map/all_to_all | solution.py:303
  94.8 6.0 %all-to-all-start.1 = ((bf16[64,8,896]{2,1,0:T(8,128)(2,1)}), bf16[64,8,896]{2,1,0:T(8,128)(2,1)S(1)}, u32[]{:S(2)}, u32[]{:S(2)}) async-start(bf16[64,8,896]{2,1,0:T(8,128)(2,1)} %bitcast.23), calls=%async_computation.1 | async-start | bytes 1835008 | tf_op jit(solution)/shard_map/all_to_all | solution.py:300
  101.0 2.3 collective-permute-start.4
  103.3 1.8 collective-permute-start.5
  105.0 8.3 %collective-permute-done.4 = bf16[2,56,640]{2,1,0:T(8,128)(2,1)S(1)} collective-permute-done((bf16[2,56,640]{2,1,0:T(8,128)(2,1)S(1)}, bf16[2,56,640]{2,1,0:T(8,128)(2,1)S(1)}, u32[]{:S(2)}, u32[]{:S(2)}) %collective-permute-start.4) | collective-permute-done | bytes 143392 | tf_op jit(solution)/shard_map/ppermute | solution.py:255
  113.3 13.7 %collective-permute-done.5 = bf16[2,56,640]{2,1,0:T(8,128)(2,1)S(1)} collective-permute-done((bf16[2,56,640]{2,1,0:T(8,128)(2,1)S(1)}, bf16[2,56,640]{2,1,0:T(8,128)(2,1)S(1)}, u32[]{:S(2)}, u32[]{:S(2)}) %collective-permute-start.5) | collective-permute-done | bytes 143392 | tf_op jit(solution)/shard_map/ppermute | solution.py:255
  127.3 0.9 copy-done.10
  128.4 1.0 copy-done.11
  129.4 0.9 constant_dynamic-slice_fusion
  130.3 2.3 collective-permute-start.10
  132.6 20.4 %collective-permute-done.9.x1 = bf16[640,896]{1,0:T(8,128)(2,1)S(1)} collective-permute-done((bf16[640,896]{1,0:T(8,128)(2,1)S(1)}, bf16[640,896]{1,0:T(8,128)(2,1)S(1)}, u32[]{:S(2)}, u32[]{:S(2)}) %collective-permute-start.9) | collective-permute-done | bytes 1146912 | tf_op jit(solution)/shard_map/ppermute | solution.py:217
  153.0 3.0 %collective-permute-start.11 = (bf16[640,896]{1,0:T(8,128)(2,1)S(1)}, bf16[640,896]{1,0:T(8,128)(2,1)S(1)}, u32[]{:S(2)}, u32[]{:S(2)}) collective-permute-start(bf16[640,896]{1,0:T(8,128)(2,1)S(1)} %collective-permute-done.9.x1), channel_id=1, source_target_pairs={{0,1},{1,0},{2,3},{3,2},{4,5},{5,4},{6,7},{7,6},{8,9},{9,8},{10,11... | collective-permute-start | bytes 3440648 | tf_op jit(solution)/shard_map/ppermute | solution.py:218
  156.0 2.4 collective-permute-done.11.x3
  158.5 12.9 %experts.1 = bf16[4,640,896]{2,1,0:T(8,128)(2,1)} custom-call(s32[1]{0:T(128)} %bitcast.19.place_ref, bf16[640,896]{1,0:T(8,128)(2,1)S(1)} %pad_maximum_fusion.x0, bf16[640,896]{1,0:T(8,128)(2,1)S(1)} %collective-permute-done.9.x1, bf16[640,896]{1,0:T(8,128)(2,1)S(1)} %collective-permute-done.10.x2, bf16[640,896]{1,0:T(8,128)(2,1)S(1)} %collective-permute-done.11.x3, ...), custom_call_target="tpu_custom_call" | custom-call | flops 5872025600 | bytes 18350080 | tf_op jit(solution)/shard_map/experts/pallas_call | solution.py:141
  171.4 2.0 slice.64
  173.9 4.1 %collective-permute-done.12 = bf16[2,640,896]{2,1,0:T(8,128)(2,1)S(1)} collective-permute-done((bf16[2,640,896]{2,1,0:T(8,128)(2,1)S(1)}, bf16[2,640,896]{2,1,0:T(8,128)(2,1)S(1)}, u32[]{:S(2)}, u32[]{:S(2)}) %collective-permute-start.12) | collective-permute-done | bytes 2293792 | tf_op jit(solution)/shard_map/ppermute | solution.py:223
  178.3 26.5 %collective-permute-done.13 = bf16[640,896]{1,0:T(8,128)(2,1)S(1)} collective-permute-done((bf16[640,896]{1,0:T(8,128)(2,1)S(1)}, bf16[640,896]{1,0:T(8,128)(2,1)S(1)}, u32[]{:S(2)}, u32[]{:S(2)}) %collective-permute-start.13) | collective-permute-done | bytes 1146912 | tf_op jit(solution)/shard_map/ppermute | solution.py:225
  205.3 0.8 reshape.121
  206.1 10.5 %all-to-all-start.4 = ((bf16[64,2,896]{2,1,0:T(2,128)(2,1)}), bf16[64,2,896]{2,1,0:T(2,128)(2,1)S(1)}, u32[]{:S(2)}, u32[]{:S(2)}) async-start(bf16[64,2,896]{2,1,0:T(2,128)(2,1)} %reshape.121), calls=%async_computation.4 | async-start | bytes 458752 | tf_op jit(solution)/shard_map/all_to_all | solution.py:314
  216.7 1.0 slice_bitcast_fusion
  217.7 10.9 %all-to-all-done.4 = bf16[64,2,896]{2,1,0:T(2,128)(2,1)S(1)} async-done(((bf16[64,2,896]{2,1,0:T(2,128)(2,1)}), bf16[64,2,896]{2,1,0:T(2,128)(2,1)S(1)}, u32[]{:S(2)}, u32[]{:S(2)}) %all-to-all-start.4) | async-done | bytes 229408 | tf_op jit(solution)/shard_map/all_to_all | solution.py:314
  228.6 5.7 %all-to-all-start.3 = ((bf16[64,8,896]{2,1,0:T(8,128)(2,1)}), bf16[64,8,896]{2,1,0:T(8,128)(2,1)S(1)}, u32[]{:S(2)}, u32[]{:S(2)}) async-start(bf16[64,8,896]{2,1,0:T(8,128)(2,1)} %slice_bitcast_fusion), calls=%async_computation.3 | async-start | bytes 1835008 | tf_op jit(solution)/shard_map/all_to_all | solution.py:311
  234.4 2.3 collective-permute-start.1
  237.0 4.9 %copy.14 = bf16[2,8,4,56,640]{4,3,2,1,0:T(8,128)(2,1)} copy(bf16[2,8,4,56,640]{4,3,0,1,2:T(8,128)(2,1)} %bitcast.93) | data formatting | bytes 9175040 | tf_op jit(solution)/shard_map/transpose | solution.py:275
  241.9 0.8 copy-done.4
  242.7 0.8 copy-done.6
  243.5 1.0 copy-done.3
  244.5 1.0 copy-done.5
  245.5 1.0 copy-done.7
  246.6 8.1 %dense.1 = bf16[4,64,3584]{2,1,0:T(8,128)(2,1)S(1)} custom-call(bf16[64,3584]{1,0:T(8,128)(2,1)S(1)} %copy-done, bf16[64,3584]{1,0:T(8,128)(2,1)S(1)} %copy-done.3, bf16[64,3584]{1,0:T(8,128)(2,1)S(1)} %copy-done.5, bf16[64,3584]{1,0:T(8,128)(2,1)S(1)} %copy-done.7, bf16[8,2,224,640]{3,2,1,0:T(8,128)(2,1)} %bitcast.92, bf16[3584,640]{1,0:T(8,128)(2,1)} %bitcast.91), custom_call_target="tpu_custom_call" | custom-call | flops 2348810240 | bytes 9175040 | tf_op jit(solution)/shard_map/dense/pallas_call | solution.py:196
  254.6 1.0 slice.59
  255.8 1.0 reshape.122.second_ref
  256.8 1.8 all-to-all-done.3
  258.7 1.0 combine.1
  259.7 0.8 copy-done.1
  260.5 7.1 %all-to-all-start.5 = ((bf16[4,64,896]{2,1,0:T(8,128)(2,1)}), bf16[4,64,896]{2,1,0:T(8,128)(2,1)S(1)}, u32[]{:S(2)}, u32[]{:S(2)}) async-start(bf16[4,64,896]{2,1,0:T(8,128)(2,1)} %bitcast.90), calls=%async_computation.5 | async-start | bytes 917504 | tf_op jit(solution)/shard_map/all_to_all | solution.py:322
  267.6 1.9 fusion.5
  269.5 1.4 collective-permute-start.8
  270.9 4.0 %all-to-all-done.5 = bf16[4,64,896]{2,1,0:T(8,128)(2,1)S(1)} async-done(((bf16[4,64,896]{2,1,0:T(8,128)(2,1)}), bf16[4,64,896]{2,1,0:T(8,128)(2,1)S(1)}, u32[]{:S(2)}, u32[]{:S(2)}) %all-to-all-start.5) | async-done | bytes 458784 | tf_op jit(solution)/shard_map/all_to_all | solution.py:322
  275.0 9.7 %collective-permute-done.8 = bf16[64,3584]{1,0:T(8,128)(2,1)S(1)} collective-permute-done((bf16[64,3584]{1,0:T(8,128)(2,1)}, bf16[64,3584]{1,0:T(8,128)(2,1)S(1)}, u32[]{:S(2)}, u32[]{:S(2)}) %collective-permute-start.8) | collective-permute-done | bytes 458784 | tf_op jit(solution)/shard_map/ppermute | solution.py:225
  284.7 2.1 fusion.4
  (70 shorter events, 3.8 us)
Async XLA Ops:
  6.5 48.7 %copy-start.12 = (s32[64,2]{0,1:T(2,128)S(1)}, s32[64,2]{0,1:T(2,128)}, u32[]{:S(2)}) copy-start(s32[64,2]{0,1:T(2,128)} %param.9) | copy-start | bytes 1540
  6.5 48.7 %copy-start.13 = (s32[64,2]{0,1:T(2,128)S(1)}, s32[64,2]{0,1:T(2,128)}, u32[]{:S(2)}) copy-start(s32[64,2]{0,1:T(2,128)} %param.8) | copy-start | bytes 1540
  6.5 48.9 %copy-start = (bf16[64,3584]{1,0:T(8,128)(2,1)S(1)}, bf16[64,3584]{1,0:T(8,128)(2,1)}, u32[]{:S(2)}) copy-start(bf16[64,3584]{1,0:T(8,128)(2,1)} %x0.1) | copy-start | bytes 1376260
  6.5 48.6 %all-gather.6.cloned.1.call-start = ((), (), s32[]{:S(2)}) async-start(), calls=%async_computation.7 | async-start | bytes 1290240 | tf_op jit(solution)/shard_map/all_gather | solution.py:273
  7.5 6.2 %collective-permute-start.3 = (bf16[112,640]{1,0:T(8,128)(2,1)S(1)}, bf16[112,640]{1,0:T(8,128)(2,1)S(1)}, u32[]{:S(2)}, u32[]{:S(2)}) collective-permute-start(bf16[112,640]{1,0:T(8,128)(2,1)S(1)} %pad_maximum_fusion.3), channel_id=1, source_target_pairs={{0,128},{4,132},{8,136},{12,140},{16,144},{20,148},{24,152},{28,15... | collective-permute-start | bytes 430088 | tf_op jit(solution)/shard_map/ppermute | solution.py:248
  15.4 221.6 %all-gather.8.cloned.1.call-start = ((), (), s32[]{:S(2)}) async-start(), calls=%async_computation.8 | async-start | bytes 5734400 | tf_op jit(solution)/shard_map/all_gather | solution.py:274
  94.8 32.4 %all-to-all-start.1 = ((bf16[64,8,896]{2,1,0:T(8,128)(2,1)}), bf16[64,8,896]{2,1,0:T(8,128)(2,1)S(1)}, u32[]{:S(2)}, u32[]{:S(2)}) async-start(bf16[64,8,896]{2,1,0:T(8,128)(2,1)} %bitcast.23), calls=%async_computation.1 | async-start | bytes 1835008 | tf_op jit(solution)/shard_map/all_to_all | solution.py:300
  100.9 142.6 %all-gather.4.cloned.1.call-start = ((), (), s32[]{:S(2)}) async-start(), calls=%async_computation.6 | async-start | bytes 5160960 | tf_op jit(solution)/shard_map/all_gather | solution.py:270
  101.0 12.3 %collective-permute-start.4 = (bf16[2,56,640]{2,1,0:T(8,128)(2,1)S(1)}, bf16[2,56,640]{2,1,0:T(8,128)(2,1)S(1)}, u32[]{:S(2)}, u32[]{:S(2)}) collective-permute-start(bf16[2,56,640]{2,1,0:T(8,128)(2,1)S(1)} %get-tuple-element.12), channel_id=1, source_target_pairs={{4,0},{8,4},{12,8},{0,12},{20,16},{24,20},{28,24},{16,28},{36,32},... | collective-permute-start | bytes 430088 | tf_op jit(solution)/shard_map/ppermute | solution.py:255
  103.3 23.8 %collective-permute-start.6 = (bf16[2,56,640]{2,1,0:T(8,128)(2,1)S(1)}, bf16[2,56,640]{2,1,0:T(8,128)(2,1)S(1)}, u32[]{:S(2)}, u32[]{:S(2)}) collective-permute-start(bf16[2,56,640]{2,1,0:T(8,128)(2,1)S(1)} %get-tuple-element.12), channel_id=1, source_target_pairs={{12,0},{0,4},{4,8},{8,12},{28,16},{16,20},{20,24},{24,28},{44,32},... | collective-permute-start | bytes 430088 | tf_op jit(solution)/shard_map/ppermute | solution.py:255
  103.3 23.8 %collective-permute-start.5 = (bf16[2,56,640]{2,1,0:T(8,128)(2,1)S(1)}, bf16[2,56,640]{2,1,0:T(8,128)(2,1)S(1)}, u32[]{:S(2)}, u32[]{:S(2)}) collective-permute-start(bf16[2,56,640]{2,1,0:T(8,128)(2,1)S(1)} %get-tuple-element.12), channel_id=1, source_target_pairs={{8,0},{12,4},{0,8},{4,12},{24,16},{28,20},{16,24},{20,28},{40,32},... | collective-permute-start | bytes 430088 | tf_op jit(solution)/shard_map/ppermute | solution.py:255
  127.2 1.0 copy-start.10
  128.2 1.2 copy-start.11
  128.3 24.7 %collective-permute-start.9 = (bf16[640,896]{1,0:T(8,128)(2,1)S(1)}, bf16[640,896]{1,0:T(8,128)(2,1)S(1)}, u32[]{:S(2)}, u32[]{:S(2)}) collective-permute-start(bf16[640,896]{1,0:T(8,128)(2,1)S(1)} %pad_maximum_fusion.x0), channel_id=1, source_target_pairs={{0,2},{2,0},{1,3},{3,1},{4,6},{6,4},{5,7},{7,5},{8,10},{10,8},{9,1... | collective-permute-start | bytes 3440648 | tf_op jit(solution)/shard_map/ppermute | solution.py:217
  130.3 25.8 %collective-permute-start.10 = (bf16[640,896]{1,0:T(8,128)(2,1)S(1)}, bf16[640,896]{1,0:T(8,128)(2,1)S(1)}, u32[]{:S(2)}, u32[]{:S(2)}) collective-permute-start(bf16[640,896]{1,0:T(8,128)(2,1)S(1)} %pad_maximum_fusion.x0), channel_id=1, source_target_pairs={{0,1},{1,0},{2,3},{3,2},{4,5},{5,4},{6,7},{7,6},{8,9},{9,8},{10,11... | collective-permute-start | bytes 3440648 | tf_op jit(solution)/shard_map/ppermute | solution.py:216
  153.0 5.5 %collective-permute-start.11 = (bf16[640,896]{1,0:T(8,128)(2,1)S(1)}, bf16[640,896]{1,0:T(8,128)(2,1)S(1)}, u32[]{:S(2)}, u32[]{:S(2)}) collective-permute-start(bf16[640,896]{1,0:T(8,128)(2,1)S(1)} %collective-permute-done.9.x1), channel_id=1, source_target_pairs={{0,1},{1,0},{2,3},{3,2},{4,5},{5,4},{6,7},{7,6},{8,9},{9,8},{10,11... | collective-permute-start | bytes 3440648 | tf_op jit(solution)/shard_map/ppermute | solution.py:218
  171.4 6.5 %copy-start.8 = (bf16[4,640,896]{2,1,0:T(8,128)(2,1)S(1)}, bf16[4,640,896]{2,1,0:T(8,128)(2,1)}, u32[]{:S(2)}) copy-start(bf16[4,640,896]{2,1,0:T(8,128)(2,1)} %experts.1) | copy-start | bytes 13762564
  173.4 4.5 %collective-permute-start.12 = (bf16[2,640,896]{2,1,0:T(8,128)(2,1)S(1)}, bf16[2,640,896]{2,1,0:T(8,128)(2,1)S(1)}, u32[]{:S(2)}, u32[]{:S(2)}) collective-permute-start(bf16[2,640,896]{2,1,0:T(8,128)(2,1)S(1)} %slice.64), channel_id=1, source_target_pairs={{0,1},{1,0},{2,3},{3,2},{4,5},{5,4},{6,7},{7,6},{8,9},{9,8},{10,11... | collective-permute-start | bytes 6881288 | tf_op jit(solution)/shard_map/ppermute | solution.py:223
  178.2 26.6 %collective-permute-start.13 = (bf16[640,896]{1,0:T(8,128)(2,1)S(1)}, bf16[640,896]{1,0:T(8,128)(2,1)S(1)}, u32[]{:S(2)}, u32[]{:S(2)}) collective-permute-start(bf16[640,896]{1,0:T(8,128)(2,1)S(1)} %fusion.1), channel_id=1, source_target_pairs={{0,2},{2,0},{1,3},{3,1},{4,6},{6,4},{5,7},{7,5},{8,10},{10,8},{9,1... | collective-permute-start | bytes 3440648 | tf_op jit(solution)/shard_map/ppermute | solution.py:225
  206.1 22.6 %all-to-all-start.4 = ((bf16[64,2,896]{2,1,0:T(2,128)(2,1)}), bf16[64,2,896]{2,1,0:T(2,128)(2,1)S(1)}, u32[]{:S(2)}, u32[]{:S(2)}) async-start(bf16[64,2,896]{2,1,0:T(2,128)(2,1)} %reshape.121), calls=%async_computation.4 | async-start | bytes 458752 | tf_op jit(solution)/shard_map/all_to_all | solution.py:314
  216.6 20.0 %collective-permute-start = (bf16[64,3584]{1,0:T(8,128)(2,1)S(1)}, bf16[64,3584]{1,0:T(8,128)(2,1)S(1)}, u32[]{:S(2)}, u32[]{:S(2)}) collective-permute-start(bf16[64,3584]{1,0:T(8,128)(2,1)S(1)} %copy-done), channel_id=1, source_target_pairs={{0,2},{2,0},{1,3},{3,1},{4,6},{6,4},{5,7},{7,5},{8,10},{10,8},{9,1... | collective-permute-start | bytes 1376264 | tf_op jit(solution)/shard_map/ppermute | solution.py:217
  228.6 13.3 %copy-start.9 = (bf16[64,2,896]{2,1,0:T(2,128)(2,1)}, bf16[64,2,896]{2,1,0:T(2,128)(2,1)S(1)}, u32[]{:S(2)}) copy-start(bf16[64,2,896]{2,1,0:T(2,128)(2,1)S(1)} %all-to-all-done.4) | copy-start | bytes 688132
  228.6 30.0 %all-to-all-start.3 = ((bf16[64,8,896]{2,1,0:T(8,128)(2,1)}), bf16[64,8,896]{2,1,0:T(8,128)(2,1)S(1)}, u32[]{:S(2)}, u32[]{:S(2)}) async-start(bf16[64,8,896]{2,1,0:T(8,128)(2,1)} %slice_bitcast_fusion), calls=%async_computation.3 | async-start | bytes 1835008 | tf_op jit(solution)/shard_map/all_to_all | solution.py:311
  234.4 7.5 %collective-permute-start.1 = (bf16[64,3584]{1,0:T(8,128)(2,1)S(1)}, bf16[64,3584]{1,0:T(8,128)(2,1)S(1)}, u32[]{:S(2)}, u32[]{:S(2)}) collective-permute-start(bf16[64,3584]{1,0:T(8,128)(2,1)S(1)} %copy-done), channel_id=1, source_target_pairs={{0,1},{1,0},{2,3},{3,2},{4,5},{5,4},{6,7},{7,6},{8,9},{9,8},{10,11... | collective-permute-start | bytes 1376264 | tf_op jit(solution)/shard_map/ppermute | solution.py:216
  236.6 5.3 %copy-start.2 = (bf16[64,3584]{1,0:T(8,128)(2,1)}, bf16[64,3584]{1,0:T(8,128)(2,1)S(1)}, u32[]{:S(2)}) copy-start(bf16[64,3584]{1,0:T(8,128)(2,1)S(1)} %collective-permute-done.x1) | copy-start | bytes 1376260
  236.6 6.1 %collective-permute-start.2 = (bf16[64,3584]{1,0:T(8,128)(2,1)S(1)}, bf16[64,3584]{1,0:T(8,128)(2,1)S(1)}, u32[]{:S(2)}, u32[]{:S(2)}) collective-permute-start(bf16[64,3584]{1,0:T(8,128)(2,1)S(1)} %collective-permute-done.x1), channel_id=1, source_target_pairs={{0,1},{1,0},{2,3},{3,2},{4,5},{5,4},{6,7},{7,6},{8,9},{9,8},{10,11... | collective-permute-start | bytes 1376264 | tf_op jit(solution)/shard_map/ppermute | solution.py:218
  241.9 0.8 copy-start.4
  242.7 0.8 copy-start.6
  243.5 1.0 copy-start.3
  244.5 1.0 copy-start.5
  245.5 1.0 copy-start.7
  255.6 11.9 %collective-permute-start.7 = (bf16[2,64,3584]{2,1,0:T(8,128)(2,1)}, bf16[2,64,3584]{2,1,0:T(8,128)(2,1)}, u32[]{:S(2)}, u32[]{:S(2)}) collective-permute-start(bf16[2,64,3584]{2,1,0:T(8,128)(2,1)} %slice.59), channel_id=1, source_target_pairs={{0,1},{1,0},{2,3},{3,2},{4,5},{5,4},{6,7},{7,6},{8,9},{9,8},{10,11... | collective-permute-start | bytes 2752520 | tf_op jit(solution)/shard_map/ppermute | solution.py:223
  259.7 0.8 copy-start.1
  260.5 14.4 %all-to-all-start.5 = ((bf16[4,64,896]{2,1,0:T(8,128)(2,1)}), bf16[4,64,896]{2,1,0:T(8,128)(2,1)S(1)}, u32[]{:S(2)}, u32[]{:S(2)}) async-start(bf16[4,64,896]{2,1,0:T(8,128)(2,1)} %bitcast.90), calls=%async_computation.5 | async-start | bytes 917504 | tf_op jit(solution)/shard_map/all_to_all | solution.py:322
  269.5 15.2 %collective-permute-start.8 = (bf16[64,3584]{1,0:T(8,128)(2,1)}, bf16[64,3584]{1,0:T(8,128)(2,1)S(1)}, u32[]{:S(2)}, u32[]{:S(2)}) collective-permute-start(bf16[64,3584]{1,0:T(8,128)(2,1)} %fusion.5), channel_id=1, source_target_pairs={{0,2},{2,0},{1,3},{3,1},{4,6},{6,4},{5,7},{7,5},{8,10},{10,8},{9,1... | collective-permute-start | bytes 1376264 | tf_op jit(solution)/shard_map/ppermute | solution.py:225
Sparse Core Ops, SparseCore 0:
  15.5 39.5 all-gather.5
  56.9 75.2 all-gather.7
  133.9 58.8 all-gather.3

commit v2 on v0

v2 whole, which is shorter than its diff:
```python
import functools

import jax
import jax.numpy as jnp
from jax import lax
from jax.experimental import pallas as pl
from jax.experimental.pallas import tpu as pltpu
from jax.sharding import PartitionSpec as P

F32 = jnp.float32
BF16 = jnp.bfloat16
CORE = [(0, 1), (1, 0), (2, 3), (3, 2)]
NEXT = [(0, 2), (2, 0), (1, 3), (3, 1)]
FAR = [(0, 3), (3, 0), (1, 2), (2, 1)]
N_X, N_Z, N_Y = 2, 8, 4
META = 16
MAIN = 8
LANES = 128
HALVES = 2
VMEM = 32 * 1024 * 1024


def dot(a, b, dims=((1,), (0,))):
    return lax.dot_general(a, b, (dims, ((), ())), preferred_element_type=F32)


def silu(v):
    return v / (1.0 + jnp.exp(-v))


def flip(step):
    return (0, 2, 1, 3)[step]


def at(place, step, size):
    return pl.multiple_of((place ^ flip(step)) * size, size)


def tiles_of(width, capacity):
    return width // LANES + capacity - MAIN


def put_tiles(ref, lead, scratch, main, tail, count, capacity):
    n, extra = main.shape[1] // LANES, capacity - MAIN
    for j in range(n):
        piece = main[:, j * LANES : (j + 1) * LANES].reshape(count, MAIN, LANES)
        ref[lead + (slice(None), j)] = piece.astype(BF16)
    for s in range(extra):
        for j in range(n):
            rows = pl.ds(s * MAIN + j, count, stride=extra * MAIN)
            scratch[rows, :] = tail[s * count : (s + 1) * count, j * LANES : (j + 1) * LANES]
    rest = scratch[...].reshape(count, extra, MAIN, LANES)
    for s in range(extra):
        ref[lead + (slice(None), n + s)] = rest[:, s].astype(BF16)


def take_tiles(ref, scratch, count, capacity):
    extra = capacity - MAIN
    n = ref.shape[1] - extra
    main = [
        ref[:, j].astype(F32).reshape(count * MAIN, LANES).astype(BF16) for j in range(n)
    ]
    scratch[...] = ref[:, n:].astype(F32).reshape(count * extra * MAIN, LANES)
    tail = []
    for s in range(extra):
        cut = [scratch[pl.ds(s * MAIN + j, count, stride=extra * MAIN), :] for j in range(n)]
        tail.append(jnp.concatenate(cut, axis=1).astype(BF16))
    return jnp.concatenate([jnp.concatenate(main, axis=1)] + tail, axis=0)


def clear(scratch):
    scratch[...] = jnp.zeros(scratch.shape, scratch.dtype)


SMEM = pl.BlockSpec(memory_space=pltpu.SMEM)
WHOLE = pl.BlockSpec(memory_space=pltpu.VMEM)
PARAMS = pltpu.CompilerParams(vmem_limit_bytes=VMEM)


def pack_kernel(place_ref, tokens_ref, meta_ref, *out_refs):
    rows, part = tokens_ref.shape[0], out_refs[0].shape[1]
    for step, out_ref in enumerate(out_refs):
        out_ref[:rows, :] = tokens_ref[:, pl.ds(at(place_ref[0], step, part), part)]
        out_ref[rows:, :] = meta_ref[...]


def pack(place, tokens, meta):
    rows, width = tokens.shape
    block = jax.ShapeDtypeStruct((rows + META, width // 4), BF16)
    return pl.pallas_call(
        pack_kernel,
        in_specs=[SMEM, WHOLE, WHOLE],
        out_specs=[WHOLE] * 4,
        out_shape=[block] * 4,
        compiler_params=PARAMS,
        name="pack",
    )(place, tokens, meta)


def dispatch_kernel(n_experts, capacity, place_ref, x0, x1, x2, x3, out_ref, plan_ref, tokens, scratch):
    rows = x0.shape[0] - META
    group = 4 * rows
    meta = jnp.zeros((META, group), F32)
    for step, x in enumerate((x0, x1, x2, x3)):
        meta = meta + x[rows:, :group].astype(F32)
        tokens[pl.ds(at(place_ref[0], step, rows), rows), :] = x[:rows, :]
    ids = [meta[k : k + 1].astype(jnp.int32) for k in range(2)]
    codes = [meta[2 + k : 3 + k] * 32.0 + meta[4 + k : 5 + k] for k in range(2)]
    names = lax.broadcasted_iota(jnp.int32, (n_experts, group), 0)
    hits = [(names == ids[k]).astype(F32) for k in range(2)]
    earlier = (
        lax.broadcasted_iota(jnp.int32, (group, group), 0)
        < lax.broadcasted_iota(jnp.int32, (group, group), 1)
    )
    before = dot((hits[0] + hits[1]).astype(BF16), earlier.astype(F32).astype(BF16))
    slots = [jnp.sum(hits[k] * before, axis=0, keepdims=True).astype(jnp.int32) for k in range(2)]
    in_main = [slots[k] < MAIN for k in range(2)]
    spot_main = [ids[k] * MAIN + slots[k] for k in range(2)]
    spot_tail = [(slots[k] - MAIN) * n_experts + ids[k] for k in range(2)]

    def placed(count, spots):
        row = lax.broadcasted_iota(jnp.int32, (count, group), 0)
        hit = jnp.where((row == spots[0]) | (row == spots[1]), 1.0, 0.0)
        return dot(hit.astype(BF16), tokens[...])

    main = placed(n_experts * MAIN, [jnp.where(in_main[k], spot_main[k], -1) for k in range(2)])
    tail = placed(
        n_experts * (capacity - MAIN), [jnp.where(in_main[k], -1, spot_tail[k]) for k in range(2)]
    )
    clear(scratch)
    put_tiles(out_ref, (), scratch, main, tail, n_experts, capacity)
    whole = codes[0] + codes[1]
    for k in range(2):
        row = jnp.where(in_main[k], spot_main[k], n_experts * MAIN + spot_tail[k])
        plan_ref[k : k + 1, :] = row.astype(F32)
        plan_ref[2 + k : 3 + k, :] = codes[k] / whole
    plan_ref[4:8, :] = jnp.zeros((4, group), F32)


def dispatch(place, xs, n_experts, capacity):
    rows_all, width = xs[0].shape
    group = 4 * (rows_all - META)
    return pl.pallas_call(
        functools.partial(dispatch_kernel, n_experts, capacity),
        in_specs=[SMEM] + [WHOLE] * 4,
        out_specs=[WHOLE] * 2,
        out_shape=[
            jax.ShapeDtypeStruct((n_experts, tiles_of(width, capacity), MAIN, LANES), BF16),
            jax.ShapeDtypeStruct((8, group), F32),
        ],
        scratch_shapes=[
            pltpu.VMEM((group, width), BF16),
            pltpu.VMEM((n_experts * (capacity - MAIN) * MAIN, LANES), F32),
        ],
        compiler_params=PARAMS,
        name="dispatch",
    )(place, *xs)


def experts_kernel(capacity, place_ref, x0, x1, x2, x3, up_ref, down_ref, mine_ref, others_ref, x_all, scratch):
    count, tiles = x0.shape[:2]
    width = (tiles - capacity + MAIN) * LANES
    for step, x in enumerate((x0, x1, x2, x3)):
        x_all[:, pl.ds(at(place_ref[0], step, width), width)] = take_tiles(x, scratch, count, capacity)
    hidden = silu(dot(x_all[...], up_ref[...])).astype(BF16)
    clear(scratch)
    for step in (2, 3, 0, 1):
        out = dot(hidden, down_ref[:, pl.ds(at(place_ref[0], step, width), width)])
        ref = mine_ref if step < 2 else others_ref
        put_tiles(ref, (step % 2,), scratch, out[: count * MAIN], out[count * MAIN :], count, capacity)


def experts(place, xs, up, down, capacity):
    count, tiles = xs[0].shape[:2]
    width, units = up.shape
    rows = count * capacity
    pair = jax.ShapeDtypeStruct((2,) + xs[0].shape, BF16)
    return pl.pallas_call(
        functools.partial(experts_kernel, capacity),
        in_specs=[SMEM] + [WHOLE] * 6,
        out_specs=[WHOLE] * 2,
        out_shape=[pair] * 2,
        scratch_shapes=[
            pltpu.VMEM((rows, width), BF16),
            pltpu.VMEM((count * (capacity - MAIN) * MAIN, LANES), F32),
        ],
        compiler_params=PARAMS,
        cost_estimate=pl.CostEstimate(
            flops=4 * rows * width * units,
            bytes_accessed=4 * width * (rows + units),
            transcendentals=rows * units,
        ),
        name="experts",
    )(place, *xs, up, down)


def combine_kernel(capacity, place_ref, x_ref, plan_ref, o0, o1, o2, o3, scratch, routed):
    count = x_ref.shape[0]
    plan = plan_ref[...]
    group = plan.shape[1]
    values = take_tiles(x_ref, scratch, count, capacity)
    row = lax.broadcasted_iota(jnp.int32, (count * capacity, group), 0)
    gate = jnp.zeros((count * capacity, group), F32)
    for k in range(2):
        gate = gate + jnp.where(row == plan[k : k + 1].astype(jnp.int32), plan[2 + k : 3 + k], 0.0)
    high = gate.astype(BF16)
    low = (gate - high.astype(F32)).astype(BF16)
    routed[...] = (dot(high, values, ((0,), (0,))) + dot(low, values, ((0,), (0,)))).astype(BF16)
    for step, ref in enumerate((o0, o1, o2, o3)):
        ref[...] = routed[pl.ds(at(place_ref[0], step, group // 4), group // 4), :]


def combine(place, x, plan, capacity):
    count, tiles = x.shape[:2]
    width = (tiles - capacity + MAIN) * LANES
    group = plan.shape[1]
    return pl.pallas_call(
        functools.partial(combine_kernel, capacity),
        in_specs=[SMEM] + [WHOLE] * 2,
        out_specs=[WHOLE] * 4,
        out_shape=[jax.ShapeDtypeStruct((group // 4, width), BF16)] * 4,
        scratch_shapes=[
            pltpu.VMEM((count * (capacity - MAIN) * MAIN, LANES), F32),
            pltpu.VMEM((group, width), BF16),
        ],
        compiler_params=PARAMS,
        name="combine",
    )(place, x, plan)


def dense_kernel(x0, x1, x2, x3, up_ref, down_ref, mine_ref, others_ref, pre, hidden):
    step = pl.program_id(0)

    @pl.when(step < N_X)
    def _():
        x = jnp.concatenate([x0[...], x1[...], x2[...], x3[...]], axis=0)
        up = up_ref[...].astype(F32).reshape(x.shape[1], up_ref.shape[-1]).astype(BF16)
        part = dot(x, up)

        @pl.when(step == 0)
        def _():
            pre[...] = part

        @pl.when(step > 0)
        def _():
            hidden[...] = silu(pre[...] + part).astype(BF16)

    @pl.when(step >= N_X)
    def _():
        down = down_ref[...].astype(F32)
        down = down.reshape(-1, down.shape[-1]).astype(BF16)
        out = dot(hidden[...], down, ((1,), (1,))).astype(BF16).reshape((4,) + mine_ref.shape[1:])
        mine_ref[...] = out[:2]
        others_ref[...] = out[2:]


def dense(xs, weights):
    rows, width = xs[0].shape
    units = weights.shape[-1]
    z, y, _, _, inner, _ = weights.shape
    tile = width // 4
    x_spec = pl.BlockSpec((rows, width // N_X), lambda i: (0, jnp.minimum(i, N_X - 1)))
    out_spec = pl.BlockSpec((2, rows, tile), lambda i: (0, 0, jnp.maximum(i - N_X, 0)))

    def down_at(i):
        n = jnp.maximum(i - N_X, 0)
        return n % 2, 0, n // 2, 1, 0, 0

    return pl.pallas_call(
        dense_kernel,
        grid=(N_X + 4,),
        in_specs=[x_spec] * 4
        + [
            pl.BlockSpec((z, y, None, None, inner, units), lambda i: (0, 0, jnp.minimum(i, N_X - 1), 0, 0, 0)),
            pl.BlockSpec((z // 2, y, None, None, inner, units), down_at),
        ],
        out_specs=[out_spec] * 2,
        out_shape=[jax.ShapeDtypeStruct((2, rows, width), BF16)] * 2,
        scratch_shapes=[pltpu.VMEM((4 * rows, units), F32), pltpu.VMEM((4 * rows, units), BF16)],
        compiler_params=PARAMS,
        cost_estimate=pl.CostEstimate(
            flops=16 * rows * width * units, bytes_accessed=4 * width * units, transcendentals=4 * rows * units
        ),
        name="dense",
    )(*xs, weights, weights)


def finish_kernel(place_ref, tokens_ref, mine_ref, got_ref, last_ref, r0, r1, r2, r3, out_ref):
    part = r0.shape[1]
    for step, ref in enumerate((r0, r1, r2, r3)):
        columns = pl.ds(at(place_ref[0], step, part), part)
        total = tokens_ref[:, columns].astype(F32) + mine_ref[0, :, columns].astype(F32)
        total = total + got_ref[0, :, columns].astype(F32) + last_ref[:, columns].astype(F32)
        out_ref[:, columns] = (total + ref[...].astype(F32)).astype(BF16)


def finish(place, tokens, mine, got, last, routed):
    return pl.pallas_call(
        finish_kernel,
        in_specs=[SMEM] + [WHOLE] * 8,
        out_specs=WHOLE,
        out_shape=jax.ShapeDtypeStruct(tokens.shape, BF16),
        compiler_params=PARAMS,
        name="finish",
    )(place, tokens, mine, got, last, *routed)


def swap(xs):
    return [xs[0]] + [lax.ppermute(x, "tensor", perm) for x, perm in zip(xs[1:], (NEXT, CORE, FAR))]


def spread(x, near):
    other = lax.ppermute(x, "tensor", CORE)
    far = lax.ppermute(near, "tensor", CORE)
    return x, near, other, far


def fold(mine, others):
    got = lax.ppermute(others, "tensor", CORE)
    rest = (mine[1].astype(F32) + got[1].astype(F32)).astype(BF16)
    return got, lax.ppermute(rest, "tensor", NEXT)


def expert_at(x, z, y):
    return (x * N_Z + z) * N_Y + y


def gather_dense(dense_up, dense_down, after):
    rows, units = dense_up.shape
    places = [(x, z, y) for x in range(N_X) for z in range(N_Z) for y in range(N_Y)]
    both = jnp.concatenate([dense_up, dense_down.T], axis=0)
    mate = lax.ppermute(both, "expert", [(expert_at(x, z, y), expert_at(1 - x, z, y)) for x, z, y in places])
    mate, after = lax.optimization_barrier((mate, after))
    low = lax.axis_index("expert") < N_Z * N_Y
    pair = jnp.concatenate([jnp.where(low, both, mate), jnp.where(low, mate, both)])
    planes = [[expert_at(x, z, y) for z in range(N_Z) for y in range(N_Y)] for x in range(N_X)]
    out = lax.all_gather(pair, "expert", axis=0, tiled=True, axis_index_groups=planes)
    return out.reshape(N_Z, N_Y, N_X, 2, rows, units), after


def local(tokens, expert_ids, gate_codes, dense_up, dense_down, expert_in, expert_out):
    rows_own, width = tokens.shape
    place = lax.axis_index("tensor")
    spot = place.reshape(1)
    n_tensor = lax.axis_size("tensor")
    group = rows_own * n_tensor
    n_experts = lax.axis_size("expert") * expert_in.shape[0]
    capacity = 5 * group // (2 * n_experts)
    part = width // n_tensor

    ids, codes = expert_ids.astype(jnp.int32).T, gate_codes.astype(jnp.int32).T
    meta = jnp.concatenate([ids, codes // 32, codes % 32, jnp.zeros((META - 6, rows_own), jnp.int32)])
    owner = jnp.arange(group, dtype=jnp.int32)[None, :] // rows_own
    meta = jnp.where(owner == place, jnp.tile(meta, (1, n_tensor)), 0).astype(BF16)
    meta = jnp.pad(meta, ((0, 0), (0, part - group)))
    grouped = swap(pack(spot, tokens, meta))
    weights, grouped = gather_dense(dense_up, dense_down, grouped)
    routed, plan = dispatch(spot, grouped, n_experts, capacity)

    routed = lax.all_to_all(routed, "expert", split_axis=0, concat_axis=0, tiled=True)
    size = n_experts // HALVES
    results, near = [], None
    for half in range(HALVES):
        x = routed[half * size : (half + 1) * size]
        if near is not None:
            x, near = lax.optimization_barrier((x, near))
        near = lax.ppermute(x, "tensor", NEXT)
        mine, others = experts(spot, spread(x, near), expert_in[0], expert_out[0], capacity)
        got, last = fold(mine, others)
        results.append((mine[0].astype(F32) + got[0].astype(F32) + last.astype(F32)).astype(BF16))
    result = jnp.concatenate(results)

    dense_own, result = lax.optimization_barrier((tokens, result))
    blocks = spread(tokens, lax.ppermute(tokens, "tensor", NEXT))
    mine, others = dense((dense_own,) + blocks[1:], weights)
    got, last = fold(mine, others)

    returned = lax.all_to_all(result, "expert", split_axis=0, concat_axis=0, tiled=True)
    pieces = swap(combine(spot, returned, plan, capacity))
    return finish(spot, tokens, mine, got, last, pieces)


def solution(mesh):
    return jax.shard_map(
        local,
        mesh=mesh,
        in_specs=(
            P(("expert", "tensor"), None),
            P(("expert", "tensor"), None),
            P(("expert", "tensor"), None),
            P("expert", "tensor"),
            P("tensor", "expert"),
            P("expert", None, "tensor"),
            P("expert", "tensor", None),
        ),
        out_specs=P(("expert", "tensor"), None),
        check_vma=False,
    )
```

time: 595 us -> 217 us (0.36)
  waiting for transfers between devices: 428 us -> 71.6 us
  local copies, waits for them, and re-layouts: 52.5 us -> 9.22 us
  matrix products: 29.3 us -> 0 us
  blocking collectives: 25.6 us -> 49.8 us
  Pallas kernels: 0 us -> 21.2 us
  starting transfers between devices: 26.3 us -> 44.3 us
  other arithmetic: 17.3 us -> 6.9 us
    all_to_all x2 -> x1, waiting for transfers between devices: 339 us -> 14.4 us  [local(): lax.all_to_all(result, 'expert', split_axis=0, concat_axis=0, tiled=True)]
    psum x1 -> x0, waiting for transfers between devices: 61.8 us -> none  [local(): lax.psum(total.astype(jnp.bfloat16), 'tensor').astype(jnp.float32)]
    ppermute x0 -> x22, waiting for transfers between devices: none -> 57.2 us  [the longest x1 21.1 us: local(): blocks = spread(tokens, lax.ppermute(tokens, 'tensor', NEXT))]
    all_to_all x0 -> x1, blocking collectives: none -> 49.8 us  [local(): lax.all_to_all(routed, 'expert', split_axis=0, concat_axis=0, tiled=True)]
    ppermute x0 -> x22, starting transfers between devices: none -> 36 us  [the longest x3 10.1 us: spread(): other = lax.ppermute(x, 'tensor', CORE)]
    reshape x4 -> x0, local copies, waits for them, and re-layouts: 31.5 us -> none  [the longest x1 8 us: local(): flat = received.reshape(sources * count, width)]
    dot_general x4 -> x0, matrix products: 29.3 us -> none  [the longest x1 9.07 us: local(): jnp.dot(dense_hidden, lax.all_gather(dense_down, 'expert', axis=1, tiled=...]
    all_gather x2 -> x0, blocking collectives: 25.6 us -> none  [the longest x1 17.3 us: local(): lax.all_gather(gate_codes, 'tensor', axis=0, tiled=True)]
  transfers between devices with their start and end apart: 6 -> 24, of which waited for: 4 -> 11; matrix products, arithmetic and copies ran while one was open for 13% -> 2% of each run, Pallas kernels for 0% -> 9%
where the time goes in v2:
time: 217 us
  waiting for transfers between devices  71.6 us (33%)
  blocking collectives  49.8 us (23%)
  starting transfers between devices  44.3 us (20%)
  Pallas kernels  21.2 us (10%)
  between operations  13.6 us (6%)
  local copies, waits for them, and re-layouts  9.22 us (4%)
  other arithmetic  6.9 us (3%)
    all_to_all x1, blocking collectives, local(): lax.all_to_all(routed, 'expert', split_axis=0, concat_axis=0, tiled=True)  49.8 us
    ppermute x1, waiting for transfers between devices, local(): blocks = spread(tokens, lax.ppermute(tokens, 'tensor', NEXT))  21.1 us
    all_to_all x1, waiting for transfers between devices, local(): lax.all_to_all(result, 'expert', split_axis=0, concat_axis=0, tiled=True)  14.4 us
    pallas_call x2, Pallas kernels, experts(): pl.pallas_call(functools.partial(experts_kernel, capacity), in_specs=[SME...  11.2 us
    ppermute x3, waiting for transfers between devices, fold(): return (got, lax.ppermute(rest, 'tensor', NEXT))  11.2 us
    ppermute x2, waiting for transfers between devices, local(): near = lax.ppermute(x, 'tensor', NEXT)  10.2 us
    ppermute x6, waiting for transfers between devices, swap(): lax.ppermute(x, 'tensor', perm)  10.1 us
    ppermute x3, starting transfers between devices, spread(): other = lax.ppermute(x, 'tensor', CORE)  10.1 us
  transfers between devices with their start and end apart: 24, of which 11 were waited for; matrix products, arithmetic and copies ran while one was open for 2% of the time, Pallas kernels for 9%

profile of v2, /device:TPU:1, one launch (start us, length us, event | category | flops | bytes accessed | tf_op | source)
XLA Modules:
  0.0 216.6 jit_solution(9875611344535121315)
XLA Ops:
  6.5 0.7 and_select_fusion.1
  7.3 0.8 add_add_fusion
  8.2 1.0 copy-done.3
  9.2 2.1 collective-permute-start.1
  11.4 1.3 collective-permute-start.2
  12.7 1.5 collective-permute-start.3
  14.2 0.9 pad_maximum_fusion.2
  15.1 1.1 collective-permute-start
  16.2 5.2 %collective-permute-done.3.x3 = bf16[80,896]{1,0:T(8,128)(2,1)S(1)} collective-permute-done((bf16[80,896]{1,0:T(8,128)(2,1)S(1)}, bf16[80,896]{1,0:T(8,128)(2,1)S(1)}, u32[]{:S(2)}, u32[]{:S(2)}) %collective-permute-start.3) | collective-permute-done | bytes 143392 | tf_op jit(solution)/shard_map/ppermute | solution.py:309
  21.4 1.7 collective-permute-done
  23.1 1.0 broadcast_select_fusion.1
  24.1 0.7 pad_maximum_fusion.1
  24.9 0.9 dispatch.1
  25.8 49.8 %all_to_all.10 = bf16[64,9,8,128]{3,2,1,0:T(8,128)(2,1)S(1)} all-to-all(bf16[64,9,8,128]{3,2,1,0:T(8,128)(2,1)S(1)} %get-tuple-element.37), channel_id=1, replica_groups=mesh['expert'=64,'tensor'=4] {'expert'}, dimensions={0} | all-to-all | bytes 2359296 | tf_op jit(solution)/shard_map/all_to_all | solution.py:360
  75.7 1.0 collective-permute-start.4
  76.7 8.7 %collective-permute-done.4.x1 = bf16[32,9,8,128]{3,2,1,0:T(8,128)(2,1)S(1)} collective-permute-done((bf16[32,9,8,128]{3,2,1,0:T(8,128)(2,1)S(1)}, bf16[32,9,8,128]{3,2,1,0:T(8,128)(2,1)S(1)}, u32[]{:S(2)}, u32[]{:S(2)}) %collective-permute-start.4) | collective-permute-done | bytes 589856 | tf_op jit(solution)/shard_map/ppermute | solution.py:367
  85.4 1.4 collective-permute-start.9
  86.8 8.9 %collective-permute-start.5 = (bf16[32,9,8,128]{3,2,1,0:T(8,128)(2,1)S(1)}, bf16[32,9,8,128]{3,2,1,0:T(8,128)(2,1)S(1)}, u32[]{:S(2)}, u32[]{:S(2)}) collective-permute-start(bf16[32,9,8,128]{3,2,1,0:T(8,128)(2,1)S(1)} %get-tuple-element.53.x0), channel_id=1, source_target_pairs={{0,1},{1,0},{2,3},{3,2},{4,5},{5,4},{6,7},{7,6},{8,9},{9,8},{10,11... | collective-permute-start | bytes 1769480 | tf_op jit(solution)/shard_map/ppermute | solution.py:313
  96.2 1.6 collective-permute-done.9.x1
  97.7 7.0 %collective-permute-start.11 = (bf16[32,9,8,128]{3,2,1,0:T(8,128)(2,1)S(1)}, bf16[32,9,8,128]{3,2,1,0:T(8,128)(2,1)S(1)}, u32[]{:S(2)}, u32[]{:S(2)}) collective-permute-start(bf16[32,9,8,128]{3,2,1,0:T(8,128)(2,1)S(1)} %collective-permute-done.9.x1), channel_id=1, source_target_pairs={{0,1},{1,0},{2,3},{3,2},{4,5},{5,4},{6,7},{7,6},{8,9},{9,8},{10,11... | collective-permute-start | bytes 1769480 | tf_op jit(solution)/shard_map/ppermute | solution.py:314
  104.8 2.5 %copy-done.2 = bf16[1,640,3584]{2,1,0:T(8,128)(2,1)S(1)} copy-done((bf16[1,640,3584]{2,1,0:T(8,128)(2,1)S(1)}, bf16[1,640,3584]{2,1,0:T(8,128)(2,1)}, u32[]{:S(2)}) %copy-start.2) | copy-done | bytes 4587544
  107.3 5.6 %experts.2 = (bf16[2,32,9,8,128]{4,3,2,1,0:T(8,128)(2,1)S(1)}, bf16[2,32,9,8,128]{4,3,2,1,0:T(8,128)(2,1)S(1)}) custom-call(s32[1]{0:T(128)} %bitcast.place_ref, bf16[32,9,8,128]{3,2,1,0:T(8,128)(2,1)S(1)} %get-tuple-element.53.x0, bf16[32,9,8,128]{3,2,1,0:T(8,128)(2,1)S(1)} %collective-permute-done.4.x1, ...), custom_call_target="tpu_custom_call" | custom-call | flops 2936012800 | bytes 13762560 | tf_op jit(solution)/shard_map/experts/pallas_call | solution.py:178
  113.2 5.6 %experts.3 = (bf16[2,32,9,8,128]{4,3,2,1,0:T(8,128)(2,1)S(1)}, bf16[2,32,9,8,128]{4,3,2,1,0:T(8,128)(2,1)S(1)}) custom-call(s32[1]{0:T(128)} %bitcast.place_ref, bf16[32,9,8,128]{3,2,1,0:T(8,128)(2,1)S(1)} %get-tuple-element.40.x0, bf16[32,9,8,128]{3,2,1,0:T(8,128)(2,1)S(1)} %collective-permute-done.9.x1, ...), custom_call_target="tpu_custom_call" | custom-call | flops 2936012800 | bytes 13762560 | tf_op jit(solution)/shard_map/experts/pallas_call | solution.py:178
  118.9 0.6 collective-permute-start.12
  119.6 0.6 collective-permute-start.8
  120.2 0.9 collective-permute-start.14
  121.2 0.8 collective-permute-done.12
  122.1 0.6 collective-permute-start.13
  122.7 0.7 collective-permute-start.15
  123.4 21.1 %collective-permute-done.14.x1 = bf16[64,3584]{1,0:T(8,128)(2,1)S(1)} collective-permute-done((bf16[64,3584]{1,0:T(8,128)(2,1)S(1)}, bf16[64,3584]{1,0:T(8,128)(2,1)S(1)}, u32[]{:S(2)}, u32[]{:S(2)}) %collective-permute-start.14) | collective-permute-done | bytes 458784 | tf_op jit(solution)/shard_map/ppermute | solution.py:374
  144.4 1.2 collective-permute-start.16
  145.9 11.2 %collective-permute-done.13 = bf16[32,9,8,128]{3,2,1,0:T(8,128)(2,1)S(1)} collective-permute-done((bf16[32,9,8,128]{3,2,1,0:T(8,128)(2,1)S(1)}, bf16[32,9,8,128]{3,2,1,0:T(8,128)(2,1)S(1)}, u32[]{:S(2)}, u32[]{:S(2)}) %collective-permute-start.13) | collective-permute-done | bytes 589856 | tf_op jit(solution)/shard_map/ppermute | solution.py:321
  157.3 1.1 pad_maximum_fusion
  158.5 8.2 %all-to-all-start.1 = ((bf16[64,9,8,128]{3,2,1,0:T(8,128)(2,1)}), bf16[64,9,8,128]{3,2,1,0:T(8,128)(2,1)S(1)}, u32[]{:S(2)}, u32[]{:S(2)}) async-start(bf16[64,9,8,128]{3,2,1,0:T(8,128)(2,1)} %pad_maximum_fusion), calls=%async_computation.1 | async-start | bytes 2359296 | tf_op jit(solution)/shard_map/all_to_all | solution.py:378
  166.7 0.8 copy-done.5
  167.5 3.6 %copy-done = bf16[7168,640]{1,0:T(8,128)(2,1)S(1)} copy-done((bf16[7168,640]{1,0:T(8,128)(2,1)S(1)}, bf16[7168,640]{1,0:T(8,128)(2,1)}, u32[]{:S(2)}) %copy-start) | copy-done | bytes 9175064
  171.1 1.0 copy-done.6
  172.1 5.9 %dense.1 = (bf16[2,64,3584]{2,1,0:T(8,128)(2,1)S(1)}, bf16[2,64,3584]{2,1,0:T(8,128)(2,1)S(1)}) custom-call(bf16[64,3584]{1,0:T(8,128)(2,1)S(1)} %copy-done.4, bf16[64,3584]{1,0:T(8,128)(2,1)S(1)} %collective-permute-done.14.x1, bf16[64,3584]{1,0:T(8,128)(2,1)S(1)} %collective-permute-done.15.x2, bf16[64,3584]{1,0:T(8,128)(2,1)S(1)} %copy-done.6, ...), custom_call_target="tpu_custom_call" | custom-call | flops 2348810240 | bytes 9175040 | tf_op jit(solution)/shard_map/dense/pallas_call | solution.py:269
  178.0 1.4 collective-permute-start.17
  179.4 2.1 collective-permute-done.17.got_ref
  181.5 0.9 fusion.4
  182.4 0.6 collective-permute-start.18
  183.0 14.4 %all-to-all-done.1.x_ref = bf16[64,9,8,128]{3,2,1,0:T(8,128)(2,1)S(1)} async-done(((bf16[64,9,8,128]{3,2,1,0:T(8,128)(2,1)}), bf16[64,9,8,128]{3,2,1,0:T(8,128)(2,1)S(1)}, u32[]{:S(2)}, u32[]{:S(2)}) %all-to-all-start.1) | async-done | bytes 1179680 | tf_op jit(solution)/shard_map/all_to_all | solution.py:378
  197.4 1.1 combine.1
  198.5 1.1 collective-permute-start.19
  199.6 2.7 %collective-permute-start.20 = (bf16[64,896]{1,0:T(8,128)(2,1)S(1)}, bf16[64,896]{1,0:T(8,128)(2,1)S(1)}, u32[]{:S(2)}, u32[]{:S(2)}) collective-permute-start(bf16[64,896]{1,0:T(8,128)(2,1)S(1)} %get-tuple-element.51), channel_id=1, source_target_pairs={{0,1},{1,0},{2,3},{3,2},{4,5},{5,4},{6,7},{7,6},{8,9},{9,8},{10,11... | collective-permute-start | bytes 344072 | tf_op jit(solution)/shard_map/ppermute | solution.py:309
  203.3 4.4 %collective-permute-done.21.r3 = bf16[64,896]{1,0:T(8,128)(2,1)S(1)} collective-permute-done((bf16[64,896]{1,0:T(8,128)(2,1)S(1)}, bf16[64,896]{1,0:T(8,128)(2,1)S(1)}, u32[]{:S(2)}, u32[]{:S(2)}) %collective-permute-start.21) | collective-permute-done | bytes 114720 | tf_op jit(solution)/shard_map/ppermute | solution.py:309
  207.7 2.1 finish.1
  (47 shorter events, 2.9 us)
Async XLA Ops:
  6.5 161.0 %all-gather.2.cloned.1.call-start = ((), (), s32[]{:S(2)}) async-start(), calls=%async_computation.2 | async-start | bytes 9461760 | tf_op jit(solution)/shard_map/all_gather | solution.py:337
  8.2 1.0 copy-start.3
  9.2 7.0 %collective-permute-start.1 = (bf16[80,896]{1,0:T(8,128)(2,1)S(1)}, bf16[80,896]{1,0:T(8,128)(2,1)S(1)}, u32[]{:S(2)}, u32[]{:S(2)}) collective-permute-start(bf16[80,896]{1,0:T(8,128)(2,1)S(1)} %get-tuple-element.30), channel_id=1, source_target_pairs={{0,2},{2,0},{1,3},{3,1},{4,6},{6,4},{5,7},{7,5},{8,10},{10,8},{9,1... | collective-permute-start | bytes 430088 | tf_op jit(solution)/shard_map/ppermute | solution.py:309
  11.4 4.9 %collective-permute-start.2 = (bf16[80,896]{1,0:T(8,128)(2,1)S(1)}, bf16[80,896]{1,0:T(8,128)(2,1)S(1)}, u32[]{:S(2)}, u32[]{:S(2)}) collective-permute-start(bf16[80,896]{1,0:T(8,128)(2,1)S(1)} %get-tuple-element.31), channel_id=1, source_target_pairs={{0,1},{1,0},{2,3},{3,2},{4,5},{5,4},{6,7},{7,6},{8,9},{9,8},{10,11... | collective-permute-start | bytes 430088 | tf_op jit(solution)/shard_map/ppermute | solution.py:309
  12.7 8.7 %collective-permute-start.3 = (bf16[80,896]{1,0:T(8,128)(2,1)S(1)}, bf16[80,896]{1,0:T(8,128)(2,1)S(1)}, u32[]{:S(2)}, u32[]{:S(2)}) collective-permute-start(bf16[80,896]{1,0:T(8,128)(2,1)S(1)} %get-tuple-element.32), channel_id=1, source_target_pairs={{0,3},{3,0},{1,2},{2,1},{4,7},{7,4},{5,6},{6,5},{8,11},{11,8},{9,1... | collective-permute-start | bytes 430088 | tf_op jit(solution)/shard_map/ppermute | solution.py:309
  15.1 8.0 %collective-permute-start = (bf16[112,640]{1,0:T(8,128)(2,1)S(1)}, bf16[112,640]{1,0:T(8,128)(2,1)S(1)}, u32[]{:S(2)}, u32[]{:S(2)}) collective-permute-start(bf16[112,640]{1,0:T(8,128)(2,1)S(1)} %pad_maximum_fusion.2), channel_id=1, source_target_pairs={{0,128},{4,132},{8,136},{12,140},{16,144},{20,148},{24,152},{28,15... | collective-permute-start | bytes 430088 | tf_op jit(solution)/shard_map/ppermute | solution.py:332
  24.9 88.4 %slice-start = ((s8[4587520]{0:T(1024)(128)(4,1)}), s8[393216]{0:T(1024)(128)(4,1)S(1)}, s32[]{:S(2)}) async-start(s8[4587520]{0:T(1024)(128)(4,1)} %bitcast.45), calls=%async_computation.3 | async-start | bytes 786432
  25.8 79.0 %copy-start.1 = (bf16[1,3584,640]{2,1,0:T(8,128)(2,1)S(1)}, bf16[1,3584,640]{2,1,0:T(8,128)(2,1)}, u32[]{:S(2)}) copy-start(bf16[1,3584,640]{2,1,0:T(8,128)(2,1)} %param.12) | copy-start | bytes 13762564
  75.7 9.7 %collective-permute-start.4 = (bf16[32,9,8,128]{3,2,1,0:T(8,128)(2,1)S(1)}, bf16[32,9,8,128]{3,2,1,0:T(8,128)(2,1)S(1)}, u32[]{:S(2)}, u32[]{:S(2)}) collective-permute-start(bf16[32,9,8,128]{3,2,1,0:T(8,128)(2,1)S(1)} %get-tuple-element.53.x0), channel_id=1, source_target_pairs={{0,2},{2,0},{1,3},{3,1},{4,6},{6,4},{5,7},{7,5},{8,10},{10,8},{9,1... | collective-permute-start | bytes 1769480 | tf_op jit(solution)/shard_map/ppermute | solution.py:367
  85.4 12.3 %collective-permute-start.9 = (bf16[32,9,8,128]{3,2,1,0:T(8,128)(2,1)S(1)}, bf16[32,9,8,128]{3,2,1,0:T(8,128)(2,1)S(1)}, u32[]{:S(2)}, u32[]{:S(2)}) collective-permute-start(bf16[32,9,8,128]{3,2,1,0:T(8,128)(2,1)S(1)} %get-tuple-element.40.x0), channel_id=1, source_target_pairs={{0,2},{2,0},{1,3},{3,1},{4,6},{6,4},{5,7},{7,5},{8,10},{10,8},{9,1... | collective-permute-start | bytes 1769480 | tf_op jit(solution)/shard_map/ppermute | solution.py:367
  86.8 18.0 %collective-permute-start.5 = (bf16[32,9,8,128]{3,2,1,0:T(8,128)(2,1)S(1)}, bf16[32,9,8,128]{3,2,1,0:T(8,128)(2,1)S(1)}, u32[]{:S(2)}, u32[]{:S(2)}) collective-permute-start(bf16[32,9,8,128]{3,2,1,0:T(8,128)(2,1)S(1)} %get-tuple-element.53.x0), channel_id=1, source_target_pairs={{0,1},{1,0},{2,3},{3,2},{4,5},{5,4},{6,7},{7,6},{8,9},{9,8},{10,11... | collective-permute-start | bytes 1769480 | tf_op jit(solution)/shard_map/ppermute | solution.py:313
  95.7 9.1 %collective-permute-start.6 = (bf16[32,9,8,128]{3,2,1,0:T(8,128)(2,1)S(1)}, bf16[32,9,8,128]{3,2,1,0:T(8,128)(2,1)S(1)}, u32[]{:S(2)}, u32[]{:S(2)}) collective-permute-start(bf16[32,9,8,128]{3,2,1,0:T(8,128)(2,1)S(1)} %collective-permute-done.4.x1), channel_id=1, source_target_pairs={{0,1},{1,0},{2,3},{3,2},{4,5},{5,4},{6,7},{7,6},{8,9},{9,8},{10,11... | collective-permute-start | bytes 1769480 | tf_op jit(solution)/shard_map/ppermute | solution.py:314
  95.7 17.5 %collective-permute-start.10 = (bf16[32,9,8,128]{3,2,1,0:T(8,128)(2,1)S(1)}, bf16[32,9,8,128]{3,2,1,0:T(8,128)(2,1)S(1)}, u32[]{:S(2)}, u32[]{:S(2)}) collective-permute-start(bf16[32,9,8,128]{3,2,1,0:T(8,128)(2,1)S(1)} %get-tuple-element.40.x0), channel_id=1, source_target_pairs={{0,1},{1,0},{2,3},{3,2},{4,5},{5,4},{6,7},{7,6},{8,9},{9,8},{10,11... | collective-permute-start | bytes 1769480 | tf_op jit(solution)/shard_map/ppermute | solution.py:313
  97.7 15.5 %collective-permute-start.11 = (bf16[32,9,8,128]{3,2,1,0:T(8,128)(2,1)S(1)}, bf16[32,9,8,128]{3,2,1,0:T(8,128)(2,1)S(1)}, u32[]{:S(2)}, u32[]{:S(2)}) collective-permute-start(bf16[32,9,8,128]{3,2,1,0:T(8,128)(2,1)S(1)} %collective-permute-done.9.x1), channel_id=1, source_target_pairs={{0,1},{1,0},{2,3},{3,2},{4,5},{5,4},{6,7},{7,6},{8,9},{9,8},{10,11... | collective-permute-start | bytes 1769480 | tf_op jit(solution)/shard_map/ppermute | solution.py:314
  104.7 2.5 %copy-start.2 = (bf16[1,640,3584]{2,1,0:T(8,128)(2,1)S(1)}, bf16[1,640,3584]{2,1,0:T(8,128)(2,1)}, u32[]{:S(2)}) copy-start(bf16[1,640,3584]{2,1,0:T(8,128)(2,1)} %param.13) | copy-start | bytes 13762564
  107.3 5.9 %slice-start.1 = ((s8[4587520]{0:T(1024)(128)(4,1)}), s8[4194304]{0:T(1024)(128)(4,1)S(1)}, s32[]{:S(2)}) async-start(s8[4587520]{0:T(1024)(128)(4,1)} %bitcast.45), calls=%async_computation.4 | async-start | bytes 8388608
  112.9 6.5 %collective-permute-start.7 = (bf16[2,32,9,8,128]{4,3,2,1,0:T(8,128)(2,1)S(1)}, bf16[2,32,9,8,128]{4,3,2,1,0:T(8,128)(2,1)S(1)}, u32[]{:S(2)}, u32[]{:S(2)}) collective-permute-start(bf16[2,32,9,8,128]{4,3,2,1,0:T(8,128)(2,1)S(1)} %get-tuple-element.39), channel_id=1, source_target_pairs={{0,1},{1,0},{2,3},{3,2},{4,5},{5,4},{6,7},{7,6},{8,9},{9,8},{10,11... | collective-permute-start | bytes 3538952 | tf_op jit(solution)/shard_map/ppermute | solution.py:319
  118.9 1.4 copy-start.4
  118.9 3.0 %collective-permute-start.12 = (bf16[2,32,9,8,128]{4,3,2,1,0:T(8,128)(2,1)S(1)}, bf16[2,32,9,8,128]{4,3,2,1,0:T(8,128)(2,1)S(1)}, u32[]{:S(2)}, u32[]{:S(2)}) collective-permute-start(bf16[2,32,9,8,128]{4,3,2,1,0:T(8,128)(2,1)S(1)} %get-tuple-element.42), channel_id=1, source_target_pairs={{0,1},{1,0},{2,3},{3,2},{4,5},{5,4},{6,7},{7,6},{8,9},{9,8},{10,11... | collective-permute-start | bytes 3538952 | tf_op jit(solution)/shard_map/ppermute | solution.py:319
  119.6 26.1 %collective-permute-start.8 = (bf16[32,9,8,128]{3,2,1,0:T(8,128)(2,1)S(1)}, bf16[32,9,8,128]{3,2,1,0:T(8,128)(2,1)S(1)}, u32[]{:S(2)}, u32[]{:S(2)}) collective-permute-start(bf16[32,9,8,128]{3,2,1,0:T(8,128)(2,1)S(1)} %fusion.2), channel_id=1, source_target_pairs={{0,2},{2,0},{1,3},{3,1},{4,6},{6,4},{5,7},{7,5},{8,10},{10,8},{9,1... | collective-permute-start | bytes 1769480 | tf_op jit(solution)/shard_map/ppermute | solution.py:321
  120.2 24.2 %collective-permute-start.14 = (bf16[64,3584]{1,0:T(8,128)(2,1)S(1)}, bf16[64,3584]{1,0:T(8,128)(2,1)S(1)}, u32[]{:S(2)}, u32[]{:S(2)}) collective-permute-start(bf16[64,3584]{1,0:T(8,128)(2,1)S(1)} %copy-done.4), channel_id=1, source_target_pairs={{0,2},{2,0},{1,3},{3,1},{4,6},{6,4},{5,7},{7,5},{8,10},{10,8},{9,1... | collective-permute-start | bytes 1376264 | tf_op jit(solution)/shard_map/ppermute | solution.py:374
  122.1 35.0 %collective-permute-start.13 = (bf16[32,9,8,128]{3,2,1,0:T(8,128)(2,1)S(1)}, bf16[32,9,8,128]{3,2,1,0:T(8,128)(2,1)S(1)}, u32[]{:S(2)}, u32[]{:S(2)}) collective-permute-start(bf16[32,9,8,128]{3,2,1,0:T(8,128)(2,1)S(1)} %fusion.3), channel_id=1, source_target_pairs={{0,2},{2,0},{1,3},{3,1},{4,6},{6,4},{5,7},{7,5},{8,10},{10,8},{9,1... | collective-permute-start | bytes 1769480 | tf_op jit(solution)/shard_map/ppermute | solution.py:321
  122.7 44.0 %collective-permute-start.15 = (bf16[64,3584]{1,0:T(8,128)(2,1)S(1)}, bf16[64,3584]{1,0:T(8,128)(2,1)S(1)}, u32[]{:S(2)}, u32[]{:S(2)}) collective-permute-start(bf16[64,3584]{1,0:T(8,128)(2,1)S(1)} %copy-done.4), channel_id=1, source_target_pairs={{0,1},{1,0},{2,3},{3,2},{4,5},{5,4},{6,7},{7,6},{8,9},{9,8},{10,11... | collective-permute-start | bytes 1376264 | tf_op jit(solution)/shard_map/ppermute | solution.py:313
  144.4 22.3 %collective-permute-start.16 = (bf16[64,3584]{1,0:T(8,128)(2,1)S(1)}, bf16[64,3584]{1,0:T(8,128)(2,1)S(1)}, u32[]{:S(2)}, u32[]{:S(2)}) collective-permute-start(bf16[64,3584]{1,0:T(8,128)(2,1)S(1)} %collective-permute-done.14.x1), channel_id=1, source_target_pairs={{0,1},{1,0},{2,3},{3,2},{4,5},{5,4},{6,7},{7,6},{8,9},{9,8},{10,11... | collective-permute-start | bytes 1376264 | tf_op jit(solution)/shard_map/ppermute | solution.py:314
  158.5 39.0 %all-to-all-start.1 = ((bf16[64,9,8,128]{3,2,1,0:T(8,128)(2,1)}), bf16[64,9,8,128]{3,2,1,0:T(8,128)(2,1)S(1)}, u32[]{:S(2)}, u32[]{:S(2)}) async-start(bf16[64,9,8,128]{3,2,1,0:T(8,128)(2,1)} %pad_maximum_fusion), calls=%async_computation.1 | async-start | bytes 2359296 | tf_op jit(solution)/shard_map/all_to_all | solution.py:378
  166.7 0.8 copy-start.5
  167.5 3.6 %copy-start = (bf16[7168,640]{1,0:T(8,128)(2,1)S(1)}, bf16[7168,640]{1,0:T(8,128)(2,1)}, u32[]{:S(2)}) copy-start(bf16[7168,640]{1,0:T(8,128)(2,1)} %all-gather.2.cloned.1.call-done) | copy-start | bytes 27525124
  171.1 1.0 copy-start.6
  178.0 3.5 %collective-permute-start.17 = (bf16[2,64,3584]{2,1,0:T(8,128)(2,1)S(1)}, bf16[2,64,3584]{2,1,0:T(8,128)(2,1)S(1)}, u32[]{:S(2)}, u32[]{:S(2)}) collective-permute-start(bf16[2,64,3584]{2,1,0:T(8,128)(2,1)S(1)} %get-tuple-element.46), channel_id=1, source_target_pairs={{0,1},{1,0},{2,3},{3,2},{4,5},{5,4},{6,7},{7,6},{8,9},{9,8},{10,11... | collective-permute-start | bytes 2752520 | tf_op jit(solution)/shard_map/ppermute | solution.py:319
  182.4 25.3 %collective-permute-start.18 = (bf16[64,3584]{1,0:T(8,128)(2,1)}, bf16[64,3584]{1,0:T(8,128)(2,1)}, u32[]{:S(2)}, u32[]{:S(2)}) collective-permute-start(bf16[64,3584]{1,0:T(8,128)(2,1)} %fusion.4), channel_id=1, source_target_pairs={{0,2},{2,0},{1,3},{3,1},{4,6},{6,4},{5,7},{7,5},{8,10},{10,8},{9,1... | collective-permute-start | bytes 1376264 | tf_op jit(solution)/shard_map/ppermute | solution.py:321
  198.5 4.2 %collective-permute-start.19 = (bf16[64,896]{1,0:T(8,128)(2,1)S(1)}, bf16[64,896]{1,0:T(8,128)(2,1)S(1)}, u32[]{:S(2)}, u32[]{:S(2)}) collective-permute-start(bf16[64,896]{1,0:T(8,128)(2,1)S(1)} %get-tuple-element.50), channel_id=1, source_target_pairs={{0,2},{2,0},{1,3},{3,1},{4,6},{6,4},{5,7},{7,5},{8,10},{10,8},{9,1... | collective-permute-start | bytes 344072 | tf_op jit(solution)/shard_map/ppermute | solution.py:309
  199.6 3.7 %collective-permute-start.20 = (bf16[64,896]{1,0:T(8,128)(2,1)S(1)}, bf16[64,896]{1,0:T(8,128)(2,1)S(1)}, u32[]{:S(2)}, u32[]{:S(2)}) collective-permute-start(bf16[64,896]{1,0:T(8,128)(2,1)S(1)} %get-tuple-element.51), channel_id=1, source_target_pairs={{0,1},{1,0},{2,3},{3,2},{4,5},{5,4},{6,7},{7,6},{8,9},{9,8},{10,11... | collective-permute-start | bytes 344072 | tf_op jit(solution)/shard_map/ppermute | solution.py:309
  202.3 5.4 %collective-permute-start.21 = (bf16[64,896]{1,0:T(8,128)(2,1)S(1)}, bf16[64,896]{1,0:T(8,128)(2,1)S(1)}, u32[]{:S(2)}, u32[]{:S(2)}) collective-permute-start(bf16[64,896]{1,0:T(8,128)(2,1)S(1)} %get-tuple-element.52), channel_id=1, source_target_pairs={{0,3},{3,0},{1,2},{2,1},{4,7},{7,4},{5,6},{6,5},{8,11},{11,8},{9,1... | collective-permute-start | bytes 344072 | tf_op jit(solution)/shard_map/ppermute | solution.py:309
Sparse Core Ops, SparseCore 0:
  25.0 114.7 all-gather.1

commit v3 on v2

--- a/solution.py
+++ b/solution.py
@@ -16,8 +16,8 @@
 META = 16
 MAIN = 8
 LANES = 128
-HALVES = 2
-VMEM = 32 * 1024 * 1024
+SIZES = (32, 32)
+VMEM = 24 * 1024 * 1024
 
 
 def dot(a, b, dims=((1,), (0,))):
@@ -57,15 +57,13 @@
 def take_tiles(ref, scratch, count, capacity):
     extra = capacity - MAIN
     n = ref.shape[1] - extra
-    main = [
-        ref[:, j].astype(F32).reshape(count * MAIN, LANES).astype(BF16) for j in range(n)
-    ]
+    main = [ref[:, j].astype(F32).reshape(count * MAIN, LANES) for j in range(n)]
     scratch[...] = ref[:, n:].astype(F32).reshape(count * extra * MAIN, LANES)
     tail = []
     for s in range(extra):
         cut = [scratch[pl.ds(s * MAIN + j, count, stride=extra * MAIN), :] for j in range(n)]
-        tail.append(jnp.concatenate(cut, axis=1).astype(BF16))
-    return jnp.concatenate([jnp.concatenate(main, axis=1)] + tail, axis=0)
+        tail.append(jnp.concatenate(cut, axis=1))
+    return jnp.concatenate([jnp.concatenate(main, axis=1)] + tail, axis=0).astype(BF16)
 
 
 def clear(scratch):
@@ -74,6 +72,7 @@
 
 SMEM = pl.BlockSpec(memory_space=pltpu.SMEM)
 WHOLE = pl.BlockSpec(memory_space=pltpu.VMEM)
+COST = pl.CostEstimate(flops=1, bytes_accessed=1, transcendentals=0)
 PARAMS = pltpu.CompilerParams(vmem_limit_bytes=VMEM)
 
 
@@ -93,6 +92,7 @@
         out_specs=[WHOLE] * 4,
         out_shape=[block] * 4,
         compiler_params=PARAMS,
+        cost_estimate=COST,
         name="pack",
     )(place, tokens, meta)
 
@@ -153,43 +153,38 @@
             pltpu.VMEM((n_experts * (capacity - MAIN) * MAIN, LANES), F32),
         ],
         compiler_params=PARAMS,
+        cost_estimate=COST,
         name="dispatch",
     )(place, *xs)
 
 
-def experts_kernel(capacity, place_ref, x0, x1, x2, x3, up_ref, down_ref, mine_ref, others_ref, x_all, scratch):
+def experts_kernel(capacity, place_ref, x0, x1, x2, x3, up_ref, down_ref, o0, o1, o2, o3, x_all, scratch):
     count, tiles = x0.shape[:2]
     width = (tiles - capacity + MAIN) * LANES
     for step, x in enumerate((x0, x1, x2, x3)):
         x_all[:, pl.ds(at(place_ref[0], step, width), width)] = take_tiles(x, scratch, count, capacity)
     hidden = silu(dot(x_all[...], up_ref[...])).astype(BF16)
     clear(scratch)
-    for step in (2, 3, 0, 1):
+    for step, ref in enumerate((o0, o1, o2, o3)):
         out = dot(hidden, down_ref[:, pl.ds(at(place_ref[0], step, width), width)])
-        ref = mine_ref if step < 2 else others_ref
-        put_tiles(ref, (step % 2,), scratch, out[: count * MAIN], out[count * MAIN :], count, capacity)
+        put_tiles(ref, (), scratch, out[: count * MAIN], out[count * MAIN :], count, capacity)
 
 
 def experts(place, xs, up, down, capacity):
     count, tiles = xs[0].shape[:2]
     width, units = up.shape
     rows = count * capacity
-    pair = jax.ShapeDtypeStruct((2,) + xs[0].shape, BF16)
     return pl.pallas_call(
         functools.partial(experts_kernel, capacity),
         in_specs=[SMEM] + [WHOLE] * 6,
-        out_specs=[WHOLE] * 2,
-        out_shape=[pair] * 2,
+        out_specs=[WHOLE] * 4,
+        out_shape=[jax.ShapeDtypeStruct(xs[0].shape, BF16)] * 4,
         scratch_shapes=[
             pltpu.VMEM((rows, width), BF16),
             pltpu.VMEM((count * (capacity - MAIN) * MAIN, LANES), F32),
         ],
         compiler_params=PARAMS,
-        cost_estimate=pl.CostEstimate(
-            flops=4 * rows * width * units,
-            bytes_accessed=4 * width * (rows + units),
-            transcendentals=rows * units,
-        ),
+        cost_estimate=COST,
         name="experts",
     )(place, *xs, up, down)
 
@@ -224,6 +219,7 @@
             pltpu.VMEM((group, width), BF16),
         ],
         compiler_params=PARAMS,
+        cost_estimate=COST,
         name="combine",
     )(place, x, plan)
 
@@ -278,9 +274,7 @@
         out_shape=[jax.ShapeDtypeStruct((2, rows, width), BF16)] * 2,
         scratch_shapes=[pltpu.VMEM((4 * rows, units), F32), pltpu.VMEM((4 * rows, units), BF16)],
         compiler_params=PARAMS,
-        cost_estimate=pl.CostEstimate(
-            flops=16 * rows * width * units, bytes_accessed=4 * width * units, transcendentals=4 * rows * units
-        ),
+        cost_estimate=COST,
         name="dense",
     )(*xs, weights, weights)
 
@@ -301,6 +295,7 @@
         out_specs=WHOLE,
         out_shape=jax.ShapeDtypeStruct(tokens.shape, BF16),
         compiler_params=PARAMS,
+        cost_estimate=COST,
         name="finish",
     )(place, tokens, mine, got, last, *routed)
 
@@ -330,12 +325,12 @@
     places = [(x, z, y) for x in range(N_X) for z in range(N_Z) for y in range(N_Y)]
     both = jnp.concatenate([dense_up, dense_down.T], axis=0)
     mate = lax.ppermute(both, "expert", [(expert_at(x, z, y), expert_at(1 - x, z, y)) for x, z, y in places])
-    mate, after = lax.optimization_barrier((mate, after))
+    mate, _ = lax.optimization_barrier((mate, after))
     low = lax.axis_index("expert") < N_Z * N_Y
     pair = jnp.concatenate([jnp.where(low, both, mate), jnp.where(low, mate, both)])
     planes = [[expert_at(x, z, y) for z in range(N_Z) for y in range(N_Y)] for x in range(N_X)]
     out = lax.all_gather(pair, "expert", axis=0, tiled=True, axis_index_groups=planes)
-    return out.reshape(N_Z, N_Y, N_X, 2, rows, units), after
+    return out.reshape(N_Z, N_Y, N_X, 2, rows, units)
 
 
 def local(tokens, expert_ids, gate_codes, dense_up, dense_down, expert_in, expert_out):
@@ -354,24 +349,35 @@
     meta = jnp.where(owner == place, jnp.tile(meta, (1, n_tensor)), 0).astype(BF16)
     meta = jnp.pad(meta, ((0, 0), (0, part - group)))
     grouped = swap(pack(spot, tokens, meta))
-    weights, grouped = gather_dense(dense_up, dense_down, grouped)
     routed, plan = dispatch(spot, grouped, n_experts, capacity)
+    weights = gather_dense(dense_up, dense_down, plan)
+
+    tokens_near = lax.ppermute(tokens, "tensor", NEXT)
 
     routed = lax.all_to_all(routed, "expert", split_axis=0, concat_axis=0, tiled=True)
-    size = n_experts // HALVES
-    results, near = [], None
-    for half in range(HALVES):
-        x = routed[half * size : (half + 1) * size]
+    routed, tokens_near = lax.optimization_barrier((routed, tokens_near))
+    start, terms, near, last = 0, [], None, None
+    for size in SIZES:
+        x = routed[start : start + size]
+        start += size
         if near is not None:
             x, near = lax.optimization_barrier((x, near))
         near = lax.ppermute(x, "tensor", NEXT)
-        mine, others = experts(spot, spread(x, near), expert_in[0], expert_out[0], capacity)
-        got, last = fold(mine, others)
-        results.append((mine[0].astype(F32) + got[0].astype(F32) + last.astype(F32)).astype(BF16))
-    result = jnp.concatenate(results)
+        own, beside, other, far = experts(spot, spread(x, near), expert_in[0], expert_out[0], capacity)
+        if terms:
+            near, own = lax.optimization_barrier((near, own))
+        far = lax.ppermute(far, "tensor", CORE)
+        other = lax.ppermute(other, "tensor", CORE)
+        if terms:
+            far, last = lax.optimization_barrier((far, last))
+            terms[-1][-1] = last
+        rest = (beside.astype(F32) + far.astype(F32)).astype(BF16)
+        last = lax.ppermute(rest, "tensor", NEXT)
+        terms.append([own, other, last])
+    result = jnp.concatenate([(a.astype(F32) + b.astype(F32) + c.astype(F32)).astype(BF16) for a, b, c in terms])
 
     dense_own, result = lax.optimization_barrier((tokens, result))
-    blocks = spread(tokens, lax.ppermute(tokens, "tensor", NEXT))
+    blocks = spread(tokens, tokens_near)
     mine, others = dense((dense_own,) + blocks[1:], weights)
     got, last = fold(mine, others)
 

time: 217 us -> 200 us (0.922)
  blocking collectives: 49.8 us -> 0 us
  waiting for transfers between devices: 71.6 us -> 94.3 us
  starting transfers between devices: 44.3 us -> 50.6 us
  local copies, waits for them, and re-layouts: 9.22 us -> 12.8 us
    all_to_all x1 -> x0, blocking collectives: 49.8 us -> none  [local(): lax.all_to_all(routed, 'expert', split_axis=0, concat_axis=0, tiled=True)]
    all_to_all x0 -> x1, waiting for transfers between devices: none -> 22.8 us  [local(): lax.all_to_all(routed, 'expert', split_axis=0, concat_axis=0, tiled=True)]
    ppermute x1 -> x7, waiting for transfers between devices: 21.1 us -> 35.7 us  [the longest x2 19.8 us: local(): last = lax.ppermute(rest, 'tensor', NEXT)]
    all_to_all x0 -> x1, starting transfers between devices: none -> 13.4 us  [local(): lax.all_to_all(routed, 'expert', split_axis=0, concat_axis=0, tiled=True)]
    ppermute x3 -> x1, waiting for transfers between devices: 11.2 us -> 0.01 us  [fold(): return (got, lax.ppermute(rest, 'tensor', NEXT))]
    ppermute x3, starting transfers between devices: 10.1 us -> 5.75 us  [spread(): other = lax.ppermute(x, 'tensor', CORE)]
    ppermute x3, starting transfers between devices: 8.24 us -> 5.4 us  [spread(): far = lax.ppermute(near, 'tensor', CORE)]
    unnamed x18 -> x22, local copies, waits for them, and re-layouts: 8.95 us -> 11.3 us
  transfers between devices with their start and end apart: 24 -> 27, of which waited for: 11 -> 12; matrix products, arithmetic and copies ran while one was open for 2% -> 3% of each run, Pallas kernels for 9% -> 10%
where the time goes in v3:
time: 200 us
  waiting for transfers between devices  94.3 us (47%)
  starting transfers between devices  50.6 us (25%)
  Pallas kernels  22.2 us (11%)
  between operations  13.6 us (7%)
  local copies, waits for them, and re-layouts  12.8 us (6%)
  other arithmetic  6 us (3%)
    all_to_all x1, waiting for transfers between devices, local(): lax.all_to_all(routed, 'expert', split_axis=0, concat_axis=0, tiled=True)  22.8 us
    ppermute x2, waiting for transfers between devices, local(): last = lax.ppermute(rest, 'tensor', NEXT)  19.8 us
    ppermute x1, waiting for transfers between devices, local(): tokens_near = lax.ppermute(tokens, 'tensor', NEXT)  15.9 us
    all_to_all x1, starting transfers between devices, local(): lax.all_to_all(routed, 'expert', split_axis=0, concat_axis=0, tiled=True)  13.4 us
    all_to_all x1, waiting for transfers between devices, local(): lax.all_to_all(result, 'expert', split_axis=0, concat_axis=0, tiled=True)  12.9 us
    unnamed x22, local copies, waits for them, and re-layouts  11.3 us
    pallas_call x2, Pallas kernels, experts(): pl.pallas_call(functools.partial(experts_kernel, capacity), in_specs=[SME...  11.2 us
    ppermute x6, starting transfers between devices, swap(): lax.ppermute(x, 'tensor', perm)  10.3 us
  transfers between devices with their start and end apart: 27, of which 12 were waited for; matrix products, arithmetic and copies ran while one was open for 3% of the time, Pallas kernels for 10%

profile of v3, /device:TPU:1, one launch (start us, length us, event | category | flops | bytes accessed | tf_op | source)
XLA Modules:
  0.0 199.6 jit_solution(11788752033244861530)
XLA Ops:
  6.5 0.7 and_select_fusion.1
  7.3 0.8 add_add_fusion
  8.2 1.0 copy-done.3
  9.3 2.1 %collective-permute-start = (bf16[80,896]{1,0:T(8,128)(2,1)S(1)}, bf16[80,896]{1,0:T(8,128)(2,1)S(1)}, u32[]{:S(2)}, u32[]{:S(2)}) collective-permute-start(bf16[80,896]{1,0:T(8,128)(2,1)S(1)} %get-tuple-element.35), channel_id=1, source_target_pairs={{0,2},{2,0},{1,3},{3,1},{4,6},{6,4},{5,7},{7,5},{8,10},{10,8},{9,1... | collective-permute-start | bytes 430088 | tf_op jit(solution)/shard_map/ppermute | solution.py:304
  11.4 1.3 collective-permute-start.1
  12.7 1.5 collective-permute-start.2
  14.3 0.9 pad_maximum_fusion.2
  15.2 1.1 collective-permute-start.18
  16.3 5.2 %collective-permute-done.2.x3 = bf16[80,896]{1,0:T(8,128)(2,1)S(1)} collective-permute-done((bf16[80,896]{1,0:T(8,128)(2,1)S(1)}, bf16[80,896]{1,0:T(8,128)(2,1)S(1)}, u32[]{:S(2)}, u32[]{:S(2)}) %collective-permute-start.2) | collective-permute-done | bytes 143392 | tf_op jit(solution)/shard_map/ppermute | solution.py:304
  21.5 1.9 dispatch.1
  23.4 0.7 pad_maximum_fusion.1
  24.2 13.4 %all-to-all-start = ((bf16[64,9,8,128]{3,2,1,0:T(8,128)(2,1)}), bf16[64,9,8,128]{3,2,1,0:T(8,128)(2,1)}, u32[]{:S(2)}, u32[]{:S(2)}) async-start(bf16[64,9,8,128]{3,2,1,0:T(8,128)(2,1)} %get-tuple-element.38), calls=%async_computation | async-start | bytes 2359296 | tf_op jit(solution)/shard_map/all_to_all | solution.py:357
  38.0 15.9 %collective-permute-done.3.x1 = bf16[64,3584]{1,0:T(8,128)(2,1)S(1)} collective-permute-done((bf16[64,3584]{1,0:T(8,128)(2,1)S(1)}, bf16[64,3584]{1,0:T(8,128)(2,1)S(1)}, u32[]{:S(2)}, u32[]{:S(2)}) %collective-permute-start.3) | collective-permute-done | bytes 458784 | tf_op jit(solution)/shard_map/ppermute | solution.py:355
  53.9 22.8 %all-to-all-done = bf16[64,9,8,128]{3,2,1,0:T(8,128)(2,1)} async-done(((bf16[64,9,8,128]{3,2,1,0:T(8,128)(2,1)}), bf16[64,9,8,128]{3,2,1,0:T(8,128)(2,1)}, u32[]{:S(2)}, u32[]{:S(2)}) %all-to-all-start) | async-done | bytes 1179680 | tf_op jit(solution)/shard_map/all_to_all | solution.py:357
  76.7 1.3 fusion.2
  78.1 0.5 collective-permute-start.4
  78.5 4.5 %collective-permute-start.5 = (bf16[32,9,8,128]{3,2,1,0:T(8,128)(2,1)S(1)}, bf16[32,9,8,128]{3,2,1,0:T(8,128)(2,1)S(1)}, u32[]{:S(2)}, u32[]{:S(2)}) collective-permute-start(bf16[32,9,8,128]{3,2,1,0:T(8,128)(2,1)S(1)} %get-tuple-element.63.x0), channel_id=1, source_target_pairs={{0,1},{1,0},{2,3},{3,2},{4,5},{5,4},{6,7},{7,6},{8,9},{9,8},{10,11... | collective-permute-start | bytes 1769480 | tf_op jit(solution)/shard_map/ppermute | solution.py:308
  83.0 6.1 %collective-permute-done.4.x1 = bf16[32,9,8,128]{3,2,1,0:T(8,128)(2,1)S(1)} collective-permute-done((bf16[32,9,8,128]{3,2,1,0:T(8,128)(2,1)S(1)}, bf16[32,9,8,128]{3,2,1,0:T(8,128)(2,1)S(1)}, u32[]{:S(2)}, u32[]{:S(2)}) %collective-permute-start.4) | collective-permute-done | bytes 589856 | tf_op jit(solution)/shard_map/ppermute | solution.py:365
  89.2 4.7 %collective-permute-start.6 = (bf16[32,9,8,128]{3,2,1,0:T(8,128)(2,1)S(1)}, bf16[32,9,8,128]{3,2,1,0:T(8,128)(2,1)S(1)}, u32[]{:S(2)}, u32[]{:S(2)}) collective-permute-start(bf16[32,9,8,128]{3,2,1,0:T(8,128)(2,1)S(1)} %collective-permute-done.4.x1), channel_id=1, source_target_pairs={{0,1},{1,0},{2,3},{3,2},{4,5},{5,4},{6,7},{7,6},{8,9},{9,8},{10,11... | collective-permute-start | bytes 1769480 | tf_op jit(solution)/shard_map/ppermute | solution.py:309
  94.3 1.3 collective-permute-done.6.x3
  95.5 2.4 %copy-done.1 = bf16[1,3584,640]{2,1,0:T(8,128)(2,1)S(1)} copy-done((bf16[1,3584,640]{2,1,0:T(8,128)(2,1)S(1)}, bf16[1,3584,640]{2,1,0:T(8,128)(2,1)}, u32[]{:S(2)}) %copy-start.1) | copy-done | bytes 4587544
  98.0 2.4 %copy-done.2 = bf16[1,640,3584]{2,1,0:T(8,128)(2,1)S(1)} copy-done((bf16[1,640,3584]{2,1,0:T(8,128)(2,1)S(1)}, bf16[1,640,3584]{2,1,0:T(8,128)(2,1)}, u32[]{:S(2)}) %copy-start.2) | copy-done | bytes 4587544
  100.4 5.6 %experts.2 = (bf16[32,9,8,128]{3,2,1,0:T(8,128)(2,1)S(1)}, bf16[32,9,8,128]{3,2,1,0:T(8,128)(2,1)S(1)}, bf16[32,9,8,128]{3,2,1,0:T(8,128)(2,1)S(1)}, bf16[32,9,8,128]{3,2,1,0:T(8,128)(2,1)S(1)}) custom-call(s32[1]{0:T(128)} %bitcast.place_ref, bf16[32,9,8,128]{3,2,1,0:T(8,128)(2,1)S(1)} %get-tuple-element.63.x0, ...), custom_call_target="tpu_custom_call" | custom-call | flops 1 | bytes 1 | tf_op jit(solution)/shard_map/experts/pallas_call | solution.py:177
  106.6 2.3 %collective-permute-done.8.x1 = bf16[32,9,8,128]{3,2,1,0:T(8,128)(2,1)S(1)} collective-permute-done((bf16[32,9,8,128]{3,2,1,0:T(8,128)(2,1)S(1)}, bf16[32,9,8,128]{3,2,1,0:T(8,128)(2,1)S(1)}, u32[]{:S(2)}, u32[]{:S(2)}) %collective-permute-start.8) | collective-permute-done | bytes 589856 | tf_op jit(solution)/shard_map/ppermute | solution.py:365
  109.0 0.7 collective-permute-start.10
  109.8 0.5 collective-permute-start.13
  110.3 1.0 collective-permute-done.10.x3
  111.3 5.6 %experts.3 = (bf16[32,9,8,128]{3,2,1,0:T(8,128)(2,1)S(1)}, bf16[32,9,8,128]{3,2,1,0:T(8,128)(2,1)S(1)}, bf16[32,9,8,128]{3,2,1,0:T(8,128)(2,1)S(1)}, bf16[32,9,8,128]{3,2,1,0:T(8,128)(2,1)S(1)}) custom-call(s32[1]{0:T(128)} %bitcast.place_ref, bf16[32,9,8,128]{3,2,1,0:T(8,128)(2,1)S(1)} %get-tuple-element.42.x0, ...), custom_call_target="tpu_custom_call" | custom-call | flops 1 | bytes 1 | tf_op jit(solution)/shard_map/experts/pallas_call | solution.py:177
  117.9 7.1 %collective-permute-done.13 = bf16[32,9,8,128]{3,2,1,0:T(8,128)(2,1)S(1)} collective-permute-done((bf16[32,9,8,128]{3,2,1,0:T(8,128)(2,1)S(1)}, bf16[32,9,8,128]{3,2,1,0:T(8,128)(2,1)S(1)}, u32[]{:S(2)}, u32[]{:S(2)}) %collective-permute-start.13) | collective-permute-done | bytes 589856 | tf_op jit(solution)/shard_map/ppermute | solution.py:375
  125.1 0.5 collective-permute-start.15
  125.6 1.0 collective-permute-start.16
  126.8 12.7 %collective-permute-done.15 = bf16[32,9,8,128]{3,2,1,0:T(8,128)(2,1)S(1)} collective-permute-done((bf16[32,9,8,128]{3,2,1,0:T(8,128)(2,1)S(1)}, bf16[32,9,8,128]{3,2,1,0:T(8,128)(2,1)S(1)}, u32[]{:S(2)}, u32[]{:S(2)}) %collective-permute-start.15) | collective-permute-done | bytes 589856 | tf_op jit(solution)/shard_map/ppermute | solution.py:375
  139.7 1.1 pad_maximum_fusion
  140.9 8.8 %all-to-all-start.1 = ((bf16[64,9,8,128]{3,2,1,0:T(8,128)(2,1)}), bf16[64,9,8,128]{3,2,1,0:T(8,128)(2,1)S(1)}, u32[]{:S(2)}, u32[]{:S(2)}) async-start(bf16[64,9,8,128]{3,2,1,0:T(8,128)(2,1)} %pad_maximum_fusion), calls=%async_computation.1 | async-start | bytes 2359296 | tf_op jit(solution)/shard_map/all_to_all | solution.py:384
  149.8 0.8 copy-done.5
  150.5 3.6 %copy-done = bf16[7168,640]{1,0:T(8,128)(2,1)S(1)} copy-done((bf16[7168,640]{1,0:T(8,128)(2,1)S(1)}, bf16[7168,640]{1,0:T(8,128)(2,1)}, u32[]{:S(2)}) %copy-start) | copy-done | bytes 9175064
  154.1 1.0 copy-done.6
  155.1 5.9 %dense.1 = (bf16[2,64,3584]{2,1,0:T(8,128)(2,1)S(1)}, bf16[2,64,3584]{2,1,0:T(8,128)(2,1)S(1)}) custom-call(bf16[64,3584]{1,0:T(8,128)(2,1)S(1)} %copy-done.4, bf16[64,3584]{1,0:T(8,128)(2,1)S(1)} %collective-permute-done.3.x1, bf16[64,3584]{1,0:T(8,128)(2,1)S(1)} %collective-permute-done.16.x2, bf16[64,3584]{1,0:T(8,128)(2,1)S(1)} %copy-done.6, ...), custom_call_target="tpu_custom_call" | custom-call | flops 1 | bytes 1 | tf_op jit(solution)/shard_map/dense/pallas_call | solution.py:265
  161.0 1.9 collective-permute-start.19
  163.0 2.1 %collective-permute-done.19.got_ref = bf16[2,64,3584]{2,1,0:T(8,128)(2,1)S(1)} collective-permute-done((bf16[2,64,3584]{2,1,0:T(8,128)(2,1)S(1)}, bf16[2,64,3584]{2,1,0:T(8,128)(2,1)S(1)}, u32[]{:S(2)}, u32[]{:S(2)}) %collective-permute-start.19) | collective-permute-done | bytes 917536 | tf_op jit(solution)/shard_map/ppermute | solution.py:314
  165.1 0.9 fusion
  166.4 12.9 %all-to-all-done.1.x_ref = bf16[64,9,8,128]{3,2,1,0:T(8,128)(2,1)S(1)} async-done(((bf16[64,9,8,128]{3,2,1,0:T(8,128)(2,1)}), bf16[64,9,8,128]{3,2,1,0:T(8,128)(2,1)S(1)}, u32[]{:S(2)}, u32[]{:S(2)}) %all-to-all-start.1) | async-done | bytes 1179680 | tf_op jit(solution)/shard_map/all_to_all | solution.py:384
  179.2 1.1 combine.1
  180.4 0.5 collective-permute-start.21
  180.9 3.9 %collective-permute-start.22 = (bf16[64,896]{1,0:T(8,128)(2,1)S(1)}, bf16[64,896]{1,0:T(8,128)(2,1)S(1)}, u32[]{:S(2)}, u32[]{:S(2)}) collective-permute-start(bf16[64,896]{1,0:T(8,128)(2,1)S(1)} %get-tuple-element.61), channel_id=1, source_target_pairs={{0,1},{1,0},{2,3},{3,2},{4,5},{5,4},{6,7},{7,6},{8,9},{9,8},{10,11... | collective-permute-start | bytes 344072 | tf_op jit(solution)/shard_map/ppermute | solution.py:304
  184.8 0.9 collective-permute-start.23
  185.7 4.9 %collective-permute-done.23.r3 = bf16[64,896]{1,0:T(8,128)(2,1)S(1)} collective-permute-done((bf16[64,896]{1,0:T(8,128)(2,1)S(1)}, bf16[64,896]{1,0:T(8,128)(2,1)S(1)}, u32[]{:S(2)}, u32[]{:S(2)}) %collective-permute-start.23) | collective-permute-done | bytes 114720 | tf_op jit(solution)/shard_map/ppermute | solution.py:304
  190.6 2.1 %finish.1 = bf16[64,3584]{1,0:T(8,128)(2,1)} custom-call(s32[1]{0:T(128)} %bitcast.place_ref, bf16[64,3584]{1,0:T(8,128)(2,1)S(1)} %copy-done.4, bf16[2,64,3584]{2,1,0:T(8,128)(2,1)S(1)} %get-tuple-element.56.mine_ref, bf16[2,64,3584]{2,1,0:T(8,128)(2,1)S(1)} %collective-permute-done.19.got_ref, bf16[64,3584]{1,0:T(8,128)(2,1)} %collective-permute-done.20.last_ref, ...), custom_call_target="tpu_custom_call" | custom-call | flops 1 | bytes 1 | tf_op jit(solution)/shard_map/finish/pallas_call | solution.py:292
  (56 shorter events, 4.0 us)
Async XLA Ops:
  6.5 16.8 %copy-start.7 = (bf16[640,56]{0,1:T(8,128)(2,1)S(1)}, bf16[640,56]{0,1:T(8,128)(2,1)}, u32[]{:S(2)}) copy-start(bf16[640,56]{0,1:T(8,128)(2,1)} %param.11) | copy-start | bytes 215044
  6.5 16.8 %copy-start.8 = (bf16[56,640]{1,0:T(8,128)(2,1)S(1)}, bf16[56,640]{1,0:T(8,128)(2,1)}, u32[]{:S(2)}) copy-start(bf16[56,640]{1,0:T(8,128)(2,1)} %param.10) | copy-start | bytes 215044
  6.5 144.0 %all-gather.2.cloned.1.call-start = ((), (), s32[]{:S(2)}) async-start(), calls=%async_computation.2 | async-start | bytes 9461760 | tf_op jit(solution)/shard_map/all_gather | solution.py:332
  8.2 1.0 copy-start.3
  9.3 7.0 %collective-permute-start = (bf16[80,896]{1,0:T(8,128)(2,1)S(1)}, bf16[80,896]{1,0:T(8,128)(2,1)S(1)}, u32[]{:S(2)}, u32[]{:S(2)}) collective-permute-start(bf16[80,896]{1,0:T(8,128)(2,1)S(1)} %get-tuple-element.35), channel_id=1, source_target_pairs={{0,2},{2,0},{1,3},{3,1},{4,6},{6,4},{5,7},{7,5},{8,10},{10,8},{9,1... | collective-permute-start | bytes 430088 | tf_op jit(solution)/shard_map/ppermute | solution.py:304
  11.4 4.9 %collective-permute-start.1 = (bf16[80,896]{1,0:T(8,128)(2,1)S(1)}, bf16[80,896]{1,0:T(8,128)(2,1)S(1)}, u32[]{:S(2)}, u32[]{:S(2)}) collective-permute-start(bf16[80,896]{1,0:T(8,128)(2,1)S(1)} %get-tuple-element.36), channel_id=1, source_target_pairs={{0,1},{1,0},{2,3},{3,2},{4,5},{5,4},{6,7},{7,6},{8,9},{9,8},{10,11... | collective-permute-start | bytes 430088 | tf_op jit(solution)/shard_map/ppermute | solution.py:304
  12.7 8.7 %collective-permute-start.2 = (bf16[80,896]{1,0:T(8,128)(2,1)S(1)}, bf16[80,896]{1,0:T(8,128)(2,1)S(1)}, u32[]{:S(2)}, u32[]{:S(2)}) collective-permute-start(bf16[80,896]{1,0:T(8,128)(2,1)S(1)} %get-tuple-element.37), channel_id=1, source_target_pairs={{0,3},{3,0},{1,2},{2,1},{4,7},{7,4},{5,6},{6,5},{8,11},{11,8},{9,1... | collective-permute-start | bytes 430088 | tf_op jit(solution)/shard_map/ppermute | solution.py:304
  15.2 8.2 %collective-permute-start.18 = (bf16[112,640]{1,0:T(8,128)(2,1)S(1)}, bf16[112,640]{1,0:T(8,128)(2,1)S(1)}, u32[]{:S(2)}, u32[]{:S(2)}) collective-permute-start(bf16[112,640]{1,0:T(8,128)(2,1)S(1)} %pad_maximum_fusion.2), channel_id=1, source_target_pairs={{0,128},{4,132},{8,136},{12,140},{16,144},{20,148},{24,152},{28,15... | collective-permute-start | bytes 430088 | tf_op jit(solution)/shard_map/ppermute | solution.py:327
  24.2 13.4 %copy-start.4 = (bf16[64,3584]{1,0:T(8,128)(2,1)S(1)}, bf16[64,3584]{1,0:T(8,128)(2,1)}, u32[]{:S(2)}) copy-start(bf16[64,3584]{1,0:T(8,128)(2,1)} %tokens_ref.3) | copy-start | bytes 1376260
  24.2 87.1 %slice-start = ((s8[4587520]{0:T(1024)(128)(4,1)}), s8[393216]{0:T(1024)(128)(4,1)S(1)}, s32[]{:S(2)}) async-start(s8[4587520]{0:T(1024)(128)(4,1)} %bitcast.31), calls=%async_computation.3 | async-start | bytes 786432
  24.2 52.5 %all-to-all-start = ((bf16[64,9,8,128]{3,2,1,0:T(8,128)(2,1)}), bf16[64,9,8,128]{3,2,1,0:T(8,128)(2,1)}, u32[]{:S(2)}, u32[]{:S(2)}) async-start(bf16[64,9,8,128]{3,2,1,0:T(8,128)(2,1)} %get-tuple-element.38), calls=%async_computation | async-start | bytes 2359296 | tf_op jit(solution)/shard_map/all_to_all | solution.py:357
  37.6 16.3 %collective-permute-start.3 = (bf16[64,3584]{1,0:T(8,128)(2,1)S(1)}, bf16[64,3584]{1,0:T(8,128)(2,1)S(1)}, u32[]{:S(2)}, u32[]{:S(2)}) collective-permute-start(bf16[64,3584]{1,0:T(8,128)(2,1)S(1)} %copy-done.4), channel_id=1, source_target_pairs={{0,2},{2,0},{1,3},{3,1},{4,6},{6,4},{5,7},{7,5},{8,10},{10,8},{9,1... | collective-permute-start | bytes 1376264 | tf_op jit(solution)/shard_map/ppermute | solution.py:355
  78.1 11.1 %collective-permute-start.4 = (bf16[32,9,8,128]{3,2,1,0:T(8,128)(2,1)S(1)}, bf16[32,9,8,128]{3,2,1,0:T(8,128)(2,1)S(1)}, u32[]{:S(2)}, u32[]{:S(2)}) collective-permute-start(bf16[32,9,8,128]{3,2,1,0:T(8,128)(2,1)S(1)} %get-tuple-element.63.x0), channel_id=1, source_target_pairs={{0,2},{2,0},{1,3},{3,1},{4,6},{6,4},{5,7},{7,5},{8,10},{10,8},{9,1... | collective-permute-start | bytes 1769480 | tf_op jit(solution)/shard_map/ppermute | solution.py:365
  78.5 15.7 %collective-permute-start.5 = (bf16[32,9,8,128]{3,2,1,0:T(8,128)(2,1)S(1)}, bf16[32,9,8,128]{3,2,1,0:T(8,128)(2,1)S(1)}, u32[]{:S(2)}, u32[]{:S(2)}) collective-permute-start(bf16[32,9,8,128]{3,2,1,0:T(8,128)(2,1)S(1)} %get-tuple-element.63.x0), channel_id=1, source_target_pairs={{0,1},{1,0},{2,3},{3,2},{4,5},{5,4},{6,7},{7,6},{8,9},{9,8},{10,11... | collective-permute-start | bytes 1769480 | tf_op jit(solution)/shard_map/ppermute | solution.py:308
  89.2 6.3 %collective-permute-start.6 = (bf16[32,9,8,128]{3,2,1,0:T(8,128)(2,1)S(1)}, bf16[32,9,8,128]{3,2,1,0:T(8,128)(2,1)S(1)}, u32[]{:S(2)}, u32[]{:S(2)}) collective-permute-start(bf16[32,9,8,128]{3,2,1,0:T(8,128)(2,1)S(1)} %collective-permute-done.4.x1), channel_id=1, source_target_pairs={{0,1},{1,0},{2,3},{3,2},{4,5},{5,4},{6,7},{7,6},{8,9},{9,8},{10,11... | collective-permute-start | bytes 1769480 | tf_op jit(solution)/shard_map/ppermute | solution.py:309
  93.9 15.1 %collective-permute-start.8 = (bf16[32,9,8,128]{3,2,1,0:T(8,128)(2,1)S(1)}, bf16[32,9,8,128]{3,2,1,0:T(8,128)(2,1)S(1)}, u32[]{:S(2)}, u32[]{:S(2)}) collective-permute-start(bf16[32,9,8,128]{3,2,1,0:T(8,128)(2,1)S(1)} %get-tuple-element.42.x0), channel_id=1, source_target_pairs={{0,2},{2,0},{1,3},{3,1},{4,6},{6,4},{5,7},{7,5},{8,10},{10,8},{9,1... | collective-permute-start | bytes 1769480 | tf_op jit(solution)/shard_map/ppermute | solution.py:365
  95.5 2.4 %copy-start.1 = (bf16[1,3584,640]{2,1,0:T(8,128)(2,1)S(1)}, bf16[1,3584,640]{2,1,0:T(8,128)(2,1)}, u32[]{:S(2)}) copy-start(bf16[1,3584,640]{2,1,0:T(8,128)(2,1)} %param.12) | copy-start | bytes 13762564
  98.0 2.4 %copy-start.2 = (bf16[1,640,3584]{2,1,0:T(8,128)(2,1)S(1)}, bf16[1,640,3584]{2,1,0:T(8,128)(2,1)}, u32[]{:S(2)}) copy-start(bf16[1,640,3584]{2,1,0:T(8,128)(2,1)} %param.13) | copy-start | bytes 13762564
  100.4 10.9 %slice-start.1 = ((s8[4587520]{0:T(1024)(128)(4,1)}), s8[4194304]{0:T(1024)(128)(4,1)S(1)}, s32[]{:S(2)}) async-start(s8[4587520]{0:T(1024)(128)(4,1)} %bitcast.31), calls=%async_computation.4 | async-start | bytes 8388608
  106.0 3.6 %collective-permute-start.12 = (bf16[32,9,8,128]{3,2,1,0:T(8,128)(2,1)S(1)}, bf16[32,9,8,128]{3,2,1,0:T(8,128)(2,1)S(1)}, u32[]{:S(2)}, u32[]{:S(2)}) collective-permute-start(bf16[32,9,8,128]{3,2,1,0:T(8,128)(2,1)S(1)} %get-tuple-element.45), channel_id=1, source_target_pairs={{0,1},{1,0},{2,3},{3,2},{4,5},{5,4},{6,7},{7,6},{8,9},{9,8},{10,11... | collective-permute-start | bytes 1769480 | tf_op jit(solution)/shard_map/ppermute | solution.py:369
  106.4 3.9 %collective-permute-start.9 = (bf16[32,9,8,128]{3,2,1,0:T(8,128)(2,1)S(1)}, bf16[32,9,8,128]{3,2,1,0:T(8,128)(2,1)S(1)}, u32[]{:S(2)}, u32[]{:S(2)}) collective-permute-start(bf16[32,9,8,128]{3,2,1,0:T(8,128)(2,1)S(1)} %get-tuple-element.42.x0), channel_id=1, source_target_pairs={{0,1},{1,0},{2,3},{3,2},{4,5},{5,4},{6,7},{7,6},{8,9},{9,8},{10,11... | collective-permute-start | bytes 1769480 | tf_op jit(solution)/shard_map/ppermute | solution.py:308
  109.0 2.3 %collective-permute-start.10 = (bf16[32,9,8,128]{3,2,1,0:T(8,128)(2,1)S(1)}, bf16[32,9,8,128]{3,2,1,0:T(8,128)(2,1)S(1)}, u32[]{:S(2)}, u32[]{:S(2)}) collective-permute-start(bf16[32,9,8,128]{3,2,1,0:T(8,128)(2,1)S(1)} %collective-permute-done.8.x1), channel_id=1, source_target_pairs={{0,1},{1,0},{2,3},{3,2},{4,5},{5,4},{6,7},{7,6},{8,9},{9,8},{10,11... | collective-permute-start | bytes 1769480 | tf_op jit(solution)/shard_map/ppermute | solution.py:309
  109.8 15.2 %collective-permute-start.13 = (bf16[32,9,8,128]{3,2,1,0:T(8,128)(2,1)S(1)}, bf16[32,9,8,128]{3,2,1,0:T(8,128)(2,1)S(1)}, u32[]{:S(2)}, u32[]{:S(2)}) collective-permute-start(bf16[32,9,8,128]{3,2,1,0:T(8,128)(2,1)S(1)} %add_convert_fusion.3), channel_id=1, source_target_pairs={{0,2},{2,0},{1,3},{3,1},{4,6},{6,4},{5,7},{7,5},{8,10},{10,8},{9,1... | collective-permute-start | bytes 1769480 | tf_op jit(solution)/shard_map/ppermute | solution.py:375
  116.9 8.1 %collective-permute-start.11 = (bf16[32,9,8,128]{3,2,1,0:T(8,128)(2,1)S(1)}, bf16[32,9,8,128]{3,2,1,0:T(8,128)(2,1)S(1)}, u32[]{:S(2)}, u32[]{:S(2)}) collective-permute-start(bf16[32,9,8,128]{3,2,1,0:T(8,128)(2,1)S(1)} %get-tuple-element.43), channel_id=1, source_target_pairs={{0,1},{1,0},{2,3},{3,2},{4,5},{5,4},{6,7},{7,6},{8,9},{9,8},{10,11... | collective-permute-start | bytes 1769480 | tf_op jit(solution)/shard_map/ppermute | solution.py:369
  117.4 9.2 %collective-permute-start.7 = (bf16[32,9,8,128]{3,2,1,0:T(8,128)(2,1)S(1)}, bf16[32,9,8,128]{3,2,1,0:T(8,128)(2,1)S(1)}, u32[]{:S(2)}, u32[]{:S(2)}) collective-permute-start(bf16[32,9,8,128]{3,2,1,0:T(8,128)(2,1)S(1)} %get-tuple-element.41), channel_id=1, source_target_pairs={{0,1},{1,0},{2,3},{3,2},{4,5},{5,4},{6,7},{7,6},{8,9},{9,8},{10,11... | collective-permute-start | bytes 1769480 | tf_op jit(solution)/shard_map/ppermute | solution.py:370
  117.5 9.3 %collective-permute-start.14 = (bf16[32,9,8,128]{3,2,1,0:T(8,128)(2,1)S(1)}, bf16[32,9,8,128]{3,2,1,0:T(8,128)(2,1)S(1)}, u32[]{:S(2)}, u32[]{:S(2)}) collective-permute-start(bf16[32,9,8,128]{3,2,1,0:T(8,128)(2,1)S(1)} %get-tuple-element.49), channel_id=1, source_target_pairs={{0,1},{1,0},{2,3},{3,2},{4,5},{5,4},{6,7},{7,6},{8,9},{9,8},{10,11... | collective-permute-start | bytes 1769480 | tf_op jit(solution)/shard_map/ppermute | solution.py:370
  125.1 14.4 %collective-permute-start.15 = (bf16[32,9,8,128]{3,2,1,0:T(8,128)(2,1)S(1)}, bf16[32,9,8,128]{3,2,1,0:T(8,128)(2,1)S(1)}, u32[]{:S(2)}, u32[]{:S(2)}) collective-permute-start(bf16[32,9,8,128]{3,2,1,0:T(8,128)(2,1)S(1)} %add_convert_fusion.1), channel_id=1, source_target_pairs={{0,2},{2,0},{1,3},{3,1},{4,6},{6,4},{5,7},{7,5},{8,10},{10,8},{9,1... | collective-permute-start | bytes 1769480 | tf_op jit(solution)/shard_map/ppermute | solution.py:375
  125.6 24.1 %collective-permute-start.16 = (bf16[64,3584]{1,0:T(8,128)(2,1)S(1)}, bf16[64,3584]{1,0:T(8,128)(2,1)S(1)}, u32[]{:S(2)}, u32[]{:S(2)}) collective-permute-start(bf16[64,3584]{1,0:T(8,128)(2,1)S(1)} %copy-done.4), channel_id=1, source_target_pairs={{0,1},{1,0},{2,3},{3,2},{4,5},{5,4},{6,7},{7,6},{8,9},{9,8},{10,11... | collective-permute-start | bytes 1376264 | tf_op jit(solution)/shard_map/ppermute | solution.py:308
  126.6 23.2 %collective-permute-start.17 = (bf16[64,3584]{1,0:T(8,128)(2,1)S(1)}, bf16[64,3584]{1,0:T(8,128)(2,1)S(1)}, u32[]{:S(2)}, u32[]{:S(2)}) collective-permute-start(bf16[64,3584]{1,0:T(8,128)(2,1)S(1)} %collective-permute-done.3.x1), channel_id=1, source_target_pairs={{0,1},{1,0},{2,3},{3,2},{4,5},{5,4},{6,7},{7,6},{8,9},{9,8},{10,11... | collective-permute-start | bytes 1376264 | tf_op jit(solution)/shard_map/ppermute | solution.py:309
  140.9 38.4 %all-to-all-start.1 = ((bf16[64,9,8,128]{3,2,1,0:T(8,128)(2,1)}), bf16[64,9,8,128]{3,2,1,0:T(8,128)(2,1)S(1)}, u32[]{:S(2)}, u32[]{:S(2)}) async-start(bf16[64,9,8,128]{3,2,1,0:T(8,128)(2,1)} %pad_maximum_fusion), calls=%async_computation.1 | async-start | bytes 2359296 | tf_op jit(solution)/shard_map/all_to_all | solution.py:384
  149.7 0.8 copy-start.5
  150.5 3.6 %copy-start = (bf16[7168,640]{1,0:T(8,128)(2,1)S(1)}, bf16[7168,640]{1,0:T(8,128)(2,1)}, u32[]{:S(2)}) copy-start(bf16[7168,640]{1,0:T(8,128)(2,1)} %all-gather.2.cloned.1.call-done) | copy-start | bytes 27525124
  154.1 1.0 copy-start.6
  161.0 4.0 %collective-permute-start.19 = (bf16[2,64,3584]{2,1,0:T(8,128)(2,1)S(1)}, bf16[2,64,3584]{2,1,0:T(8,128)(2,1)S(1)}, u32[]{:S(2)}, u32[]{:S(2)}) collective-permute-start(bf16[2,64,3584]{2,1,0:T(8,128)(2,1)S(1)} %get-tuple-element.57), channel_id=1, source_target_pairs={{0,1},{1,0},{2,3},{3,2},{4,5},{5,4},{6,7},{7,6},{8,9},{9,8},{10,11... | collective-permute-start | bytes 2752520 | tf_op jit(solution)/shard_map/ppermute | solution.py:314
  165.9 24.7 %collective-permute-start.20 = (bf16[64,3584]{1,0:T(8,128)(2,1)}, bf16[64,3584]{1,0:T(8,128)(2,1)}, u32[]{:S(2)}, u32[]{:S(2)}) collective-permute-start(bf16[64,3584]{1,0:T(8,128)(2,1)} %fusion), channel_id=1, source_target_pairs={{0,2},{2,0},{1,3},{3,1},{4,6},{6,4},{5,7},{7,5},{8,10},{10,8},{9,1... | collective-permute-start | bytes 1376264 | tf_op jit(solution)/shard_map/ppermute | solution.py:316
  180.4 5.3 %collective-permute-start.21 = (bf16[64,896]{1,0:T(8,128)(2,1)S(1)}, bf16[64,896]{1,0:T(8,128)(2,1)S(1)}, u32[]{:S(2)}, u32[]{:S(2)}) collective-permute-start(bf16[64,896]{1,0:T(8,128)(2,1)S(1)} %get-tuple-element.60), channel_id=1, source_target_pairs={{0,2},{2,0},{1,3},{3,1},{4,6},{6,4},{5,7},{7,5},{8,10},{10,8},{9,1... | collective-permute-start | bytes 344072 | tf_op jit(solution)/shard_map/ppermute | solution.py:304
  180.9 4.9 %collective-permute-start.22 = (bf16[64,896]{1,0:T(8,128)(2,1)S(1)}, bf16[64,896]{1,0:T(8,128)(2,1)S(1)}, u32[]{:S(2)}, u32[]{:S(2)}) collective-permute-start(bf16[64,896]{1,0:T(8,128)(2,1)S(1)} %get-tuple-element.61), channel_id=1, source_target_pairs={{0,1},{1,0},{2,3},{3,2},{4,5},{5,4},{6,7},{7,6},{8,9},{9,8},{10,11... | collective-permute-start | bytes 344072 | tf_op jit(solution)/shard_map/ppermute | solution.py:304
  184.8 5.8 %collective-permute-start.23 = (bf16[64,896]{1,0:T(8,128)(2,1)S(1)}, bf16[64,896]{1,0:T(8,128)(2,1)S(1)}, u32[]{:S(2)}, u32[]{:S(2)}) collective-permute-start(bf16[64,896]{1,0:T(8,128)(2,1)S(1)} %get-tuple-element.62), channel_id=1, source_target_pairs={{0,3},{3,0},{1,2},{2,1},{4,7},{7,4},{5,6},{6,5},{8,11},{11,8},{9,1... | collective-permute-start | bytes 344072 | tf_op jit(solution)/shard_map/ppermute | solution.py:304
Sparse Core Ops, SparseCore 0:
  24.3 115.4 all-gather.1

commit v4 on v3

--- a/solution.py
+++ b/solution.py
@@ -17,7 +17,7 @@
 MAIN = 8
 LANES = 128
 SIZES = (32, 32)
-VMEM = 24 * 1024 * 1024
+VMEM = 32 * 1024 * 1024
 
 
 def dot(a, b, dims=((1,), (0,))):
@@ -73,28 +73,55 @@
 SMEM = pl.BlockSpec(memory_space=pltpu.SMEM)
 WHOLE = pl.BlockSpec(memory_space=pltpu.VMEM)
 COST = pl.CostEstimate(flops=1, bytes_accessed=1, transcendentals=0)
+LONG = pl.CostEstimate(flops=10_000_000_000_000, bytes_accessed=1, transcendentals=0)
 PARAMS = pltpu.CompilerParams(vmem_limit_bytes=VMEM)
 
 
-def pack_kernel(place_ref, tokens_ref, meta_ref, *out_refs):
+def pack_kernel(place_ref, tokens_ref, ids_ref, codes_ref, *out_refs):
     rows, part = tokens_ref.shape[0], out_refs[0].shape[1]
+    group = len(out_refs) * rows
+    codes = codes_ref[...]
+    fields = [ids_ref[...], codes >> 5, codes & 31, jnp.zeros((META - 6, rows), jnp.int32)]
+    fields = jnp.concatenate(fields, axis=0).astype(F32)
+    lane = lax.broadcasted_iota(jnp.int32, (META, group), 1)
+    own = (lane >= place_ref[0] * rows) & (lane < (place_ref[0] + 1) * rows)
+    meta = jnp.where(own, jnp.concatenate([fields] * len(out_refs), axis=1), 0.0)
+    meta = jnp.concatenate([meta, jnp.zeros((META, part - group), F32)], axis=1).astype(BF16)
     for step, out_ref in enumerate(out_refs):
         out_ref[:rows, :] = tokens_ref[:, pl.ds(at(place_ref[0], step, part), part)]
-        out_ref[rows:, :] = meta_ref[...]
-
-
-def pack(place, tokens, meta):
+        out_ref[rows:, :] = meta
+
+
+def pack(place, tokens, ids, codes):
     rows, width = tokens.shape
     block = jax.ShapeDtypeStruct((rows + META, width // 4), BF16)
     return pl.pallas_call(
         pack_kernel,
-        in_specs=[SMEM, WHOLE, WHOLE],
+        in_specs=[SMEM] + [WHOLE] * 3,
         out_specs=[WHOLE] * 4,
         out_shape=[block] * 4,
         compiler_params=PARAMS,
         cost_estimate=COST,
         name="pack",
-    )(place, tokens, meta)
+    )(place, tokens, ids, codes)
+
+
+def pair_kernel(a_ref, b_ref, out_ref):
+    rows = a_ref.shape[0]
+    out_ref[:rows, :] = a_ref[...]
+    out_ref[rows:, :] = b_ref[...]
+
+
+def pair_up(a, b):
+    return pl.pallas_call(
+        pair_kernel,
+        in_specs=[WHOLE] * 2,
+        out_specs=WHOLE,
+        out_shape=jax.ShapeDtypeStruct((2 * a.shape[0], a.shape[1]), a.dtype),
+        compiler_params=PARAMS,
+        cost_estimate=LONG,
+        name="pair_up",
+    )(a, b)
 
 
 def dispatch_kernel(n_experts, capacity, place_ref, x0, x1, x2, x3, out_ref, plan_ref, tokens, scratch):
@@ -224,59 +251,52 @@
     )(place, x, plan)
 
 
-def dense_kernel(x0, x1, x2, x3, up_ref, down_ref, mine_ref, others_ref, pre, hidden):
-    step = pl.program_id(0)
-
-    @pl.when(step < N_X)
-    def _():
-        x = jnp.concatenate([x0[...], x1[...], x2[...], x3[...]], axis=0)
-        up = up_ref[...].astype(F32).reshape(x.shape[1], up_ref.shape[-1]).astype(BF16)
-        part = dot(x, up)
-
-        @pl.when(step == 0)
-        def _():
-            pre[...] = part
-
-        @pl.when(step > 0)
-        def _():
-            hidden[...] = silu(pre[...] + part).astype(BF16)
-
-    @pl.when(step >= N_X)
-    def _():
-        down = down_ref[...].astype(F32)
-        down = down.reshape(-1, down.shape[-1]).astype(BF16)
-        out = dot(hidden[...], down, ((1,), (1,))).astype(BF16).reshape((4,) + mine_ref.shape[1:])
-        mine_ref[...] = out[:2]
-        others_ref[...] = out[2:]
+def dense_kernel(x_mine, x_others, weights, mine_ref, others_ref, up_ref, down_ref, sems):
+    z, half = weights.shape[0], weights.shape[0] // 2
+    width = x_mine.shape[1]
+    copies = [pltpu.make_async_copy(weights.at[:, :, i, 0], up_ref.at[i], sems.at[i]) for i in range(N_X)]
+    for n in range(4):
+        rows = pl.ds(n % 2 * half, half)
+        copies.append(pltpu.make_async_copy(weights.at[rows, :, n // 2, 1], down_ref.at[n], sems.at[N_X + n]))
+    for copy in copies:
+        copy.start()
+
+    def rows_of(block):
+        return block.astype(F32).reshape(-1, block.shape[-1]).astype(BF16)
+
+    pre = None
+    for i in range(N_X):
+        cut = slice(i * width // N_X, (i + 1) * width // N_X)
+        x = jnp.concatenate([x_mine[:, cut], x_others[:, cut]], axis=0)
+        copies[i].wait()
+        part = dot(x, rows_of(up_ref[i]))
+        pre = part if pre is None else pre + part
+    hidden = silu(pre).astype(BF16)
+    for n in range(4):
+        cut = slice(n * width // 4, (n + 1) * width // 4)
+        copies[N_X + n].wait()
+        out = dot(hidden, rows_of(down_ref[n]), ((1,), (1,))).astype(BF16)
+        out = out.reshape((4,) + mine_ref.shape[1:2] + (width // 4,))
+        mine_ref[:, :, cut] = out[:2]
+        others_ref[:, :, cut] = out[2:]
 
 
 def dense(xs, weights):
-    rows, width = xs[0].shape
-    units = weights.shape[-1]
-    z, y, _, _, inner, _ = weights.shape
-    tile = width // 4
-    x_spec = pl.BlockSpec((rows, width // N_X), lambda i: (0, jnp.minimum(i, N_X - 1)))
-    out_spec = pl.BlockSpec((2, rows, tile), lambda i: (0, 0, jnp.maximum(i - N_X, 0)))
-
-    def down_at(i):
-        n = jnp.maximum(i - N_X, 0)
-        return n % 2, 0, n // 2, 1, 0, 0
-
+    z, y, _, _, inner, units = weights.shape
     return pl.pallas_call(
         dense_kernel,
-        grid=(N_X + 4,),
-        in_specs=[x_spec] * 4
-        + [
-            pl.BlockSpec((z, y, None, None, inner, units), lambda i: (0, 0, jnp.minimum(i, N_X - 1), 0, 0, 0)),
-            pl.BlockSpec((z // 2, y, None, None, inner, units), down_at),
+        in_specs=[WHOLE] * 2 + [pl.BlockSpec(memory_space=pltpu.HBM)],
+        out_specs=[WHOLE] * 2,
+        out_shape=[jax.ShapeDtypeStruct((2, xs[0].shape[0] // 2, xs[0].shape[1]), BF16)] * 2,
+        scratch_shapes=[
+            pltpu.VMEM((N_X, z, y, inner, units), BF16),
+            pltpu.VMEM((4, z // 2, y, inner, units), BF16),
+            pltpu.SemaphoreType.DMA((N_X + 4,)),
         ],
-        out_specs=[out_spec] * 2,
-        out_shape=[jax.ShapeDtypeStruct((2, rows, width), BF16)] * 2,
-        scratch_shapes=[pltpu.VMEM((4 * rows, units), F32), pltpu.VMEM((4 * rows, units), BF16)],
         compiler_params=PARAMS,
         cost_estimate=COST,
         name="dense",
-    )(*xs, weights, weights)
+    )(*xs, weights)
 
 
 def finish_kernel(place_ref, tokens_ref, mine_ref, got_ref, last_ref, r0, r1, r2, r3, out_ref):
@@ -343,19 +363,15 @@
     capacity = 5 * group // (2 * n_experts)
     part = width // n_tensor
 
-    ids, codes = expert_ids.astype(jnp.int32).T, gate_codes.astype(jnp.int32).T
-    meta = jnp.concatenate([ids, codes // 32, codes % 32, jnp.zeros((META - 6, rows_own), jnp.int32)])
-    owner = jnp.arange(group, dtype=jnp.int32)[None, :] // rows_own
-    meta = jnp.where(owner == place, jnp.tile(meta, (1, n_tensor)), 0).astype(BF16)
-    meta = jnp.pad(meta, ((0, 0), (0, part - group)))
-    grouped = swap(pack(spot, tokens, meta))
+    grouped = swap(pack(spot, tokens, expert_ids.T, gate_codes.T))
     routed, plan = dispatch(spot, grouped, n_experts, capacity)
     weights = gather_dense(dense_up, dense_down, plan)
 
-    tokens_near = lax.ppermute(tokens, "tensor", NEXT)
+    tokens_pair = pair_up(tokens, lax.ppermute(tokens, "tensor", NEXT))
 
     routed = lax.all_to_all(routed, "expert", split_axis=0, concat_axis=0, tiled=True)
-    routed, tokens_near = lax.optimization_barrier((routed, tokens_near))
+    tokens_by = tokens_pair, lax.ppermute(tokens_pair, "tensor", CORE)
+    routed, tokens_by = lax.optimization_barrier((routed, tokens_by))
     start, terms, near, last = 0, [], None, None
     for size in SIZES:
         x = routed[start : start + size]
@@ -376,9 +392,8 @@
         terms.append([own, other, last])
     result = jnp.concatenate([(a.astype(F32) + b.astype(F32) + c.astype(F32)).astype(BF16) for a, b, c in terms])
 
-    dense_own, result = lax.optimization_barrier((tokens, result))
-    blocks = spread(tokens, tokens_near)
-    mine, others = dense((dense_own,) + blocks[1:], weights)
+    tokens_by, result = lax.optimization_barrier((tokens_by, result))
+    mine, others = dense(tokens_by, weights)
     got, last = fold(mine, others)
 
     returned = lax.all_to_all(result, "expert", split_axis=0, concat_axis=0, tiled=True)

time: 200 us -> 193 us (0.965)
  starting transfers between devices: 50.6 us -> 38.1 us
  waiting for transfers between devices: 94.3 us -> 99.3 us
    ppermute x1 -> x2, waiting for transfers between devices: 15.9 us -> 2.46 us  [the longest x1 2.46 us: local(): tokens_by = (tokens_pair, lax.ppermute(tokens_pair, 'tensor', CORE))]
    ppermute x2, waiting for transfers between devices: 8.47 us -> 17.1 us  [local(): near = lax.ppermute(x, 'tensor', NEXT)]
    all_to_all x1, waiting for transfers between devices: 22.8 us -> 30.4 us  [local(): lax.all_to_all(routed, 'expert', split_axis=0, concat_axis=0, tiled=True)]
    ppermute x3 -> x2, starting transfers between devices: 5.75 us -> 0.48 us  [spread(): other = lax.ppermute(x, 'tensor', CORE)]
    ppermute x3 -> x2, starting transfers between devices: 5.4 us -> 1.21 us  [spread(): far = lax.ppermute(near, 'tensor', CORE)]
    all_gather x1, waiting for transfers between devices: 0.01 us -> 2.73 us  [gather_dense(): lax.all_gather(pair, 'expert', axis=0, tiled=True, axis_index_groups=planes)]
    all_to_all x1, starting transfers between devices: 8.85 us -> 6.39 us  [local(): lax.all_to_all(result, 'expert', split_axis=0, concat_axis=0, tiled=True)]
    all_to_all x1, waiting for transfers between devices: 12.9 us -> 10.6 us  [local(): lax.all_to_all(result, 'expert', split_axis=0, concat_axis=0, tiled=True)]
  transfers between devices with their start and end apart: 27 -> 26, of which waited for: 12 -> 13; matrix products, arithmetic and copies ran while one was open for 3% -> 3% of each run, Pallas kernels for 10% -> 11%
where the time goes in v4:
time: 193 us
  waiting for transfers between devices  99.3 us (51%)
  starting transfers between devices  38.1 us (20%)
  Pallas kernels  23.5 us (12%)
  between operations  13.6 us (7%)
  local copies, waits for them, and re-layouts  13.5 us (7%)
  other arithmetic  4.52 us (2%)
    all_to_all x1, waiting for transfers between devices, local(): lax.all_to_all(routed, 'expert', split_axis=0, concat_axis=0, tiled=True)  30.4 us
    ppermute x2, waiting for transfers between devices, local(): last = lax.ppermute(rest, 'tensor', NEXT)  21.1 us
    ppermute x2, waiting for transfers between devices, local(): near = lax.ppermute(x, 'tensor', NEXT)  17.1 us
    all_to_all x1, starting transfers between devices, local(): lax.all_to_all(routed, 'expert', split_axis=0, concat_axis=0, tiled=True)  13.2 us
    unnamed x20, local copies, waits for them, and re-layouts  12.2 us
    pallas_call x2, Pallas kernels, experts(): pl.pallas_call(functools.partial(experts_kernel, capacity), in_specs=[SME...  11.2 us
    all_to_all x1, waiting for transfers between devices, local(): lax.all_to_all(result, 'expert', split_axis=0, concat_axis=0, tiled=True)  10.6 us
    ppermute x6, starting transfers between devices, swap(): lax.ppermute(x, 'tensor', perm)  10.3 us
  transfers between devices with their start and end apart: 26, of which 13 were waited for; matrix products, arithmetic and copies ran while one was open for 3% of the time, Pallas kernels for 11%

profile of v4, /device:TPU:1, one launch (start us, length us, event | category | flops | bytes accessed | tf_op | source)
XLA Modules:
  0.0 192.5 jit_solution(14983333439424064276)
XLA Ops:
  6.5 0.7 copy-done.6
  7.2 0.7 copy-done.7
  7.9 1.1 pack.1
  9.0 2.1 %collective-permute-start = (bf16[80,896]{1,0:T(8,128)(2,1)S(1)}, bf16[80,896]{1,0:T(8,128)(2,1)S(1)}, u32[]{:S(2)}, u32[]{:S(2)}) collective-permute-start(bf16[80,896]{1,0:T(8,128)(2,1)S(1)} %get-tuple-element.37), channel_id=1, source_target_pairs={{0,2},{2,0},{1,3},{3,1},{4,6},{6,4},{5,7},{7,5},{8,10},{10,8},{9,1... | collective-permute-start | bytes 430088 | tf_op jit(solution)/shard_map/ppermute | solution.py:324
  11.1 1.3 collective-permute-start.1
  12.4 1.5 collective-permute-start.2
  13.9 0.9 pad_maximum_fusion.2
  14.9 1.1 collective-permute-start.17
  16.3 5.0 %collective-permute-done.2.x3 = bf16[80,896]{1,0:T(8,128)(2,1)S(1)} collective-permute-done((bf16[80,896]{1,0:T(8,128)(2,1)S(1)}, bf16[80,896]{1,0:T(8,128)(2,1)S(1)}, u32[]{:S(2)}, u32[]{:S(2)}) %collective-permute-start.2) | collective-permute-done | bytes 143392 | tf_op jit(solution)/shard_map/ppermute | solution.py:324
  21.3 1.9 dispatch.1
  23.2 13.2 %all-to-all-start = ((bf16[64,9,8,128]{3,2,1,0:T(8,128)(2,1)}), bf16[64,9,8,128]{3,2,1,0:T(8,128)(2,1)}, u32[]{:S(2)}, u32[]{:S(2)}) async-start(bf16[64,9,8,128]{3,2,1,0:T(8,128)(2,1)} %get-tuple-element.40), calls=%async_computation | async-start | bytes 2359296 | tf_op jit(solution)/shard_map/all_to_all | solution.py:372
  36.6 0.7 pad_maximum_fusion.1
  37.3 1.1 pair_up.1.x_mine
  38.5 2.5 %collective-permute-done.4.x_others = bf16[128,3584]{1,0:T(8,128)(2,1)S(1)} collective-permute-done((bf16[128,3584]{1,0:T(8,128)(2,1)S(1)}, bf16[128,3584]{1,0:T(8,128)(2,1)S(1)}, u32[]{:S(2)}, u32[]{:S(2)}) %collective-permute-start.4) | collective-permute-done | bytes 917536 | tf_op jit(solution)/shard_map/ppermute | solution.py:373
  41.0 1.0 copy-done.4
  42.0 30.4 %all-to-all-done = bf16[64,9,8,128]{3,2,1,0:T(8,128)(2,1)} async-done(((bf16[64,9,8,128]{3,2,1,0:T(8,128)(2,1)}), bf16[64,9,8,128]{3,2,1,0:T(8,128)(2,1)}, u32[]{:S(2)}, u32[]{:S(2)}) %all-to-all-start) | async-done | bytes 1179680 | tf_op jit(solution)/shard_map/all_to_all | solution.py:372
  72.3 1.3 fusion.1
  73.9 15.1 %collective-permute-done.5.x1 = bf16[32,9,8,128]{3,2,1,0:T(8,128)(2,1)S(1)} collective-permute-done((bf16[32,9,8,128]{3,2,1,0:T(8,128)(2,1)S(1)}, bf16[32,9,8,128]{3,2,1,0:T(8,128)(2,1)S(1)}, u32[]{:S(2)}, u32[]{:S(2)}) %collective-permute-start.5) | collective-permute-done | bytes 589856 | tf_op jit(solution)/shard_map/ppermute | solution.py:381
  89.0 0.5 collective-permute-start.7
  89.5 1.6 collective-permute-done.7.x3
  91.1 2.3 %copy-done = bf16[1,3584,640]{2,1,0:T(8,128)(2,1)S(1)} copy-done((bf16[1,3584,640]{2,1,0:T(8,128)(2,1)S(1)}, bf16[1,3584,640]{2,1,0:T(8,128)(2,1)}, u32[]{:S(2)}) %copy-start) | copy-done | bytes 4587544
  93.4 2.8 %copy-done.2 = bf16[1,640,3584]{2,1,0:T(8,128)(2,1)S(1)} copy-done((bf16[1,640,3584]{2,1,0:T(8,128)(2,1)S(1)}, bf16[1,640,3584]{2,1,0:T(8,128)(2,1)}, u32[]{:S(2)}) %copy-start.2) | copy-done | bytes 4587544
  96.2 5.6 %experts.2 = (bf16[32,9,8,128]{3,2,1,0:T(8,128)(2,1)S(1)}, bf16[32,9,8,128]{3,2,1,0:T(8,128)(2,1)S(1)}, bf16[32,9,8,128]{3,2,1,0:T(8,128)(2,1)S(1)}, bf16[32,9,8,128]{3,2,1,0:T(8,128)(2,1)S(1)}) custom-call(s32[1]{0:T(128)} %bitcast.place_ref, bf16[32,9,8,128]{3,2,1,0:T(8,128)(2,1)S(1)} %get-tuple-element.67.x0, ...), custom_call_target="tpu_custom_call" | custom-call | flops 1 | bytes 1 | tf_op jit(solution)/shard_map/experts/pallas_call | solution.py:204
  101.8 0.4 collective-permute-start.13
  102.2 0.4 collective-permute-start.10
  102.6 2.0 %collective-permute-done.9.x1 = bf16[32,9,8,128]{3,2,1,0:T(8,128)(2,1)S(1)} collective-permute-done((bf16[32,9,8,128]{3,2,1,0:T(8,128)(2,1)S(1)}, bf16[32,9,8,128]{3,2,1,0:T(8,128)(2,1)S(1)}, u32[]{:S(2)}, u32[]{:S(2)}) %collective-permute-start.9) | collective-permute-done | bytes 589856 | tf_op jit(solution)/shard_map/ppermute | solution.py:381
  104.6 0.7 collective-permute-start.11
  105.5 1.4 collective-permute-done.11.x3
  106.9 5.6 %experts.3 = (bf16[32,9,8,128]{3,2,1,0:T(8,128)(2,1)S(1)}, bf16[32,9,8,128]{3,2,1,0:T(8,128)(2,1)S(1)}, bf16[32,9,8,128]{3,2,1,0:T(8,128)(2,1)S(1)}, bf16[32,9,8,128]{3,2,1,0:T(8,128)(2,1)S(1)}) custom-call(s32[1]{0:T(128)} %bitcast.place_ref, bf16[32,9,8,128]{3,2,1,0:T(8,128)(2,1)S(1)} %get-tuple-element.46.x0, ...), custom_call_target="tpu_custom_call" | custom-call | flops 1 | bytes 1 | tf_op jit(solution)/shard_map/experts/pallas_call | solution.py:204
  112.5 0.5 collective-permute-start.12
  113.4 7.1 %collective-permute-done.14 = bf16[32,9,8,128]{3,2,1,0:T(8,128)(2,1)S(1)} collective-permute-done((bf16[32,9,8,128]{3,2,1,0:T(8,128)(2,1)S(1)}, bf16[32,9,8,128]{3,2,1,0:T(8,128)(2,1)S(1)}, u32[]{:S(2)}, u32[]{:S(2)}) %collective-permute-start.14) | collective-permute-done | bytes 589856 | tf_op jit(solution)/shard_map/ppermute | solution.py:391
  121.1 14.0 %collective-permute-done.16 = bf16[32,9,8,128]{3,2,1,0:T(8,128)(2,1)S(1)} collective-permute-done((bf16[32,9,8,128]{3,2,1,0:T(8,128)(2,1)S(1)}, bf16[32,9,8,128]{3,2,1,0:T(8,128)(2,1)S(1)}, u32[]{:S(2)}, u32[]{:S(2)}) %collective-permute-start.16) | collective-permute-done | bytes 589856 | tf_op jit(solution)/shard_map/ppermute | solution.py:391
  135.3 1.1 pad_maximum_fusion
  136.5 6.4 %all-to-all-start.1 = ((bf16[64,9,8,128]{3,2,1,0:T(8,128)(2,1)}), bf16[64,9,8,128]{3,2,1,0:T(8,128)(2,1)S(1)}, u32[]{:S(2)}, u32[]{:S(2)}) async-start(bf16[64,9,8,128]{3,2,1,0:T(8,128)(2,1)} %pad_maximum_fusion), calls=%async_computation.1 | async-start | bytes 2359296 | tf_op jit(solution)/shard_map/all_to_all | solution.py:399
  142.9 2.7 %all-gather.2.cloned.1.call-done = bf16[7168,640]{1,0:T(8,128)(2,1)} async-done(((bf16[224,640]{1,0:T(8,128)(2,1)}), bf16[7168,640]{1,0:T(8,128)(2,1)}) %all-gather.2.cloned.1.call-update) | async-done | bytes 9175056 | tf_op jit(solution)/shard_map/all_gather | solution.py:352
  145.6 3.6 %copy-done.3 = bf16[7168,640]{1,0:T(8,128)(2,1)S(1)} copy-done((bf16[7168,640]{1,0:T(8,128)(2,1)S(1)}, bf16[7168,640]{1,0:T(8,128)(2,1)}, u32[]{:S(2)}) %copy-start.3) | copy-done | bytes 9175064
  149.2 1.2 copy-done.5
  150.4 5.0 %dense.1 = (bf16[2,64,3584]{2,1,0:T(8,128)(2,1)S(1)}, bf16[2,64,3584]{2,1,0:T(8,128)(2,1)S(1)}) custom-call(bf16[128,3584]{1,0:T(8,128)(2,1)S(1)} %pair_up.1.x_mine, bf16[128,3584]{1,0:T(8,128)(2,1)S(1)} %copy-done.5, bf16[8,4,2,2,56,640]{5,4,3,2,1,0:T(8,128)(2,1)S(1)} %bitcast.13), custom_call_target="tpu_custom_call" | custom-call | flops 1 | bytes 1 | tf_op jit(solution)/shard_map/dense/pallas_call | solution.py:286
  155.4 1.2 collective-permute-start.18
  156.6 2.1 %collective-permute-done.18.got_ref = bf16[2,64,3584]{2,1,0:T(8,128)(2,1)S(1)} collective-permute-done((bf16[2,64,3584]{2,1,0:T(8,128)(2,1)S(1)}, bf16[2,64,3584]{2,1,0:T(8,128)(2,1)S(1)}, u32[]{:S(2)}, u32[]{:S(2)}) %collective-permute-start.18) | collective-permute-done | bytes 917536 | tf_op jit(solution)/shard_map/ppermute | solution.py:334
  158.7 0.9 fusion
  159.6 2.1 %collective-permute-start.19 = (bf16[64,3584]{1,0:T(8,128)(2,1)}, bf16[64,3584]{1,0:T(8,128)(2,1)S(1)}, u32[]{:S(2)}, u32[]{:S(2)}) collective-permute-start(bf16[64,3584]{1,0:T(8,128)(2,1)} %fusion), channel_id=1, source_target_pairs={{0,2},{2,0},{1,3},{3,1},{4,6},{6,4},{5,7},{7,5},{8,10},{10,8},{9,1... | collective-permute-start | bytes 1376264 | tf_op jit(solution)/shard_map/ppermute | solution.py:336
  161.7 10.6 %all-to-all-done.1.x_ref = bf16[64,9,8,128]{3,2,1,0:T(8,128)(2,1)S(1)} async-done(((bf16[64,9,8,128]{3,2,1,0:T(8,128)(2,1)}), bf16[64,9,8,128]{3,2,1,0:T(8,128)(2,1)S(1)}, u32[]{:S(2)}, u32[]{:S(2)}) %all-to-all-start.1) | async-done | bytes 1179680 | tf_op jit(solution)/shard_map/all_to_all | solution.py:399
  172.3 1.1 combine.1
  173.5 3.8 %collective-permute-start.21 = (bf16[64,896]{1,0:T(8,128)(2,1)S(1)}, bf16[64,896]{1,0:T(8,128)(2,1)S(1)}, u32[]{:S(2)}, u32[]{:S(2)}) collective-permute-start(bf16[64,896]{1,0:T(8,128)(2,1)S(1)} %get-tuple-element.65), channel_id=1, source_target_pairs={{0,1},{1,0},{2,3},{3,2},{4,5},{5,4},{6,7},{7,6},{8,9},{9,8},{10,11... | collective-permute-start | bytes 344072 | tf_op jit(solution)/shard_map/ppermute | solution.py:324
  177.4 1.5 collective-permute-start.22
  178.9 4.7 %collective-permute-done.22.r3 = bf16[64,896]{1,0:T(8,128)(2,1)S(1)} collective-permute-done((bf16[64,896]{1,0:T(8,128)(2,1)S(1)}, bf16[64,896]{1,0:T(8,128)(2,1)S(1)}, u32[]{:S(2)}, u32[]{:S(2)}) %collective-permute-start.22) | collective-permute-done | bytes 114720 | tf_op jit(solution)/shard_map/ppermute | solution.py:324
  183.6 2.1 %finish.1 = bf16[64,3584]{1,0:T(8,128)(2,1)} custom-call(s32[1]{0:T(128)} %bitcast.place_ref, bf16[64,3584]{1,0:T(8,128)(2,1)} %tokens_ref.3, bf16[2,64,3584]{2,1,0:T(8,128)(2,1)S(1)} %get-tuple-element.60.mine_ref, bf16[2,64,3584]{2,1,0:T(8,128)(2,1)S(1)} %collective-permute-done.18.got_ref, bf16[64,3584]{1,0:T(8,128)(2,1)S(1)} %collective-permute-done.19.last_ref, ...), custom_call_target="tpu_custom_call" | custom-call | flops 1 | bytes 1 | tf_op jit(solution)/shard_map/finish/pallas_call | solution.py:312
  (43 shorter events, 2.3 us)
Async XLA Ops:
  6.5 0.7 copy-start.6
  7.2 0.7 copy-start.7
  9.0 7.3 %collective-permute-start = (bf16[80,896]{1,0:T(8,128)(2,1)S(1)}, bf16[80,896]{1,0:T(8,128)(2,1)S(1)}, u32[]{:S(2)}, u32[]{:S(2)}) collective-permute-start(bf16[80,896]{1,0:T(8,128)(2,1)S(1)} %get-tuple-element.37), channel_id=1, source_target_pairs={{0,2},{2,0},{1,3},{3,1},{4,6},{6,4},{5,7},{7,5},{8,10},{10,8},{9,1... | collective-permute-start | bytes 430088 | tf_op jit(solution)/shard_map/ppermute | solution.py:324
  11.1 5.2 %collective-permute-start.1 = (bf16[80,896]{1,0:T(8,128)(2,1)S(1)}, bf16[80,896]{1,0:T(8,128)(2,1)S(1)}, u32[]{:S(2)}, u32[]{:S(2)}) collective-permute-start(bf16[80,896]{1,0:T(8,128)(2,1)S(1)} %get-tuple-element.38), channel_id=1, source_target_pairs={{0,1},{1,0},{2,3},{3,2},{4,5},{5,4},{6,7},{7,6},{8,9},{9,8},{10,11... | collective-permute-start | bytes 430088 | tf_op jit(solution)/shard_map/ppermute | solution.py:324
  12.4 8.9 %collective-permute-start.2 = (bf16[80,896]{1,0:T(8,128)(2,1)S(1)}, bf16[80,896]{1,0:T(8,128)(2,1)S(1)}, u32[]{:S(2)}, u32[]{:S(2)}) collective-permute-start(bf16[80,896]{1,0:T(8,128)(2,1)S(1)} %get-tuple-element.39), channel_id=1, source_target_pairs={{0,3},{3,0},{1,2},{2,1},{4,7},{7,4},{5,6},{6,5},{8,11},{11,8},{9,1... | collective-permute-start | bytes 430088 | tf_op jit(solution)/shard_map/ppermute | solution.py:324
  14.9 21.6 %collective-permute-start.17 = (bf16[112,640]{1,0:T(8,128)(2,1)S(1)}, bf16[112,640]{1,0:T(8,128)(2,1)S(1)}, u32[]{:S(2)}, u32[]{:S(2)}) collective-permute-start(bf16[112,640]{1,0:T(8,128)(2,1)S(1)} %pad_maximum_fusion.2), channel_id=1, source_target_pairs={{0,128},{4,132},{8,136},{12,140},{16,144},{20,148},{24,152},{28,15... | collective-permute-start | bytes 430088 | tf_op jit(solution)/shard_map/ppermute | solution.py:347
  16.0 21.4 %collective-permute-start.3 = (bf16[64,3584]{1,0:T(8,128)(2,1)}, bf16[64,3584]{1,0:T(8,128)(2,1)S(1)}, u32[]{:S(2)}, u32[]{:S(2)}) collective-permute-start(bf16[64,3584]{1,0:T(8,128)(2,1)} %tokens_ref.3), channel_id=1, source_target_pairs={{0,2},{2,0},{1,3},{3,1},{4,6},{6,4},{5,7},{7,5},{8,10},{10,8},{9,1... | collective-permute-start | bytes 1376264 | tf_op jit(solution)/shard_map/ppermute | solution.py:370
  23.2 13.3 %copy-start.8 = (bf16[640,56]{0,1:T(8,128)(2,1)S(1)}, bf16[640,56]{0,1:T(8,128)(2,1)}, u32[]{:S(2)}) copy-start(bf16[640,56]{0,1:T(8,128)(2,1)} %param.11) | copy-start | bytes 215044
  23.2 13.3 %copy-start.9 = (bf16[56,640]{1,0:T(8,128)(2,1)S(1)}, bf16[56,640]{1,0:T(8,128)(2,1)}, u32[]{:S(2)}) copy-start(bf16[56,640]{1,0:T(8,128)(2,1)} %param.10) | copy-start | bytes 215044
  23.2 49.1 %all-to-all-start = ((bf16[64,9,8,128]{3,2,1,0:T(8,128)(2,1)}), bf16[64,9,8,128]{3,2,1,0:T(8,128)(2,1)}, u32[]{:S(2)}, u32[]{:S(2)}) async-start(bf16[64,9,8,128]{3,2,1,0:T(8,128)(2,1)} %get-tuple-element.40), calls=%async_computation | async-start | bytes 2359296 | tf_op jit(solution)/shard_map/all_to_all | solution.py:372
  36.4 109.2 %all-gather.2.cloned.1.call-start = ((), (), s32[]{:S(2)}) async-start(), calls=%async_computation.2 | async-start | bytes 9461760 | tf_op jit(solution)/shard_map/all_gather | solution.py:352
  38.4 2.6 %collective-permute-start.4 = (bf16[128,3584]{1,0:T(8,128)(2,1)S(1)}, bf16[128,3584]{1,0:T(8,128)(2,1)S(1)}, u32[]{:S(2)}, u32[]{:S(2)}) collective-permute-start(bf16[128,3584]{1,0:T(8,128)(2,1)S(1)} %pair_up.1.x_mine), channel_id=1, source_target_pairs={{0,1},{1,0},{2,3},{3,2},{4,5},{5,4},{6,7},{7,6},{8,9},{9,8},{10,11... | collective-permute-start | bytes 2752520 | tf_op jit(solution)/shard_map/ppermute | solution.py:373
  41.0 1.0 copy-start.4
  73.7 15.3 %collective-permute-start.5 = (bf16[32,9,8,128]{3,2,1,0:T(8,128)(2,1)S(1)}, bf16[32,9,8,128]{3,2,1,0:T(8,128)(2,1)S(1)}, u32[]{:S(2)}, u32[]{:S(2)}) collective-permute-start(bf16[32,9,8,128]{3,2,1,0:T(8,128)(2,1)S(1)} %get-tuple-element.67.x0), channel_id=1, source_target_pairs={{0,2},{2,0},{1,3},{3,1},{4,6},{6,4},{5,7},{7,5},{8,10},{10,8},{9,1... | collective-permute-start | bytes 1769480 | tf_op jit(solution)/shard_map/ppermute | solution.py:381
  73.8 15.7 %collective-permute-start.6 = (bf16[32,9,8,128]{3,2,1,0:T(8,128)(2,1)S(1)}, bf16[32,9,8,128]{3,2,1,0:T(8,128)(2,1)S(1)}, u32[]{:S(2)}, u32[]{:S(2)}) collective-permute-start(bf16[32,9,8,128]{3,2,1,0:T(8,128)(2,1)S(1)} %get-tuple-element.67.x0), channel_id=1, source_target_pairs={{0,1},{1,0},{2,3},{3,2},{4,5},{5,4},{6,7},{7,6},{8,9},{9,8},{10,11... | collective-permute-start | bytes 1769480 | tf_op jit(solution)/shard_map/ppermute | solution.py:328
  89.0 2.2 %collective-permute-start.7 = (bf16[32,9,8,128]{3,2,1,0:T(8,128)(2,1)S(1)}, bf16[32,9,8,128]{3,2,1,0:T(8,128)(2,1)S(1)}, u32[]{:S(2)}, u32[]{:S(2)}) collective-permute-start(bf16[32,9,8,128]{3,2,1,0:T(8,128)(2,1)S(1)} %collective-permute-done.5.x1), channel_id=1, source_target_pairs={{0,1},{1,0},{2,3},{3,2},{4,5},{5,4},{6,7},{7,6},{8,9},{9,8},{10,11... | collective-permute-start | bytes 1769480 | tf_op jit(solution)/shard_map/ppermute | solution.py:329
  89.5 15.1 %collective-permute-start.9 = (bf16[32,9,8,128]{3,2,1,0:T(8,128)(2,1)S(1)}, bf16[32,9,8,128]{3,2,1,0:T(8,128)(2,1)S(1)}, u32[]{:S(2)}, u32[]{:S(2)}) collective-permute-start(bf16[32,9,8,128]{3,2,1,0:T(8,128)(2,1)S(1)} %get-tuple-element.46.x0), channel_id=1, source_target_pairs={{0,2},{2,0},{1,3},{3,1},{4,6},{6,4},{5,7},{7,5},{8,10},{10,8},{9,1... | collective-permute-start | bytes 1769480 | tf_op jit(solution)/shard_map/ppermute | solution.py:381
  91.1 2.3 %copy-start = (bf16[1,3584,640]{2,1,0:T(8,128)(2,1)S(1)}, bf16[1,3584,640]{2,1,0:T(8,128)(2,1)}, u32[]{:S(2)}) copy-start(bf16[1,3584,640]{2,1,0:T(8,128)(2,1)} %param.12) | copy-start | bytes 13762564
  93.4 2.8 %copy-start.2 = (bf16[1,640,3584]{2,1,0:T(8,128)(2,1)S(1)}, bf16[1,640,3584]{2,1,0:T(8,128)(2,1)}, u32[]{:S(2)}) copy-start(bf16[1,640,3584]{2,1,0:T(8,128)(2,1)} %param.13) | copy-start | bytes 13762564
  96.2 10.7 %copy-start.1 = (bf16[1,3584,640]{2,1,0:T(8,128)(2,1)S(1)}, bf16[1,3584,640]{2,1,0:T(8,128)(2,1)}, u32[]{:S(2)}) copy-start(bf16[1,3584,640]{2,1,0:T(8,128)(2,1)} %param.12) | copy-start | bytes 13762564
  101.8 3.4 %collective-permute-start.13 = (bf16[32,9,8,128]{3,2,1,0:T(8,128)(2,1)S(1)}, bf16[32,9,8,128]{3,2,1,0:T(8,128)(2,1)S(1)}, u32[]{:S(2)}, u32[]{:S(2)}) collective-permute-start(bf16[32,9,8,128]{3,2,1,0:T(8,128)(2,1)S(1)} %get-tuple-element.49), channel_id=1, source_target_pairs={{0,1},{1,0},{2,3},{3,2},{4,5},{5,4},{6,7},{7,6},{8,9},{9,8},{10,11... | collective-permute-start | bytes 1769480 | tf_op jit(solution)/shard_map/ppermute | solution.py:385
  102.2 3.3 %collective-permute-start.10 = (bf16[32,9,8,128]{3,2,1,0:T(8,128)(2,1)S(1)}, bf16[32,9,8,128]{3,2,1,0:T(8,128)(2,1)S(1)}, u32[]{:S(2)}, u32[]{:S(2)}) collective-permute-start(bf16[32,9,8,128]{3,2,1,0:T(8,128)(2,1)S(1)} %get-tuple-element.46.x0), channel_id=1, source_target_pairs={{0,1},{1,0},{2,3},{3,2},{4,5},{5,4},{6,7},{7,6},{8,9},{9,8},{10,11... | collective-permute-start | bytes 1769480 | tf_op jit(solution)/shard_map/ppermute | solution.py:328
  104.6 2.3 %collective-permute-start.11 = (bf16[32,9,8,128]{3,2,1,0:T(8,128)(2,1)S(1)}, bf16[32,9,8,128]{3,2,1,0:T(8,128)(2,1)S(1)}, u32[]{:S(2)}, u32[]{:S(2)}) collective-permute-start(bf16[32,9,8,128]{3,2,1,0:T(8,128)(2,1)S(1)} %collective-permute-done.9.x1), channel_id=1, source_target_pairs={{0,1},{1,0},{2,3},{3,2},{4,5},{5,4},{6,7},{7,6},{8,9},{9,8},{10,11... | collective-permute-start | bytes 1769480 | tf_op jit(solution)/shard_map/ppermute | solution.py:329
  105.4 15.2 %collective-permute-start.14 = (bf16[32,9,8,128]{3,2,1,0:T(8,128)(2,1)S(1)}, bf16[32,9,8,128]{3,2,1,0:T(8,128)(2,1)S(1)}, u32[]{:S(2)}, u32[]{:S(2)}) collective-permute-start(bf16[32,9,8,128]{3,2,1,0:T(8,128)(2,1)S(1)} %add_convert_fusion.3), channel_id=1, source_target_pairs={{0,2},{2,0},{1,3},{3,1},{4,6},{6,4},{5,7},{7,5},{8,10},{10,8},{9,1... | collective-permute-start | bytes 1769480 | tf_op jit(solution)/shard_map/ppermute | solution.py:391
  112.5 8.1 %collective-permute-start.12 = (bf16[32,9,8,128]{3,2,1,0:T(8,128)(2,1)S(1)}, bf16[32,9,8,128]{3,2,1,0:T(8,128)(2,1)S(1)}, u32[]{:S(2)}, u32[]{:S(2)}) collective-permute-start(bf16[32,9,8,128]{3,2,1,0:T(8,128)(2,1)S(1)} %get-tuple-element.47), channel_id=1, source_target_pairs={{0,1},{1,0},{2,3},{3,2},{4,5},{5,4},{6,7},{7,6},{8,9},{9,8},{10,11... | collective-permute-start | bytes 1769480 | tf_op jit(solution)/shard_map/ppermute | solution.py:385
  112.9 7.9 %collective-permute-start.8 = (bf16[32,9,8,128]{3,2,1,0:T(8,128)(2,1)S(1)}, bf16[32,9,8,128]{3,2,1,0:T(8,128)(2,1)S(1)}, u32[]{:S(2)}, u32[]{:S(2)}) collective-permute-start(bf16[32,9,8,128]{3,2,1,0:T(8,128)(2,1)S(1)} %get-tuple-element.45), channel_id=1, source_target_pairs={{0,1},{1,0},{2,3},{3,2},{4,5},{5,4},{6,7},{7,6},{8,9},{9,8},{10,11... | collective-permute-start | bytes 1769480 | tf_op jit(solution)/shard_map/ppermute | solution.py:386
  113.1 8.0 %collective-permute-start.15 = (bf16[32,9,8,128]{3,2,1,0:T(8,128)(2,1)S(1)}, bf16[32,9,8,128]{3,2,1,0:T(8,128)(2,1)S(1)}, u32[]{:S(2)}, u32[]{:S(2)}) collective-permute-start(bf16[32,9,8,128]{3,2,1,0:T(8,128)(2,1)S(1)} %get-tuple-element.53), channel_id=1, source_target_pairs={{0,1},{1,0},{2,3},{3,2},{4,5},{5,4},{6,7},{7,6},{8,9},{9,8},{10,11... | collective-permute-start | bytes 1769480 | tf_op jit(solution)/shard_map/ppermute | solution.py:386
  120.7 14.4 %collective-permute-start.16 = (bf16[32,9,8,128]{3,2,1,0:T(8,128)(2,1)S(1)}, bf16[32,9,8,128]{3,2,1,0:T(8,128)(2,1)S(1)}, u32[]{:S(2)}, u32[]{:S(2)}) collective-permute-start(bf16[32,9,8,128]{3,2,1,0:T(8,128)(2,1)S(1)} %add_convert_fusion.1), channel_id=1, source_target_pairs={{0,2},{2,0},{1,3},{3,1},{4,6},{6,4},{5,7},{7,5},{8,10},{10,8},{9,1... | collective-permute-start | bytes 1769480 | tf_op jit(solution)/shard_map/ppermute | solution.py:391
  136.5 35.8 %all-to-all-start.1 = ((bf16[64,9,8,128]{3,2,1,0:T(8,128)(2,1)}), bf16[64,9,8,128]{3,2,1,0:T(8,128)(2,1)S(1)}, u32[]{:S(2)}, u32[]{:S(2)}) async-start(bf16[64,9,8,128]{3,2,1,0:T(8,128)(2,1)} %pad_maximum_fusion), calls=%async_computation.1 | async-start | bytes 2359296 | tf_op jit(solution)/shard_map/all_to_all | solution.py:399
  145.6 3.6 %copy-start.3 = (bf16[7168,640]{1,0:T(8,128)(2,1)S(1)}, bf16[7168,640]{1,0:T(8,128)(2,1)}, u32[]{:S(2)}) copy-start(bf16[7168,640]{1,0:T(8,128)(2,1)} %all-gather.2.cloned.1.call-done) | copy-start | bytes 27525124
  149.2 1.2 copy-start.5
  155.4 3.3 %collective-permute-start.18 = (bf16[2,64,3584]{2,1,0:T(8,128)(2,1)S(1)}, bf16[2,64,3584]{2,1,0:T(8,128)(2,1)S(1)}, u32[]{:S(2)}, u32[]{:S(2)}) collective-permute-start(bf16[2,64,3584]{2,1,0:T(8,128)(2,1)S(1)} %get-tuple-element.61), channel_id=1, source_target_pairs={{0,1},{1,0},{2,3},{3,2},{4,5},{5,4},{6,7},{7,6},{8,9},{9,8},{10,11... | collective-permute-start | bytes 2752520 | tf_op jit(solution)/shard_map/ppermute | solution.py:334
  159.6 24.0 %collective-permute-start.19 = (bf16[64,3584]{1,0:T(8,128)(2,1)}, bf16[64,3584]{1,0:T(8,128)(2,1)S(1)}, u32[]{:S(2)}, u32[]{:S(2)}) collective-permute-start(bf16[64,3584]{1,0:T(8,128)(2,1)} %fusion), channel_id=1, source_target_pairs={{0,2},{2,0},{1,3},{3,1},{4,6},{6,4},{5,7},{7,5},{8,10},{10,8},{9,1... | collective-permute-start | bytes 1376264 | tf_op jit(solution)/shard_map/ppermute | solution.py:336
  173.4 5.4 %collective-permute-start.20 = (bf16[64,896]{1,0:T(8,128)(2,1)S(1)}, bf16[64,896]{1,0:T(8,128)(2,1)S(1)}, u32[]{:S(2)}, u32[]{:S(2)}) collective-permute-start(bf16[64,896]{1,0:T(8,128)(2,1)S(1)} %get-tuple-element.64), channel_id=1, source_target_pairs={{0,2},{2,0},{1,3},{3,1},{4,6},{6,4},{5,7},{7,5},{8,10},{10,8},{9,1... | collective-permute-start | bytes 344072 | tf_op jit(solution)/shard_map/ppermute | solution.py:324
  173.5 5.3 %collective-permute-start.21 = (bf16[64,896]{1,0:T(8,128)(2,1)S(1)}, bf16[64,896]{1,0:T(8,128)(2,1)S(1)}, u32[]{:S(2)}, u32[]{:S(2)}) collective-permute-start(bf16[64,896]{1,0:T(8,128)(2,1)S(1)} %get-tuple-element.65), channel_id=1, source_target_pairs={{0,1},{1,0},{2,3},{3,2},{4,5},{5,4},{6,7},{7,6},{8,9},{9,8},{10,11... | collective-permute-start | bytes 344072 | tf_op jit(solution)/shard_map/ppermute | solution.py:324
  177.4 6.2 %collective-permute-start.22 = (bf16[64,896]{1,0:T(8,128)(2,1)S(1)}, bf16[64,896]{1,0:T(8,128)(2,1)S(1)}, u32[]{:S(2)}, u32[]{:S(2)}) collective-permute-start(bf16[64,896]{1,0:T(8,128)(2,1)S(1)} %get-tuple-element.66), channel_id=1, source_target_pairs={{0,3},{3,0},{1,2},{2,1},{4,7},{7,4},{5,6},{6,5},{8,11},{11,8},{9,1... | collective-permute-start | bytes 344072 | tf_op jit(solution)/shard_map/ppermute | solution.py:324
Sparse Core Ops, SparseCore 0:
  39.8 105.7 all-gather.1

commit v5 on v4

--- a/solution.py
+++ b/solution.py
@@ -77,11 +77,11 @@
 PARAMS = pltpu.CompilerParams(vmem_limit_bytes=VMEM)
 
 
-def pack_kernel(place_ref, tokens_ref, ids_ref, codes_ref, *out_refs):
+def pack_kernel(place_ref, tokens_ref, pairs_ref, *out_refs):
     rows, part = tokens_ref.shape[0], out_refs[0].shape[1]
     group = len(out_refs) * rows
-    codes = codes_ref[...]
-    fields = [ids_ref[...], codes >> 5, codes & 31, jnp.zeros((META - 6, rows), jnp.int32)]
+    ids, codes = pairs_ref[:2, :], pairs_ref[2:4, :]
+    fields = [ids, codes >> 5, codes & 31, jnp.zeros((META - 6, rows), jnp.int32)]
     fields = jnp.concatenate(fields, axis=0).astype(F32)
     lane = lax.broadcasted_iota(jnp.int32, (META, group), 1)
     own = (lane >= place_ref[0] * rows) & (lane < (place_ref[0] + 1) * rows)
@@ -92,18 +92,18 @@
         out_ref[rows:, :] = meta
 
 
-def pack(place, tokens, ids, codes):
+def pack(place, tokens, pairs):
     rows, width = tokens.shape
     block = jax.ShapeDtypeStruct((rows + META, width // 4), BF16)
     return pl.pallas_call(
         pack_kernel,
-        in_specs=[SMEM] + [WHOLE] * 3,
+        in_specs=[SMEM] + [WHOLE] * 2,
         out_specs=[WHOLE] * 4,
         out_shape=[block] * 4,
         compiler_params=PARAMS,
         cost_estimate=COST,
         name="pack",
-    )(place, tokens, ids, codes)
+    )(place, tokens, pairs)
 
 
 def pair_kernel(a_ref, b_ref, out_ref):
@@ -216,6 +216,25 @@
     )(place, *xs, up, down)
 
 
+def total_kernel(first_ref, a_ref, b_ref, c_ref, out_ref):
+    done = first_ref.shape[0]
+    out_ref[:done] = first_ref[...]
+    total = a_ref[...].astype(F32) + b_ref[...].astype(F32) + c_ref[...].astype(F32)
+    out_ref[done:] = total.astype(BF16)
+
+
+def total_of(first, terms):
+    return pl.pallas_call(
+        total_kernel,
+        in_specs=[WHOLE] * 4,
+        out_specs=WHOLE,
+        out_shape=jax.ShapeDtypeStruct((first.shape[0] + terms[0].shape[0],) + first.shape[1:], BF16),
+        compiler_params=PARAMS,
+        cost_estimate=COST,
+        name="total",
+    )(first, *terms)
+
+
 def combine_kernel(capacity, place_ref, x_ref, plan_ref, o0, o1, o2, o3, scratch, routed):
     count = x_ref.shape[0]
     plan = plan_ref[...]
@@ -340,10 +359,11 @@
     return (x * N_Z + z) * N_Y + y
 
 
-def gather_dense(dense_up, dense_down, after):
+def gather_dense(dense_up, dense_down, before, after):
     rows, units = dense_up.shape
     places = [(x, z, y) for x in range(N_X) for z in range(N_Z) for y in range(N_Y)]
     both = jnp.concatenate([dense_up, dense_down.T], axis=0)
+    both, _ = lax.optimization_barrier((both, before))
     mate = lax.ppermute(both, "expert", [(expert_at(x, z, y), expert_at(1 - x, z, y)) for x, z, y in places])
     mate, _ = lax.optimization_barrier((mate, after))
     low = lax.axis_index("expert") < N_Z * N_Y
@@ -363,11 +383,12 @@
     capacity = 5 * group // (2 * n_experts)
     part = width // n_tensor
 
-    grouped = swap(pack(spot, tokens, expert_ids.T, gate_codes.T))
+    grouped = swap(pack(spot, tokens, jnp.concatenate([expert_ids.T, gate_codes.T], axis=0)))
     routed, plan = dispatch(spot, grouped, n_experts, capacity)
-    weights = gather_dense(dense_up, dense_down, plan)
-
-    tokens_pair = pair_up(tokens, lax.ppermute(tokens, "tensor", NEXT))
+    weights = gather_dense(dense_up, dense_down, grouped, plan)
+
+    later, _ = lax.optimization_barrier((tokens, grouped))
+    tokens_pair = pair_up(tokens, lax.ppermute(later, "tensor", NEXT))
 
     routed = lax.all_to_all(routed, "expert", split_axis=0, concat_axis=0, tiled=True)
     tokens_by = tokens_pair, lax.ppermute(tokens_pair, "tensor", CORE)
@@ -390,7 +411,8 @@
         rest = (beside.astype(F32) + far.astype(F32)).astype(BF16)
         last = lax.ppermute(rest, "tensor", NEXT)
         terms.append([own, other, last])
-    result = jnp.concatenate([(a.astype(F32) + b.astype(F32) + c.astype(F32)).astype(BF16) for a, b, c in terms])
+    a, b, c = terms[0]
+    result = total_of((a.astype(F32) + b.astype(F32) + c.astype(F32)).astype(BF16), terms[1])
 
     tokens_by, result = lax.optimization_barrier((tokens_by, result))
     mine, others = dense(tokens_by, weights)

time: 193 us -> 193 us (level)
  starting transfers between devices: 38.1 us -> 51.3 us
  waiting for transfers between devices: 99.3 us -> 87 us
    ppermute x2, waiting for transfers between devices: 17.1 us -> 10.4 us  [local(): near = lax.ppermute(x, 'tensor', NEXT)]
    ppermute x2, starting transfers between devices: 1.21 us -> 4.94 us  [spread(): far = lax.ppermute(near, 'tensor', CORE)]
    all_to_all x1, waiting for transfers between devices: 10.6 us -> 7.33 us  [local(): lax.all_to_all(result, 'expert', split_axis=0, concat_axis=0, tiled=True)]
    ppermute x2, starting transfers between devices: 0.48 us -> 3.67 us  [spread(): other = lax.ppermute(x, 'tensor', CORE)]
    all_to_all x1, waiting for transfers between devices: 30.4 us -> 27.6 us  [local(): lax.all_to_all(routed, 'expert', split_axis=0, concat_axis=0, tiled=True)]
    all_to_all x1, starting transfers between devices: 6.39 us -> 8.81 us  [local(): lax.all_to_all(result, 'expert', split_axis=0, concat_axis=0, tiled=True)]
    ppermute x1, starting transfers between devices: 2.1 us -> 4.22 us  [fold(): return (got, lax.ppermute(rest, 'tensor', NEXT))]
    unnamed x20 -> x14, local copies, waits for them, and re-layouts: 12.2 us -> 10.4 us
  transfers between devices with their start and end apart: 26 -> 26, of which waited for: 13 -> 14; matrix products, arithmetic and copies ran while one was open for 3% -> 2% of each run, Pallas kernels for 11% -> 11%
where the time goes in v5:
time: 193 us; the launch traced here: 192 us
  waiting for transfers between devices  87 us (45%)
  starting transfers between devices  51.3 us (27%)
  Pallas kernels  24.8 us (13%)
  between operations  13.6 us (7%)
  local copies, waits for them, and re-layouts  11.7 us (6%)
  other arithmetic  3.83 us (2%)
    all_to_all x1, waiting for transfers between devices, local(): lax.all_to_all(routed, 'expert', split_axis=0, concat_axis=0, tiled=True)  27.6 us
    ppermute x2, waiting for transfers between devices, local(): last = lax.ppermute(rest, 'tensor', NEXT)  21.1 us
    all_to_all x1, starting transfers between devices, local(): lax.all_to_all(routed, 'expert', split_axis=0, concat_axis=0, tiled=True)  13.5 us
    pallas_call x2, Pallas kernels, experts(): pl.pallas_call(functools.partial(experts_kernel, capacity), in_specs=[SME...  11.2 us
    ppermute x2, waiting for transfers between devices, local(): near = lax.ppermute(x, 'tensor', NEXT)  10.4 us
    unnamed x14, local copies, waits for them, and re-layouts  10.4 us
    ppermute x6, starting transfers between devices, swap(): lax.ppermute(x, 'tensor', perm)  10.3 us
    ppermute x6, waiting for transfers between devices, swap(): lax.ppermute(x, 'tensor', perm)  9.74 us
  transfers between devices with their start and end apart: 26, of which 14 were waited for; matrix products, arithmetic and copies ran while one was open for 2% of the time, Pallas kernels for 11%

profile of v5, /device:TPU:1, one launch (start us, length us, event | category | flops | bytes accessed | tf_op | source)
XLA Modules:
  0.0 192.2 jit_solution(10755086361892567958)
XLA Ops:
  6.5 0.7 pad_add_fusion.pairs_ref
  7.2 1.1 pack.1
  8.3 2.1 %collective-permute-start = (bf16[80,896]{1,0:T(8,128)(2,1)S(1)}, bf16[80,896]{1,0:T(8,128)(2,1)S(1)}, u32[]{:S(2)}, u32[]{:S(2)}) collective-permute-start(bf16[80,896]{1,0:T(8,128)(2,1)S(1)} %get-tuple-element.39), channel_id=1, source_target_pairs={{0,2},{2,0},{1,3},{3,1},{4,6},{6,4},{5,7},{7,5},{8,10},{10,8},{9,1... | collective-permute-start | bytes 430088 | tf_op jit(solution)/shard_map/ppermute | solution.py:343
  10.4 1.3 collective-permute-start.1
  11.7 1.5 collective-permute-start.2
  13.3 0.9 pad_maximum_fusion.1
  14.2 4.7 %collective-permute-done.2.x3 = bf16[80,896]{1,0:T(8,128)(2,1)S(1)} collective-permute-done((bf16[80,896]{1,0:T(8,128)(2,1)S(1)}, bf16[80,896]{1,0:T(8,128)(2,1)S(1)}, u32[]{:S(2)}, u32[]{:S(2)}) %collective-permute-start.2) | collective-permute-done | bytes 143392 | tf_op jit(solution)/shard_map/ppermute | solution.py:343
  18.9 1.6 collective-permute-start.17
  20.8 1.9 dispatch.1
  22.7 13.5 %all-to-all-start = ((bf16[64,9,8,128]{3,2,1,0:T(8,128)(2,1)}), bf16[64,9,8,128]{3,2,1,0:T(8,128)(2,1)}, u32[]{:S(2)}, u32[]{:S(2)}) async-start(bf16[64,9,8,128]{3,2,1,0:T(8,128)(2,1)} %get-tuple-element.42), calls=%async_computation | async-start | bytes 2359296 | tf_op jit(solution)/shard_map/all_to_all | solution.py:393
  36.4 0.7 pad_maximum_fusion
  37.1 1.1 pair_up.1.x_mine
  38.7 2.1 %collective-permute-done.4.x_others = bf16[128,3584]{1,0:T(8,128)(2,1)S(1)} collective-permute-done((bf16[128,3584]{1,0:T(8,128)(2,1)S(1)}, bf16[128,3584]{1,0:T(8,128)(2,1)S(1)}, u32[]{:S(2)}, u32[]{:S(2)}) %collective-permute-start.4) | collective-permute-done | bytes 917536 | tf_op jit(solution)/shard_map/ppermute | solution.py:394
  40.8 1.0 copy-done.5
  41.7 27.6 %all-to-all-done = bf16[64,9,8,128]{3,2,1,0:T(8,128)(2,1)} async-done(((bf16[64,9,8,128]{3,2,1,0:T(8,128)(2,1)}), bf16[64,9,8,128]{3,2,1,0:T(8,128)(2,1)}, u32[]{:S(2)}, u32[]{:S(2)}) %all-to-all-start) | async-done | bytes 1179680 | tf_op jit(solution)/shard_map/all_to_all | solution.py:393
  69.3 1.3 fusion.1
  70.8 3.5 %collective-permute-start.6 = (bf16[32,9,8,128]{3,2,1,0:T(8,128)(2,1)S(1)}, bf16[32,9,8,128]{3,2,1,0:T(8,128)(2,1)S(1)}, u32[]{:S(2)}, u32[]{:S(2)}) collective-permute-start(bf16[32,9,8,128]{3,2,1,0:T(8,128)(2,1)S(1)} %get-tuple-element.71.x0), channel_id=1, source_target_pairs={{0,1},{1,0},{2,3},{3,2},{4,5},{5,4},{6,7},{7,6},{8,9},{9,8},{10,11... | collective-permute-start | bytes 1769480 | tf_op jit(solution)/shard_map/ppermute | solution.py:347
  74.3 7.9 %collective-permute-done.5.x1 = bf16[32,9,8,128]{3,2,1,0:T(8,128)(2,1)S(1)} collective-permute-done((bf16[32,9,8,128]{3,2,1,0:T(8,128)(2,1)S(1)}, bf16[32,9,8,128]{3,2,1,0:T(8,128)(2,1)S(1)}, u32[]{:S(2)}, u32[]{:S(2)}) %collective-permute-start.5) | collective-permute-done | bytes 589856 | tf_op jit(solution)/shard_map/ppermute | solution.py:402
  82.3 4.3 %collective-permute-start.7 = (bf16[32,9,8,128]{3,2,1,0:T(8,128)(2,1)S(1)}, bf16[32,9,8,128]{3,2,1,0:T(8,128)(2,1)S(1)}, u32[]{:S(2)}, u32[]{:S(2)}) collective-permute-start(bf16[32,9,8,128]{3,2,1,0:T(8,128)(2,1)S(1)} %collective-permute-done.5.x1), channel_id=1, source_target_pairs={{0,1},{1,0},{2,3},{3,2},{4,5},{5,4},{6,7},{7,6},{8,9},{9,8},{10,11... | collective-permute-start | bytes 1769480 | tf_op jit(solution)/shard_map/ppermute | solution.py:348
  86.5 1.6 collective-permute-done.7.x3
  88.2 2.3 %copy-done = bf16[1,3584,640]{2,1,0:T(8,128)(2,1)S(1)} copy-done((bf16[1,3584,640]{2,1,0:T(8,128)(2,1)S(1)}, bf16[1,3584,640]{2,1,0:T(8,128)(2,1)}, u32[]{:S(2)}) %copy-start) | copy-done | bytes 4587544
  90.5 2.3 %copy-done.2 = bf16[1,640,3584]{2,1,0:T(8,128)(2,1)S(1)} copy-done((bf16[1,640,3584]{2,1,0:T(8,128)(2,1)S(1)}, bf16[1,640,3584]{2,1,0:T(8,128)(2,1)}, u32[]{:S(2)}) %copy-start.2) | copy-done | bytes 4587544
  92.8 5.6 %experts.2 = (bf16[32,9,8,128]{3,2,1,0:T(8,128)(2,1)S(1)}, bf16[32,9,8,128]{3,2,1,0:T(8,128)(2,1)S(1)}, bf16[32,9,8,128]{3,2,1,0:T(8,128)(2,1)S(1)}, bf16[32,9,8,128]{3,2,1,0:T(8,128)(2,1)S(1)}) custom-call(s32[1]{0:T(128)} %bitcast.place_ref, bf16[32,9,8,128]{3,2,1,0:T(8,128)(2,1)S(1)} %get-tuple-element.71.x0, ...), custom_call_target="tpu_custom_call" | custom-call | flops 1 | bytes 1 | tf_op jit(solution)/shard_map/experts/pallas_call | solution.py:204
  98.4 0.6 collective-permute-start.13
  99.2 2.4 %collective-permute-done.9.x1 = bf16[32,9,8,128]{3,2,1,0:T(8,128)(2,1)S(1)} collective-permute-done((bf16[32,9,8,128]{3,2,1,0:T(8,128)(2,1)S(1)}, bf16[32,9,8,128]{3,2,1,0:T(8,128)(2,1)S(1)}, u32[]{:S(2)}, u32[]{:S(2)}) %collective-permute-start.9) | collective-permute-done | bytes 589856 | tf_op jit(solution)/shard_map/ppermute | solution.py:402
  101.6 0.7 collective-permute-start.11
  102.5 1.4 collective-permute-done.11.x3
  103.9 5.6 %experts.3 = (bf16[32,9,8,128]{3,2,1,0:T(8,128)(2,1)S(1)}, bf16[32,9,8,128]{3,2,1,0:T(8,128)(2,1)S(1)}, bf16[32,9,8,128]{3,2,1,0:T(8,128)(2,1)S(1)}, bf16[32,9,8,128]{3,2,1,0:T(8,128)(2,1)S(1)}) custom-call(s32[1]{0:T(128)} %bitcast.place_ref, bf16[32,9,8,128]{3,2,1,0:T(8,128)(2,1)S(1)} %get-tuple-element.49.x0, ...), custom_call_target="tpu_custom_call" | custom-call | flops 1 | bytes 1 | tf_op jit(solution)/shard_map/experts/pallas_call | solution.py:204
  109.5 0.5 collective-permute-start.12
  110.5 7.1 %collective-permute-done.14 = bf16[32,9,8,128]{3,2,1,0:T(8,128)(2,1)S(1)} collective-permute-done((bf16[32,9,8,128]{3,2,1,0:T(8,128)(2,1)S(1)}, bf16[32,9,8,128]{3,2,1,0:T(8,128)(2,1)S(1)}, u32[]{:S(2)}, u32[]{:S(2)}) %collective-permute-start.14) | collective-permute-done | bytes 589856 | tf_op jit(solution)/shard_map/ppermute | solution.py:412
  118.1 14.0 %collective-permute-done.16.c_ref = bf16[32,9,8,128]{3,2,1,0:T(8,128)(2,1)S(1)} collective-permute-done((bf16[32,9,8,128]{3,2,1,0:T(8,128)(2,1)S(1)}, bf16[32,9,8,128]{3,2,1,0:T(8,128)(2,1)S(1)}, u32[]{:S(2)}, u32[]{:S(2)}) %collective-permute-start.16) | collective-permute-done | bytes 589856 | tf_op jit(solution)/shard_map/ppermute | solution.py:412
  132.1 1.3 total.1
  133.4 8.8 %all-to-all-start.1 = ((bf16[64,9,8,128]{3,2,1,0:T(8,128)(2,1)}), bf16[64,9,8,128]{3,2,1,0:T(8,128)(2,1)S(1)}, u32[]{:S(2)}, u32[]{:S(2)}) async-start(bf16[64,9,8,128]{3,2,1,0:T(8,128)(2,1)} %total.1), calls=%async_computation.1 | async-start | bytes 2359296 | tf_op jit(solution)/shard_map/all_to_all | solution.py:421
  142.2 3.6 %all-gather.2.cloned.1.call-done = bf16[7168,640]{1,0:T(8,128)(2,1)} async-done(((bf16[224,640]{1,0:T(8,128)(2,1)}), bf16[7168,640]{1,0:T(8,128)(2,1)}) %all-gather.2.cloned.1.call-update) | async-done | bytes 9175056 | tf_op jit(solution)/shard_map/all_gather | solution.py:372
  145.8 3.6 %copy-done.4 = bf16[7168,640]{1,0:T(8,128)(2,1)S(1)} copy-done((bf16[7168,640]{1,0:T(8,128)(2,1)S(1)}, bf16[7168,640]{1,0:T(8,128)(2,1)}, u32[]{:S(2)}) %copy-start.4) | copy-done | bytes 9175064
  149.4 1.2 copy-done.6
  150.6 5.0 %dense.1 = (bf16[2,64,3584]{2,1,0:T(8,128)(2,1)S(1)}, bf16[2,64,3584]{2,1,0:T(8,128)(2,1)S(1)}) custom-call(bf16[128,3584]{1,0:T(8,128)(2,1)S(1)} %pair_up.1.x_mine, bf16[128,3584]{1,0:T(8,128)(2,1)S(1)} %copy-done.6, bf16[8,4,2,2,56,640]{5,4,3,2,1,0:T(8,128)(2,1)S(1)} %bitcast.13), custom_call_target="tpu_custom_call" | custom-call | flops 1 | bytes 1 | tf_op jit(solution)/shard_map/dense/pallas_call | solution.py:305
  155.7 1.5 collective-permute-start.18
  157.2 2.1 %collective-permute-done.18.got_ref = bf16[2,64,3584]{2,1,0:T(8,128)(2,1)S(1)} collective-permute-done((bf16[2,64,3584]{2,1,0:T(8,128)(2,1)S(1)}, bf16[2,64,3584]{2,1,0:T(8,128)(2,1)S(1)}, u32[]{:S(2)}, u32[]{:S(2)}) %collective-permute-start.18) | collective-permute-done | bytes 917536 | tf_op jit(solution)/shard_map/ppermute | solution.py:353
  159.3 0.9 fusion
  160.1 4.2 %collective-permute-start.19 = (bf16[64,3584]{1,0:T(8,128)(2,1)}, bf16[64,3584]{1,0:T(8,128)(2,1)S(1)}, u32[]{:S(2)}, u32[]{:S(2)}) collective-permute-start(bf16[64,3584]{1,0:T(8,128)(2,1)} %fusion), channel_id=1, source_target_pairs={{0,2},{2,0},{1,3},{3,1},{4,6},{6,4},{5,7},{7,5},{8,10},{10,8},{9,1... | collective-permute-start | bytes 1376264 | tf_op jit(solution)/shard_map/ppermute | solution.py:355
  164.4 7.3 %all-to-all-done.1.x_ref = bf16[64,9,8,128]{3,2,1,0:T(8,128)(2,1)S(1)} async-done(((bf16[64,9,8,128]{3,2,1,0:T(8,128)(2,1)}), bf16[64,9,8,128]{3,2,1,0:T(8,128)(2,1)S(1)}, u32[]{:S(2)}, u32[]{:S(2)}) %all-to-all-start.1) | async-done | bytes 1179680 | tf_op jit(solution)/shard_map/all_to_all | solution.py:421
  171.7 1.1 combine.1
  172.9 3.8 %collective-permute-start.21 = (bf16[64,896]{1,0:T(8,128)(2,1)S(1)}, bf16[64,896]{1,0:T(8,128)(2,1)S(1)}, u32[]{:S(2)}, u32[]{:S(2)}) collective-permute-start(bf16[64,896]{1,0:T(8,128)(2,1)S(1)} %get-tuple-element.69), channel_id=1, source_target_pairs={{0,1},{1,0},{2,3},{3,2},{4,5},{5,4},{6,7},{7,6},{8,9},{9,8},{10,11... | collective-permute-start | bytes 344072 | tf_op jit(solution)/shard_map/ppermute | solution.py:343
  176.7 1.5 collective-permute-start.22
  178.2 1.6 collective-permute-done.20.r1
  179.9 3.4 %collective-permute-done.22.r3 = bf16[64,896]{1,0:T(8,128)(2,1)S(1)} collective-permute-done((bf16[64,896]{1,0:T(8,128)(2,1)S(1)}, bf16[64,896]{1,0:T(8,128)(2,1)S(1)}, u32[]{:S(2)}, u32[]{:S(2)}) %collective-permute-start.22) | collective-permute-done | bytes 114720 | tf_op jit(solution)/shard_map/ppermute | solution.py:343
  183.2 2.1 %finish.1 = bf16[64,3584]{1,0:T(8,128)(2,1)} custom-call(s32[1]{0:T(128)} %bitcast.place_ref, bf16[64,3584]{1,0:T(8,128)(2,1)} %tokens_ref.3, bf16[2,64,3584]{2,1,0:T(8,128)(2,1)S(1)} %get-tuple-element.64.mine_ref, bf16[2,64,3584]{2,1,0:T(8,128)(2,1)S(1)} %collective-permute-done.18.got_ref, bf16[64,3584]{1,0:T(8,128)(2,1)S(1)} %collective-permute-done.19.last_ref, ...), custom_call_target="tpu_custom_call" | custom-call | flops 1 | bytes 1 | tf_op jit(solution)/shard_map/finish/pallas_call | solution.py:331
  (37 shorter events, 2.5 us)
Async XLA Ops:
  8.3 5.9 %collective-permute-start = (bf16[80,896]{1,0:T(8,128)(2,1)S(1)}, bf16[80,896]{1,0:T(8,128)(2,1)S(1)}, u32[]{:S(2)}, u32[]{:S(2)}) collective-permute-start(bf16[80,896]{1,0:T(8,128)(2,1)S(1)} %get-tuple-element.39), channel_id=1, source_target_pairs={{0,2},{2,0},{1,3},{3,1},{4,6},{6,4},{5,7},{7,5},{8,10},{10,8},{9,1... | collective-permute-start | bytes 430088 | tf_op jit(solution)/shard_map/ppermute | solution.py:343
  10.4 3.8 %collective-permute-start.1 = (bf16[80,896]{1,0:T(8,128)(2,1)S(1)}, bf16[80,896]{1,0:T(8,128)(2,1)S(1)}, u32[]{:S(2)}, u32[]{:S(2)}) collective-permute-start(bf16[80,896]{1,0:T(8,128)(2,1)S(1)} %get-tuple-element.40), channel_id=1, source_target_pairs={{0,1},{1,0},{2,3},{3,2},{4,5},{5,4},{6,7},{7,6},{8,9},{9,8},{10,11... | collective-permute-start | bytes 430088 | tf_op jit(solution)/shard_map/ppermute | solution.py:343
  11.7 7.2 %collective-permute-start.2 = (bf16[80,896]{1,0:T(8,128)(2,1)S(1)}, bf16[80,896]{1,0:T(8,128)(2,1)S(1)}, u32[]{:S(2)}, u32[]{:S(2)}) collective-permute-start(bf16[80,896]{1,0:T(8,128)(2,1)S(1)} %get-tuple-element.41), channel_id=1, source_target_pairs={{0,3},{3,0},{1,2},{2,1},{4,7},{7,4},{5,6},{6,5},{8,11},{11,8},{9,1... | collective-permute-start | bytes 430088 | tf_op jit(solution)/shard_map/ppermute | solution.py:343
  18.9 17.4 %collective-permute-start.17 = (bf16[112,640]{1,0:T(8,128)(2,1)S(1)}, bf16[112,640]{1,0:T(8,128)(2,1)S(1)}, u32[]{:S(2)}, u32[]{:S(2)}) collective-permute-start(bf16[112,640]{1,0:T(8,128)(2,1)S(1)} %pad_maximum_fusion.1), channel_id=1, source_target_pairs={{0,128},{4,132},{8,136},{12,140},{16,144},{20,148},{24,152},{28,15... | collective-permute-start | bytes 430088 | tf_op jit(solution)/shard_map/ppermute | solution.py:367
  20.5 16.6 %collective-permute-start.3 = (bf16[64,3584]{1,0:T(8,128)(2,1)}, bf16[64,3584]{1,0:T(8,128)(2,1)S(1)}, u32[]{:S(2)}, u32[]{:S(2)}) collective-permute-start(bf16[64,3584]{1,0:T(8,128)(2,1)} %tokens_ref.3), channel_id=1, source_target_pairs={{0,2},{2,0},{1,3},{3,1},{4,6},{6,4},{5,7},{7,5},{8,10},{10,8},{9,1... | collective-permute-start | bytes 1376264 | tf_op jit(solution)/shard_map/ppermute | solution.py:391
  22.7 46.6 %all-to-all-start = ((bf16[64,9,8,128]{3,2,1,0:T(8,128)(2,1)}), bf16[64,9,8,128]{3,2,1,0:T(8,128)(2,1)}, u32[]{:S(2)}, u32[]{:S(2)}) async-start(bf16[64,9,8,128]{3,2,1,0:T(8,128)(2,1)} %get-tuple-element.42), calls=%async_computation | async-start | bytes 2359296 | tf_op jit(solution)/shard_map/all_to_all | solution.py:393
  36.3 109.6 %all-gather.2.cloned.1.call-start = ((), (), s32[]{:S(2)}) async-start(), calls=%async_computation.2 | async-start | bytes 9461760 | tf_op jit(solution)/shard_map/all_gather | solution.py:372
  38.2 2.6 %collective-permute-start.4 = (bf16[128,3584]{1,0:T(8,128)(2,1)S(1)}, bf16[128,3584]{1,0:T(8,128)(2,1)S(1)}, u32[]{:S(2)}, u32[]{:S(2)}) collective-permute-start(bf16[128,3584]{1,0:T(8,128)(2,1)S(1)} %pair_up.1.x_mine), channel_id=1, source_target_pairs={{0,1},{1,0},{2,3},{3,2},{4,5},{5,4},{6,7},{7,6},{8,9},{9,8},{10,11... | collective-permute-start | bytes 2752520 | tf_op jit(solution)/shard_map/ppermute | solution.py:394
  40.8 1.0 copy-start.5
  70.7 11.6 %collective-permute-start.5 = (bf16[32,9,8,128]{3,2,1,0:T(8,128)(2,1)S(1)}, bf16[32,9,8,128]{3,2,1,0:T(8,128)(2,1)S(1)}, u32[]{:S(2)}, u32[]{:S(2)}) collective-permute-start(bf16[32,9,8,128]{3,2,1,0:T(8,128)(2,1)S(1)} %get-tuple-element.71.x0), channel_id=1, source_target_pairs={{0,2},{2,0},{1,3},{3,1},{4,6},{6,4},{5,7},{7,5},{8,10},{10,8},{9,1... | collective-permute-start | bytes 1769480 | tf_op jit(solution)/shard_map/ppermute | solution.py:402
  70.8 15.7 %collective-permute-start.6 = (bf16[32,9,8,128]{3,2,1,0:T(8,128)(2,1)S(1)}, bf16[32,9,8,128]{3,2,1,0:T(8,128)(2,1)S(1)}, u32[]{:S(2)}, u32[]{:S(2)}) collective-permute-start(bf16[32,9,8,128]{3,2,1,0:T(8,128)(2,1)S(1)} %get-tuple-element.71.x0), channel_id=1, source_target_pairs={{0,1},{1,0},{2,3},{3,2},{4,5},{5,4},{6,7},{7,6},{8,9},{9,8},{10,11... | collective-permute-start | bytes 1769480 | tf_op jit(solution)/shard_map/ppermute | solution.py:347
  82.3 5.9 %collective-permute-start.7 = (bf16[32,9,8,128]{3,2,1,0:T(8,128)(2,1)S(1)}, bf16[32,9,8,128]{3,2,1,0:T(8,128)(2,1)S(1)}, u32[]{:S(2)}, u32[]{:S(2)}) collective-permute-start(bf16[32,9,8,128]{3,2,1,0:T(8,128)(2,1)S(1)} %collective-permute-done.5.x1), channel_id=1, source_target_pairs={{0,1},{1,0},{2,3},{3,2},{4,5},{5,4},{6,7},{7,6},{8,9},{9,8},{10,11... | collective-permute-start | bytes 1769480 | tf_op jit(solution)/shard_map/ppermute | solution.py:348
  86.5 15.1 %collective-permute-start.9 = (bf16[32,9,8,128]{3,2,1,0:T(8,128)(2,1)S(1)}, bf16[32,9,8,128]{3,2,1,0:T(8,128)(2,1)S(1)}, u32[]{:S(2)}, u32[]{:S(2)}) collective-permute-start(bf16[32,9,8,128]{3,2,1,0:T(8,128)(2,1)S(1)} %get-tuple-element.49.x0), channel_id=1, source_target_pairs={{0,2},{2,0},{1,3},{3,1},{4,6},{6,4},{5,7},{7,5},{8,10},{10,8},{9,1... | collective-permute-start | bytes 1769480 | tf_op jit(solution)/shard_map/ppermute | solution.py:402
  88.2 2.3 %copy-start = (bf16[1,3584,640]{2,1,0:T(8,128)(2,1)S(1)}, bf16[1,3584,640]{2,1,0:T(8,128)(2,1)}, u32[]{:S(2)}) copy-start(bf16[1,3584,640]{2,1,0:T(8,128)(2,1)} %param.12) | copy-start | bytes 13762564
  90.5 2.3 %copy-start.2 = (bf16[1,640,3584]{2,1,0:T(8,128)(2,1)S(1)}, bf16[1,640,3584]{2,1,0:T(8,128)(2,1)}, u32[]{:S(2)}) copy-start(bf16[1,640,3584]{2,1,0:T(8,128)(2,1)} %param.13) | copy-start | bytes 13762564
  92.8 11.1 %copy-start.1 = (bf16[1,3584,640]{2,1,0:T(8,128)(2,1)S(1)}, bf16[1,3584,640]{2,1,0:T(8,128)(2,1)}, u32[]{:S(2)}) copy-start(bf16[1,3584,640]{2,1,0:T(8,128)(2,1)} %param.12) | copy-start | bytes 13762564
  92.8 11.1 %copy-start.3 = (bf16[1,640,3584]{2,1,0:T(8,128)(2,1)S(1)}, bf16[1,640,3584]{2,1,0:T(8,128)(2,1)}, u32[]{:S(2)}) copy-start(bf16[1,640,3584]{2,1,0:T(8,128)(2,1)} %param.13) | copy-start | bytes 13762564
  98.4 3.9 %collective-permute-start.13 = (bf16[32,9,8,128]{3,2,1,0:T(8,128)(2,1)S(1)}, bf16[32,9,8,128]{3,2,1,0:T(8,128)(2,1)S(1)}, u32[]{:S(2)}, u32[]{:S(2)}) collective-permute-start(bf16[32,9,8,128]{3,2,1,0:T(8,128)(2,1)S(1)} %get-tuple-element.52), channel_id=1, source_target_pairs={{0,1},{1,0},{2,3},{3,2},{4,5},{5,4},{6,7},{7,6},{8,9},{9,8},{10,11... | collective-permute-start | bytes 1769480 | tf_op jit(solution)/shard_map/ppermute | solution.py:406
  99.0 3.5 %collective-permute-start.10 = (bf16[32,9,8,128]{3,2,1,0:T(8,128)(2,1)S(1)}, bf16[32,9,8,128]{3,2,1,0:T(8,128)(2,1)S(1)}, u32[]{:S(2)}, u32[]{:S(2)}) collective-permute-start(bf16[32,9,8,128]{3,2,1,0:T(8,128)(2,1)S(1)} %get-tuple-element.49.x0), channel_id=1, source_target_pairs={{0,1},{1,0},{2,3},{3,2},{4,5},{5,4},{6,7},{7,6},{8,9},{9,8},{10,11... | collective-permute-start | bytes 1769480 | tf_op jit(solution)/shard_map/ppermute | solution.py:347
  101.6 2.3 %collective-permute-start.11 = (bf16[32,9,8,128]{3,2,1,0:T(8,128)(2,1)S(1)}, bf16[32,9,8,128]{3,2,1,0:T(8,128)(2,1)S(1)}, u32[]{:S(2)}, u32[]{:S(2)}) collective-permute-start(bf16[32,9,8,128]{3,2,1,0:T(8,128)(2,1)S(1)} %collective-permute-done.9.x1), channel_id=1, source_target_pairs={{0,1},{1,0},{2,3},{3,2},{4,5},{5,4},{6,7},{7,6},{8,9},{9,8},{10,11... | collective-permute-start | bytes 1769480 | tf_op jit(solution)/shard_map/ppermute | solution.py:348
  102.4 15.2 %collective-permute-start.14 = (bf16[32,9,8,128]{3,2,1,0:T(8,128)(2,1)S(1)}, bf16[32,9,8,128]{3,2,1,0:T(8,128)(2,1)S(1)}, u32[]{:S(2)}, u32[]{:S(2)}) collective-permute-start(bf16[32,9,8,128]{3,2,1,0:T(8,128)(2,1)S(1)} %add_convert_fusion.2), channel_id=1, source_target_pairs={{0,2},{2,0},{1,3},{3,1},{4,6},{6,4},{5,7},{7,5},{8,10},{10,8},{9,1... | collective-permute-start | bytes 1769480 | tf_op jit(solution)/shard_map/ppermute | solution.py:412
  109.5 8.1 %collective-permute-start.12 = (bf16[32,9,8,128]{3,2,1,0:T(8,128)(2,1)S(1)}, bf16[32,9,8,128]{3,2,1,0:T(8,128)(2,1)S(1)}, u32[]{:S(2)}, u32[]{:S(2)}) collective-permute-start(bf16[32,9,8,128]{3,2,1,0:T(8,128)(2,1)S(1)} %get-tuple-element.50), channel_id=1, source_target_pairs={{0,1},{1,0},{2,3},{3,2},{4,5},{5,4},{6,7},{7,6},{8,9},{9,8},{10,11... | collective-permute-start | bytes 1769480 | tf_op jit(solution)/shard_map/ppermute | solution.py:406
  110.0 7.9 %collective-permute-start.8 = (bf16[32,9,8,128]{3,2,1,0:T(8,128)(2,1)S(1)}, bf16[32,9,8,128]{3,2,1,0:T(8,128)(2,1)S(1)}, u32[]{:S(2)}, u32[]{:S(2)}) collective-permute-start(bf16[32,9,8,128]{3,2,1,0:T(8,128)(2,1)S(1)} %get-tuple-element.48), channel_id=1, source_target_pairs={{0,1},{1,0},{2,3},{3,2},{4,5},{5,4},{6,7},{7,6},{8,9},{9,8},{10,11... | collective-permute-start | bytes 1769480 | tf_op jit(solution)/shard_map/ppermute | solution.py:407
  110.1 8.0 %collective-permute-start.15 = (bf16[32,9,8,128]{3,2,1,0:T(8,128)(2,1)S(1)}, bf16[32,9,8,128]{3,2,1,0:T(8,128)(2,1)S(1)}, u32[]{:S(2)}, u32[]{:S(2)}) collective-permute-start(bf16[32,9,8,128]{3,2,1,0:T(8,128)(2,1)S(1)} %get-tuple-element.56), channel_id=1, source_target_pairs={{0,1},{1,0},{2,3},{3,2},{4,5},{5,4},{6,7},{7,6},{8,9},{9,8},{10,11... | collective-permute-start | bytes 1769480 | tf_op jit(solution)/shard_map/ppermute | solution.py:407
  117.8 14.4 %collective-permute-start.16 = (bf16[32,9,8,128]{3,2,1,0:T(8,128)(2,1)S(1)}, bf16[32,9,8,128]{3,2,1,0:T(8,128)(2,1)S(1)}, u32[]{:S(2)}, u32[]{:S(2)}) collective-permute-start(bf16[32,9,8,128]{3,2,1,0:T(8,128)(2,1)S(1)} %add_convert_fusion), channel_id=1, source_target_pairs={{0,2},{2,0},{1,3},{3,1},{4,6},{6,4},{5,7},{7,5},{8,10},{10,8},{9,1... | collective-permute-start | bytes 1769480 | tf_op jit(solution)/shard_map/ppermute | solution.py:412
  133.4 38.3 %all-to-all-start.1 = ((bf16[64,9,8,128]{3,2,1,0:T(8,128)(2,1)}), bf16[64,9,8,128]{3,2,1,0:T(8,128)(2,1)S(1)}, u32[]{:S(2)}, u32[]{:S(2)}) async-start(bf16[64,9,8,128]{3,2,1,0:T(8,128)(2,1)} %total.1), calls=%async_computation.1 | async-start | bytes 2359296 | tf_op jit(solution)/shard_map/all_to_all | solution.py:421
  145.8 3.6 %copy-start.4 = (bf16[7168,640]{1,0:T(8,128)(2,1)S(1)}, bf16[7168,640]{1,0:T(8,128)(2,1)}, u32[]{:S(2)}) copy-start(bf16[7168,640]{1,0:T(8,128)(2,1)} %all-gather.2.cloned.1.call-done) | copy-start | bytes 27525124
  149.4 1.2 copy-start.6
  155.7 3.6 %collective-permute-start.18 = (bf16[2,64,3584]{2,1,0:T(8,128)(2,1)S(1)}, bf16[2,64,3584]{2,1,0:T(8,128)(2,1)S(1)}, u32[]{:S(2)}, u32[]{:S(2)}) collective-permute-start(bf16[2,64,3584]{2,1,0:T(8,128)(2,1)S(1)} %get-tuple-element.65), channel_id=1, source_target_pairs={{0,1},{1,0},{2,3},{3,2},{4,5},{5,4},{6,7},{7,6},{8,9},{9,8},{10,11... | collective-permute-start | bytes 2752520 | tf_op jit(solution)/shard_map/ppermute | solution.py:353
  160.1 23.1 %collective-permute-start.19 = (bf16[64,3584]{1,0:T(8,128)(2,1)}, bf16[64,3584]{1,0:T(8,128)(2,1)S(1)}, u32[]{:S(2)}, u32[]{:S(2)}) collective-permute-start(bf16[64,3584]{1,0:T(8,128)(2,1)} %fusion), channel_id=1, source_target_pairs={{0,2},{2,0},{1,3},{3,1},{4,6},{6,4},{5,7},{7,5},{8,10},{10,8},{9,1... | collective-permute-start | bytes 1376264 | tf_op jit(solution)/shard_map/ppermute | solution.py:355
  172.8 7.1 %collective-permute-start.20 = (bf16[64,896]{1,0:T(8,128)(2,1)S(1)}, bf16[64,896]{1,0:T(8,128)(2,1)S(1)}, u32[]{:S(2)}, u32[]{:S(2)}) collective-permute-start(bf16[64,896]{1,0:T(8,128)(2,1)S(1)} %get-tuple-element.68), channel_id=1, source_target_pairs={{0,2},{2,0},{1,3},{3,1},{4,6},{6,4},{5,7},{7,5},{8,10},{10,8},{9,1... | collective-permute-start | bytes 344072 | tf_op jit(solution)/shard_map/ppermute | solution.py:343
  172.9 7.0 %collective-permute-start.21 = (bf16[64,896]{1,0:T(8,128)(2,1)S(1)}, bf16[64,896]{1,0:T(8,128)(2,1)S(1)}, u32[]{:S(2)}, u32[]{:S(2)}) collective-permute-start(bf16[64,896]{1,0:T(8,128)(2,1)S(1)} %get-tuple-element.69), channel_id=1, source_target_pairs={{0,1},{1,0},{2,3},{3,2},{4,5},{5,4},{6,7},{7,6},{8,9},{9,8},{10,11... | collective-permute-start | bytes 344072 | tf_op jit(solution)/shard_map/ppermute | solution.py:343
  176.7 6.6 %collective-permute-start.22 = (bf16[64,896]{1,0:T(8,128)(2,1)S(1)}, bf16[64,896]{1,0:T(8,128)(2,1)S(1)}, u32[]{:S(2)}, u32[]{:S(2)}) collective-permute-start(bf16[64,896]{1,0:T(8,128)(2,1)S(1)} %get-tuple-element.70), channel_id=1, source_target_pairs={{0,3},{3,0},{1,2},{2,1},{4,7},{7,4},{5,6},{6,5},{8,11},{11,8},{9,1... | collective-permute-start | bytes 344072 | tf_op jit(solution)/shard_map/ppermute | solution.py:343
Sparse Core Ops, SparseCore 0:
  39.7 106.1 all-gather.1

commit v6 on v5

--- a/solution.py
+++ b/solution.py
@@ -17,7 +17,7 @@
 MAIN = 8
 LANES = 128
 SIZES = (32, 32)
-VMEM = 32 * 1024 * 1024
+VMEM = 16 * 1024 * 1024
 
 
 def dot(a, b, dims=((1,), (0,))):
@@ -312,7 +312,7 @@
             pltpu.VMEM((4, z // 2, y, inner, units), BF16),
             pltpu.SemaphoreType.DMA((N_X + 4,)),
         ],
-        compiler_params=PARAMS,
+        compiler_params=pltpu.CompilerParams(vmem_limit_bytes=56 * 1024 * 1024),
         cost_estimate=COST,
         name="dense",
     )(*xs, weights)

time: 193 us -> 193 us (level)
  local copies, waits for them, and re-layouts: 11.7 us -> 5.96 us
  Pallas kernels: 24.8 us -> 29 us
    unnamed x14, local copies, waits for them, and re-layouts: 10.4 us -> 4.62 us
    pallas_call x1, Pallas kernels: 5.03 us -> 9.12 us  [dense(): pl.pallas_call(dense_kernel, in_specs=[WHOLE] * 2 + [pl.BlockSpec(memory_...]
  transfers between devices with their start and end apart: 26 -> 26, of which waited for: 14 -> 14; matrix products, arithmetic and copies ran while one was open for 2% -> 3% of each run, Pallas kernels for 11% -> 13%
where the time goes in v6:
time: 193 us
  waiting for transfers between devices  87.9 us (46%)
  starting transfers between devices  51.2 us (27%)
  Pallas kernels  29 us (15%)
  between operations  13.6 us (7%)
  local copies, waits for them, and re-layouts  5.96 us (3%)
  other arithmetic  4.93 us (3%)
    all_to_all x1, waiting for transfers between devices, local(): lax.all_to_all(routed, 'expert', split_axis=0, concat_axis=0, tiled=True)  28.6 us
    ppermute x2, waiting for transfers between devices, local(): last = lax.ppermute(rest, 'tensor', NEXT)  21.1 us
    all_to_all x1, starting transfers between devices, local(): lax.all_to_all(routed, 'expert', split_axis=0, concat_axis=0, tiled=True)  13.5 us
    pallas_call x2, Pallas kernels, experts(): pl.pallas_call(functools.partial(experts_kernel, capacity), in_specs=[SME...  11.2 us
    ppermute x2, waiting for transfers between devices, local(): near = lax.ppermute(x, 'tensor', NEXT)  10.4 us
    ppermute x6, starting transfers between devices, swap(): lax.ppermute(x, 'tensor', perm)  10.3 us
    ppermute x6, waiting for transfers between devices, swap(): lax.ppermute(x, 'tensor', perm)  10.1 us
    pallas_call x1, Pallas kernels, dense(): pl.pallas_call(dense_kernel, in_specs=[WHOLE] * 2 + [pl.BlockSpec(memory_...  9.12 us
  transfers between devices with their start and end apart: 26, of which 14 were waited for; matrix products, arithmetic and copies ran while one was open for 3% of the time, Pallas kernels for 13%

profile of v6, /device:TPU:1, one launch (start us, length us, event | category | flops | bytes accessed | tf_op | source)
XLA Modules:
  0.0 192.6 jit_solution(8262889941578117869)
XLA Ops:
  6.5 0.7 pad_add_fusion.pairs_ref
  7.2 1.1 pack.1
  8.3 2.1 %collective-permute-start = (bf16[80,896]{1,0:T(8,128)(2,1)S(1)}, bf16[80,896]{1,0:T(8,128)(2,1)S(1)}, u32[]{:S(2)}, u32[]{:S(2)}) collective-permute-start(bf16[80,896]{1,0:T(8,128)(2,1)S(1)} %get-tuple-element.39), channel_id=1, source_target_pairs={{0,2},{2,0},{1,3},{3,1},{4,6},{6,4},{5,7},{7,5},{8,10},{10,8},{9,1... | collective-permute-start | bytes 430088 | tf_op jit(solution)/shard_map/ppermute | solution.py:343
  10.4 1.3 collective-permute-start.1
  11.7 1.5 collective-permute-start.2
  13.3 0.9 pad_maximum_fusion.1
  14.2 4.7 %collective-permute-done.2.x3 = bf16[80,896]{1,0:T(8,128)(2,1)S(1)} collective-permute-done((bf16[80,896]{1,0:T(8,128)(2,1)S(1)}, bf16[80,896]{1,0:T(8,128)(2,1)S(1)}, u32[]{:S(2)}, u32[]{:S(2)}) %collective-permute-start.2) | collective-permute-done | bytes 143392 | tf_op jit(solution)/shard_map/ppermute | solution.py:343
  18.9 1.6 collective-permute-start.17
  20.5 0.3 collective-permute-start.3
  20.8 1.9 %dispatch.1 = (bf16[64,9,8,128]{3,2,1,0:T(8,128)(2,1)}, f32[8,256]{1,0:T(8,128)S(1)}) custom-call(s32[1]{0:T(128)} %bitcast.place_ref, bf16[80,896]{1,0:T(8,128)(2,1)S(1)} %get-tuple-element.38.x0, bf16[80,896]{1,0:T(8,128)(2,1)S(1)} %collective-permute-done.x1, bf16[80,896]{1,0:T(8,128)(2,1)S(1)} %collective-permute-done.1.x2, ...), custom_call_target="tpu_custom_call" | custom-call | flops 1 | bytes 1 | tf_op jit(solution)/shard_map/dispatch/pallas_call | solution.py:170
  22.8 13.5 %all-to-all-start = ((bf16[64,9,8,128]{3,2,1,0:T(8,128)(2,1)}), bf16[64,9,8,128]{3,2,1,0:T(8,128)(2,1)}, u32[]{:S(2)}, u32[]{:S(2)}) async-start(bf16[64,9,8,128]{3,2,1,0:T(8,128)(2,1)} %get-tuple-element.42), calls=%async_computation | async-start | bytes 2359296 | tf_op jit(solution)/shard_map/all_to_all | solution.py:393
  36.4 0.7 pad_maximum_fusion
  37.2 1.1 pair_up.1.x_mine
  38.3 0.4 collective-permute-start.4
  38.7 2.1 %collective-permute-done.4.x_others = bf16[128,3584]{1,0:T(8,128)(2,1)S(1)} collective-permute-done((bf16[128,3584]{1,0:T(8,128)(2,1)S(1)}, bf16[128,3584]{1,0:T(8,128)(2,1)S(1)}, u32[]{:S(2)}, u32[]{:S(2)}) %collective-permute-start.4) | collective-permute-done | bytes 917536 | tf_op jit(solution)/shard_map/ppermute | solution.py:394
  40.8 28.6 %all-to-all-done = bf16[64,9,8,128]{3,2,1,0:T(8,128)(2,1)} async-done(((bf16[64,9,8,128]{3,2,1,0:T(8,128)(2,1)}), bf16[64,9,8,128]{3,2,1,0:T(8,128)(2,1)}, u32[]{:S(2)}, u32[]{:S(2)}) %all-to-all-start) | async-done | bytes 1179680 | tf_op jit(solution)/shard_map/all_to_all | solution.py:393
  69.4 1.3 fusion.1
  70.9 3.5 %collective-permute-start.6 = (bf16[32,9,8,128]{3,2,1,0:T(8,128)(2,1)S(1)}, bf16[32,9,8,128]{3,2,1,0:T(8,128)(2,1)S(1)}, u32[]{:S(2)}, u32[]{:S(2)}) collective-permute-start(bf16[32,9,8,128]{3,2,1,0:T(8,128)(2,1)S(1)} %get-tuple-element.71.x0), channel_id=1, source_target_pairs={{0,1},{1,0},{2,3},{3,2},{4,5},{5,4},{6,7},{7,6},{8,9},{9,8},{10,11... | collective-permute-start | bytes 1769480 | tf_op jit(solution)/shard_map/ppermute | solution.py:347
  74.4 7.9 %collective-permute-done.5.x1 = bf16[32,9,8,128]{3,2,1,0:T(8,128)(2,1)S(1)} collective-permute-done((bf16[32,9,8,128]{3,2,1,0:T(8,128)(2,1)S(1)}, bf16[32,9,8,128]{3,2,1,0:T(8,128)(2,1)S(1)}, u32[]{:S(2)}, u32[]{:S(2)}) %collective-permute-start.5) | collective-permute-done | bytes 589856 | tf_op jit(solution)/shard_map/ppermute | solution.py:402
  82.3 4.3 %collective-permute-start.7 = (bf16[32,9,8,128]{3,2,1,0:T(8,128)(2,1)S(1)}, bf16[32,9,8,128]{3,2,1,0:T(8,128)(2,1)S(1)}, u32[]{:S(2)}, u32[]{:S(2)}) collective-permute-start(bf16[32,9,8,128]{3,2,1,0:T(8,128)(2,1)S(1)} %collective-permute-done.5.x1), channel_id=1, source_target_pairs={{0,1},{1,0},{2,3},{3,2},{4,5},{5,4},{6,7},{7,6},{8,9},{9,8},{10,11... | collective-permute-start | bytes 1769480 | tf_op jit(solution)/shard_map/ppermute | solution.py:348
  86.6 1.6 collective-permute-done.7.x3
  88.2 2.3 %copy-done = bf16[1,3584,640]{2,1,0:T(8,128)(2,1)S(1)} copy-done((bf16[1,3584,640]{2,1,0:T(8,128)(2,1)S(1)}, bf16[1,3584,640]{2,1,0:T(8,128)(2,1)}, u32[]{:S(2)}) %copy-start) | copy-done | bytes 4587544
  90.5 2.3 %copy-done.2 = bf16[1,640,3584]{2,1,0:T(8,128)(2,1)S(1)} copy-done((bf16[1,640,3584]{2,1,0:T(8,128)(2,1)S(1)}, bf16[1,640,3584]{2,1,0:T(8,128)(2,1)}, u32[]{:S(2)}) %copy-start.2) | copy-done | bytes 4587544
  92.8 5.6 %experts.2 = (bf16[32,9,8,128]{3,2,1,0:T(8,128)(2,1)S(1)}, bf16[32,9,8,128]{3,2,1,0:T(8,128)(2,1)S(1)}, bf16[32,9,8,128]{3,2,1,0:T(8,128)(2,1)S(1)}, bf16[32,9,8,128]{3,2,1,0:T(8,128)(2,1)S(1)}) custom-call(s32[1]{0:T(128)} %bitcast.place_ref, bf16[32,9,8,128]{3,2,1,0:T(8,128)(2,1)S(1)} %get-tuple-element.71.x0, ...), custom_call_target="tpu_custom_call" | custom-call | flops 1 | bytes 1 | tf_op jit(solution)/shard_map/experts/pallas_call | solution.py:204
  98.5 0.6 collective-permute-start.13
  99.2 2.4 %collective-permute-done.9.x1 = bf16[32,9,8,128]{3,2,1,0:T(8,128)(2,1)S(1)} collective-permute-done((bf16[32,9,8,128]{3,2,1,0:T(8,128)(2,1)S(1)}, bf16[32,9,8,128]{3,2,1,0:T(8,128)(2,1)S(1)}, u32[]{:S(2)}, u32[]{:S(2)}) %collective-permute-start.9) | collective-permute-done | bytes 589856 | tf_op jit(solution)/shard_map/ppermute | solution.py:402
  101.7 0.7 collective-permute-start.11
  102.6 1.4 collective-permute-done.11.x3
  104.0 5.6 %experts.3 = (bf16[32,9,8,128]{3,2,1,0:T(8,128)(2,1)S(1)}, bf16[32,9,8,128]{3,2,1,0:T(8,128)(2,1)S(1)}, bf16[32,9,8,128]{3,2,1,0:T(8,128)(2,1)S(1)}, bf16[32,9,8,128]{3,2,1,0:T(8,128)(2,1)S(1)}) custom-call(s32[1]{0:T(128)} %bitcast.place_ref, bf16[32,9,8,128]{3,2,1,0:T(8,128)(2,1)S(1)} %get-tuple-element.49.x0, ...), custom_call_target="tpu_custom_call" | custom-call | flops 1 | bytes 1 | tf_op jit(solution)/shard_map/experts/pallas_call | solution.py:204
  109.6 0.5 collective-permute-start.12
  110.2 0.4 collective-permute-start.15
  110.6 7.1 %collective-permute-done.14 = bf16[32,9,8,128]{3,2,1,0:T(8,128)(2,1)S(1)} collective-permute-done((bf16[32,9,8,128]{3,2,1,0:T(8,128)(2,1)S(1)}, bf16[32,9,8,128]{3,2,1,0:T(8,128)(2,1)S(1)}, u32[]{:S(2)}, u32[]{:S(2)}) %collective-permute-start.14) | collective-permute-done | bytes 589856 | tf_op jit(solution)/shard_map/ppermute | solution.py:412
  118.2 14.0 %collective-permute-done.16.c_ref = bf16[32,9,8,128]{3,2,1,0:T(8,128)(2,1)S(1)} collective-permute-done((bf16[32,9,8,128]{3,2,1,0:T(8,128)(2,1)S(1)}, bf16[32,9,8,128]{3,2,1,0:T(8,128)(2,1)S(1)}, u32[]{:S(2)}, u32[]{:S(2)}) %collective-permute-start.16) | collective-permute-done | bytes 589856 | tf_op jit(solution)/shard_map/ppermute | solution.py:412
  132.2 1.3 total.1
  133.5 8.8 %all-to-all-start.1 = ((bf16[64,9,8,128]{3,2,1,0:T(8,128)(2,1)}), bf16[64,9,8,128]{3,2,1,0:T(8,128)(2,1)S(1)}, u32[]{:S(2)}, u32[]{:S(2)}) async-start(bf16[64,9,8,128]{3,2,1,0:T(8,128)(2,1)} %total.1), calls=%async_computation.1 | async-start | bytes 2359296 | tf_op jit(solution)/shard_map/all_to_all | solution.py:421
  142.3 3.6 %all-gather.2.cloned.1.call-done = bf16[7168,640]{1,0:T(8,128)(2,1)} async-done(((bf16[224,640]{1,0:T(8,128)(2,1)}), bf16[7168,640]{1,0:T(8,128)(2,1)}) %all-gather.2.cloned.1.call-update) | async-done | bytes 9175056 | tf_op jit(solution)/shard_map/all_gather | solution.py:372
  145.9 9.1 %dense.1 = (bf16[2,64,3584]{2,1,0:T(8,128)(2,1)}, bf16[2,64,3584]{2,1,0:T(8,128)(2,1)}) custom-call(bf16[128,3584]{1,0:T(8,128)(2,1)} %copy-done.5, bf16[128,3584]{1,0:T(8,128)(2,1)} %copy-done.6, bf16[8,4,2,2,56,640]{5,4,3,2,1,0:T(8,128)(2,1)} %bitcast.13), custom_call_target="tpu_custom_call" | custom-call | flops 1 | bytes 1 | tf_op jit(solution)/shard_map/dense/pallas_call | solution.py:305
  155.0 1.5 collective-permute-start.18
  156.5 2.3 %collective-permute-done.18.got_ref = bf16[2,64,3584]{2,1,0:T(8,128)(2,1)S(1)} collective-permute-done((bf16[2,64,3584]{2,1,0:T(8,128)(2,1)}, bf16[2,64,3584]{2,1,0:T(8,128)(2,1)S(1)}, u32[]{:S(2)}, u32[]{:S(2)}) %collective-permute-start.18) | collective-permute-done | bytes 917536 | tf_op jit(solution)/shard_map/ppermute | solution.py:353
  158.8 2.0 %fusion = bf16[64,3584]{1,0:T(8,128)(2,1)} fusion(bf16[2,64,3584]{2,1,0:T(8,128)(2,1)S(1)} %collective-permute-done.18.got_ref, bf16[2,64,3584]{2,1,0:T(8,128)(2,1)} %get-tuple-element.64.mine_ref), kind=kLoop, calls=%fused_computation.4 | loop fusion | flops 917504 | bytes 1376256 | tf_op jit(solution)/shard_map/convert_element_type | solution.py:354
  160.7 4.2 %collective-permute-start.19 = (bf16[64,3584]{1,0:T(8,128)(2,1)}, bf16[64,3584]{1,0:T(8,128)(2,1)S(1)}, u32[]{:S(2)}, u32[]{:S(2)}) collective-permute-start(bf16[64,3584]{1,0:T(8,128)(2,1)} %fusion), channel_id=1, source_target_pairs={{0,2},{2,0},{1,3},{3,1},{4,6},{6,4},{5,7},{7,5},{8,10},{10,8},{9,1... | collective-permute-start | bytes 1376264 | tf_op jit(solution)/shard_map/ppermute | solution.py:355
  165.0 6.8 %all-to-all-done.1.x_ref = bf16[64,9,8,128]{3,2,1,0:T(8,128)(2,1)S(1)} async-done(((bf16[64,9,8,128]{3,2,1,0:T(8,128)(2,1)}), bf16[64,9,8,128]{3,2,1,0:T(8,128)(2,1)S(1)}, u32[]{:S(2)}, u32[]{:S(2)}) %all-to-all-start.1) | async-done | bytes 1179680 | tf_op jit(solution)/shard_map/all_to_all | solution.py:421
  171.8 1.1 combine.1
  173.0 3.8 %collective-permute-start.21 = (bf16[64,896]{1,0:T(8,128)(2,1)S(1)}, bf16[64,896]{1,0:T(8,128)(2,1)S(1)}, u32[]{:S(2)}, u32[]{:S(2)}) collective-permute-start(bf16[64,896]{1,0:T(8,128)(2,1)S(1)} %get-tuple-element.69), channel_id=1, source_target_pairs={{0,1},{1,0},{2,3},{3,2},{4,5},{5,4},{6,7},{7,6},{8,9},{9,8},{10,11... | collective-permute-start | bytes 344072 | tf_op jit(solution)/shard_map/ppermute | solution.py:343
  176.8 1.5 collective-permute-start.22
  178.3 2.3 %collective-permute-done.20.r1 = bf16[64,896]{1,0:T(8,128)(2,1)S(1)} collective-permute-done((bf16[64,896]{1,0:T(8,128)(2,1)S(1)}, bf16[64,896]{1,0:T(8,128)(2,1)S(1)}, u32[]{:S(2)}, u32[]{:S(2)}) %collective-permute-start.20) | collective-permute-done | bytes 114720 | tf_op jit(solution)/shard_map/ppermute | solution.py:343
  180.6 3.0 %collective-permute-done.22.r3 = bf16[64,896]{1,0:T(8,128)(2,1)S(1)} collective-permute-done((bf16[64,896]{1,0:T(8,128)(2,1)S(1)}, bf16[64,896]{1,0:T(8,128)(2,1)S(1)}, u32[]{:S(2)}, u32[]{:S(2)}) %collective-permute-start.22) | collective-permute-done | bytes 114720 | tf_op jit(solution)/shard_map/ppermute | solution.py:343
  183.6 2.1 %finish.1 = bf16[64,3584]{1,0:T(8,128)(2,1)} custom-call(s32[1]{0:T(128)} %bitcast.place_ref, bf16[64,3584]{1,0:T(8,128)(2,1)} %tokens_ref.3, bf16[2,64,3584]{2,1,0:T(8,128)(2,1)S(1)} %copy-done.4, bf16[2,64,3584]{2,1,0:T(8,128)(2,1)S(1)} %collective-permute-done.18.got_ref, bf16[64,3584]{1,0:T(8,128)(2,1)S(1)} %collective-permute-done.19.last_ref, ...), custom_call_target="tpu_custom_call" | custom-call | flops 1 | bytes 1 | tf_op jit(solution)/shard_map/finish/pallas_call | solution.py:331
  (37 shorter events, 1.3 us)
Async XLA Ops:
  8.3 5.9 %collective-permute-start = (bf16[80,896]{1,0:T(8,128)(2,1)S(1)}, bf16[80,896]{1,0:T(8,128)(2,1)S(1)}, u32[]{:S(2)}, u32[]{:S(2)}) collective-permute-start(bf16[80,896]{1,0:T(8,128)(2,1)S(1)} %get-tuple-element.39), channel_id=1, source_target_pairs={{0,2},{2,0},{1,3},{3,1},{4,6},{6,4},{5,7},{7,5},{8,10},{10,8},{9,1... | collective-permute-start | bytes 430088 | tf_op jit(solution)/shard_map/ppermute | solution.py:343
  10.4 3.8 %collective-permute-start.1 = (bf16[80,896]{1,0:T(8,128)(2,1)S(1)}, bf16[80,896]{1,0:T(8,128)(2,1)S(1)}, u32[]{:S(2)}, u32[]{:S(2)}) collective-permute-start(bf16[80,896]{1,0:T(8,128)(2,1)S(1)} %get-tuple-element.40), channel_id=1, source_target_pairs={{0,1},{1,0},{2,3},{3,2},{4,5},{5,4},{6,7},{7,6},{8,9},{9,8},{10,11... | collective-permute-start | bytes 430088 | tf_op jit(solution)/shard_map/ppermute | solution.py:343
  11.7 7.2 %collective-permute-start.2 = (bf16[80,896]{1,0:T(8,128)(2,1)S(1)}, bf16[80,896]{1,0:T(8,128)(2,1)S(1)}, u32[]{:S(2)}, u32[]{:S(2)}) collective-permute-start(bf16[80,896]{1,0:T(8,128)(2,1)S(1)} %get-tuple-element.41), channel_id=1, source_target_pairs={{0,3},{3,0},{1,2},{2,1},{4,7},{7,4},{5,6},{6,5},{8,11},{11,8},{9,1... | collective-permute-start | bytes 430088 | tf_op jit(solution)/shard_map/ppermute | solution.py:343
  18.9 17.4 %collective-permute-start.17 = (bf16[112,640]{1,0:T(8,128)(2,1)S(1)}, bf16[112,640]{1,0:T(8,128)(2,1)S(1)}, u32[]{:S(2)}, u32[]{:S(2)}) collective-permute-start(bf16[112,640]{1,0:T(8,128)(2,1)S(1)} %pad_maximum_fusion.1), channel_id=1, source_target_pairs={{0,128},{4,132},{8,136},{12,140},{16,144},{20,148},{24,152},{28,15... | collective-permute-start | bytes 430088 | tf_op jit(solution)/shard_map/ppermute | solution.py:367
  20.5 16.6 %collective-permute-start.3 = (bf16[64,3584]{1,0:T(8,128)(2,1)}, bf16[64,3584]{1,0:T(8,128)(2,1)S(1)}, u32[]{:S(2)}, u32[]{:S(2)}) collective-permute-start(bf16[64,3584]{1,0:T(8,128)(2,1)} %tokens_ref.3), channel_id=1, source_target_pairs={{0,2},{2,0},{1,3},{3,1},{4,6},{6,4},{5,7},{7,5},{8,10},{10,8},{9,1... | collective-permute-start | bytes 1376264 | tf_op jit(solution)/shard_map/ppermute | solution.py:391
  22.8 46.6 %all-to-all-start = ((bf16[64,9,8,128]{3,2,1,0:T(8,128)(2,1)}), bf16[64,9,8,128]{3,2,1,0:T(8,128)(2,1)}, u32[]{:S(2)}, u32[]{:S(2)}) async-start(bf16[64,9,8,128]{3,2,1,0:T(8,128)(2,1)} %get-tuple-element.42), calls=%async_computation | async-start | bytes 2359296 | tf_op jit(solution)/shard_map/all_to_all | solution.py:393
  36.3 109.6 %all-gather.2.cloned.1.call-start = ((), (), s32[]{:S(2)}) async-start(), calls=%async_computation.2 | async-start | bytes 9461760 | tf_op jit(solution)/shard_map/all_gather | solution.py:372
  38.3 32.5 %copy-start.5 = (bf16[128,3584]{1,0:T(8,128)(2,1)}, bf16[128,3584]{1,0:T(8,128)(2,1)S(1)}, u32[]{:S(2)}) copy-start(bf16[128,3584]{1,0:T(8,128)(2,1)S(1)} %pair_up.1.x_mine) | copy-start | bytes 2752516
  38.3 2.6 %collective-permute-start.4 = (bf16[128,3584]{1,0:T(8,128)(2,1)S(1)}, bf16[128,3584]{1,0:T(8,128)(2,1)S(1)}, u32[]{:S(2)}, u32[]{:S(2)}) collective-permute-start(bf16[128,3584]{1,0:T(8,128)(2,1)S(1)} %pair_up.1.x_mine), channel_id=1, source_target_pairs={{0,1},{1,0},{2,3},{3,2},{4,5},{5,4},{6,7},{7,6},{8,9},{9,8},{10,11... | collective-permute-start | bytes 2752520 | tf_op jit(solution)/shard_map/ppermute | solution.py:394
  40.8 29.9 %copy-start.6 = (bf16[128,3584]{1,0:T(8,128)(2,1)}, bf16[128,3584]{1,0:T(8,128)(2,1)S(1)}, u32[]{:S(2)}) copy-start(bf16[128,3584]{1,0:T(8,128)(2,1)S(1)} %collective-permute-done.4.x_others) | copy-start | bytes 2752516
  70.8 11.6 %collective-permute-start.5 = (bf16[32,9,8,128]{3,2,1,0:T(8,128)(2,1)S(1)}, bf16[32,9,8,128]{3,2,1,0:T(8,128)(2,1)S(1)}, u32[]{:S(2)}, u32[]{:S(2)}) collective-permute-start(bf16[32,9,8,128]{3,2,1,0:T(8,128)(2,1)S(1)} %get-tuple-element.71.x0), channel_id=1, source_target_pairs={{0,2},{2,0},{1,3},{3,1},{4,6},{6,4},{5,7},{7,5},{8,10},{10,8},{9,1... | collective-permute-start | bytes 1769480 | tf_op jit(solution)/shard_map/ppermute | solution.py:402
  70.9 15.7 %collective-permute-start.6 = (bf16[32,9,8,128]{3,2,1,0:T(8,128)(2,1)S(1)}, bf16[32,9,8,128]{3,2,1,0:T(8,128)(2,1)S(1)}, u32[]{:S(2)}, u32[]{:S(2)}) collective-permute-start(bf16[32,9,8,128]{3,2,1,0:T(8,128)(2,1)S(1)} %get-tuple-element.71.x0), channel_id=1, source_target_pairs={{0,1},{1,0},{2,3},{3,2},{4,5},{5,4},{6,7},{7,6},{8,9},{9,8},{10,11... | collective-permute-start | bytes 1769480 | tf_op jit(solution)/shard_map/ppermute | solution.py:347
  82.3 5.9 %collective-permute-start.7 = (bf16[32,9,8,128]{3,2,1,0:T(8,128)(2,1)S(1)}, bf16[32,9,8,128]{3,2,1,0:T(8,128)(2,1)S(1)}, u32[]{:S(2)}, u32[]{:S(2)}) collective-permute-start(bf16[32,9,8,128]{3,2,1,0:T(8,128)(2,1)S(1)} %collective-permute-done.5.x1), channel_id=1, source_target_pairs={{0,1},{1,0},{2,3},{3,2},{4,5},{5,4},{6,7},{7,6},{8,9},{9,8},{10,11... | collective-permute-start | bytes 1769480 | tf_op jit(solution)/shard_map/ppermute | solution.py:348
  86.6 15.1 %collective-permute-start.9 = (bf16[32,9,8,128]{3,2,1,0:T(8,128)(2,1)S(1)}, bf16[32,9,8,128]{3,2,1,0:T(8,128)(2,1)S(1)}, u32[]{:S(2)}, u32[]{:S(2)}) collective-permute-start(bf16[32,9,8,128]{3,2,1,0:T(8,128)(2,1)S(1)} %get-tuple-element.49.x0), channel_id=1, source_target_pairs={{0,2},{2,0},{1,3},{3,1},{4,6},{6,4},{5,7},{7,5},{8,10},{10,8},{9,1... | collective-permute-start | bytes 1769480 | tf_op jit(solution)/shard_map/ppermute | solution.py:402
  88.2 2.3 %copy-start = (bf16[1,3584,640]{2,1,0:T(8,128)(2,1)S(1)}, bf16[1,3584,640]{2,1,0:T(8,128)(2,1)}, u32[]{:S(2)}) copy-start(bf16[1,3584,640]{2,1,0:T(8,128)(2,1)} %param.12) | copy-start | bytes 13762564
  90.5 2.3 %copy-start.2 = (bf16[1,640,3584]{2,1,0:T(8,128)(2,1)S(1)}, bf16[1,640,3584]{2,1,0:T(8,128)(2,1)}, u32[]{:S(2)}) copy-start(bf16[1,640,3584]{2,1,0:T(8,128)(2,1)} %param.13) | copy-start | bytes 13762564
  92.8 11.1 %copy-start.1 = (bf16[1,3584,640]{2,1,0:T(8,128)(2,1)S(1)}, bf16[1,3584,640]{2,1,0:T(8,128)(2,1)}, u32[]{:S(2)}) copy-start(bf16[1,3584,640]{2,1,0:T(8,128)(2,1)} %param.12) | copy-start | bytes 13762564
  92.8 11.1 %copy-start.3 = (bf16[1,640,3584]{2,1,0:T(8,128)(2,1)S(1)}, bf16[1,640,3584]{2,1,0:T(8,128)(2,1)}, u32[]{:S(2)}) copy-start(bf16[1,640,3584]{2,1,0:T(8,128)(2,1)} %param.13) | copy-start | bytes 13762564
  98.5 3.9 %collective-permute-start.13 = (bf16[32,9,8,128]{3,2,1,0:T(8,128)(2,1)S(1)}, bf16[32,9,8,128]{3,2,1,0:T(8,128)(2,1)S(1)}, u32[]{:S(2)}, u32[]{:S(2)}) collective-permute-start(bf16[32,9,8,128]{3,2,1,0:T(8,128)(2,1)S(1)} %get-tuple-element.52), channel_id=1, source_target_pairs={{0,1},{1,0},{2,3},{3,2},{4,5},{5,4},{6,7},{7,6},{8,9},{9,8},{10,11... | collective-permute-start | bytes 1769480 | tf_op jit(solution)/shard_map/ppermute | solution.py:406
  99.1 3.5 %collective-permute-start.10 = (bf16[32,9,8,128]{3,2,1,0:T(8,128)(2,1)S(1)}, bf16[32,9,8,128]{3,2,1,0:T(8,128)(2,1)S(1)}, u32[]{:S(2)}, u32[]{:S(2)}) collective-permute-start(bf16[32,9,8,128]{3,2,1,0:T(8,128)(2,1)S(1)} %get-tuple-element.49.x0), channel_id=1, source_target_pairs={{0,1},{1,0},{2,3},{3,2},{4,5},{5,4},{6,7},{7,6},{8,9},{9,8},{10,11... | collective-permute-start | bytes 1769480 | tf_op jit(solution)/shard_map/ppermute | solution.py:347
  101.7 2.3 %collective-permute-start.11 = (bf16[32,9,8,128]{3,2,1,0:T(8,128)(2,1)S(1)}, bf16[32,9,8,128]{3,2,1,0:T(8,128)(2,1)S(1)}, u32[]{:S(2)}, u32[]{:S(2)}) collective-permute-start(bf16[32,9,8,128]{3,2,1,0:T(8,128)(2,1)S(1)} %collective-permute-done.9.x1), channel_id=1, source_target_pairs={{0,1},{1,0},{2,3},{3,2},{4,5},{5,4},{6,7},{7,6},{8,9},{9,8},{10,11... | collective-permute-start | bytes 1769480 | tf_op jit(solution)/shard_map/ppermute | solution.py:348
  102.5 15.2 %collective-permute-start.14 = (bf16[32,9,8,128]{3,2,1,0:T(8,128)(2,1)S(1)}, bf16[32,9,8,128]{3,2,1,0:T(8,128)(2,1)S(1)}, u32[]{:S(2)}, u32[]{:S(2)}) collective-permute-start(bf16[32,9,8,128]{3,2,1,0:T(8,128)(2,1)S(1)} %add_convert_fusion.2), channel_id=1, source_target_pairs={{0,2},{2,0},{1,3},{3,1},{4,6},{6,4},{5,7},{7,5},{8,10},{10,8},{9,1... | collective-permute-start | bytes 1769480 | tf_op jit(solution)/shard_map/ppermute | solution.py:412
  109.6 8.1 %collective-permute-start.12 = (bf16[32,9,8,128]{3,2,1,0:T(8,128)(2,1)S(1)}, bf16[32,9,8,128]{3,2,1,0:T(8,128)(2,1)S(1)}, u32[]{:S(2)}, u32[]{:S(2)}) collective-permute-start(bf16[32,9,8,128]{3,2,1,0:T(8,128)(2,1)S(1)} %get-tuple-element.50), channel_id=1, source_target_pairs={{0,1},{1,0},{2,3},{3,2},{4,5},{5,4},{6,7},{7,6},{8,9},{9,8},{10,11... | collective-permute-start | bytes 1769480 | tf_op jit(solution)/shard_map/ppermute | solution.py:406
  110.1 7.9 %collective-permute-start.8 = (bf16[32,9,8,128]{3,2,1,0:T(8,128)(2,1)S(1)}, bf16[32,9,8,128]{3,2,1,0:T(8,128)(2,1)S(1)}, u32[]{:S(2)}, u32[]{:S(2)}) collective-permute-start(bf16[32,9,8,128]{3,2,1,0:T(8,128)(2,1)S(1)} %get-tuple-element.48), channel_id=1, source_target_pairs={{0,1},{1,0},{2,3},{3,2},{4,5},{5,4},{6,7},{7,6},{8,9},{9,8},{10,11... | collective-permute-start | bytes 1769480 | tf_op jit(solution)/shard_map/ppermute | solution.py:407
  110.2 8.0 %collective-permute-start.15 = (bf16[32,9,8,128]{3,2,1,0:T(8,128)(2,1)S(1)}, bf16[32,9,8,128]{3,2,1,0:T(8,128)(2,1)S(1)}, u32[]{:S(2)}, u32[]{:S(2)}) collective-permute-start(bf16[32,9,8,128]{3,2,1,0:T(8,128)(2,1)S(1)} %get-tuple-element.56), channel_id=1, source_target_pairs={{0,1},{1,0},{2,3},{3,2},{4,5},{5,4},{6,7},{7,6},{8,9},{9,8},{10,11... | collective-permute-start | bytes 1769480 | tf_op jit(solution)/shard_map/ppermute | solution.py:407
  117.8 14.4 %collective-permute-start.16 = (bf16[32,9,8,128]{3,2,1,0:T(8,128)(2,1)S(1)}, bf16[32,9,8,128]{3,2,1,0:T(8,128)(2,1)S(1)}, u32[]{:S(2)}, u32[]{:S(2)}) collective-permute-start(bf16[32,9,8,128]{3,2,1,0:T(8,128)(2,1)S(1)} %add_convert_fusion), channel_id=1, source_target_pairs={{0,2},{2,0},{1,3},{3,1},{4,6},{6,4},{5,7},{7,5},{8,10},{10,8},{9,1... | collective-permute-start | bytes 1769480 | tf_op jit(solution)/shard_map/ppermute | solution.py:412
  133.5 38.3 %all-to-all-start.1 = ((bf16[64,9,8,128]{3,2,1,0:T(8,128)(2,1)}), bf16[64,9,8,128]{3,2,1,0:T(8,128)(2,1)S(1)}, u32[]{:S(2)}, u32[]{:S(2)}) async-start(bf16[64,9,8,128]{3,2,1,0:T(8,128)(2,1)} %total.1), calls=%async_computation.1 | async-start | bytes 2359296 | tf_op jit(solution)/shard_map/all_to_all | solution.py:421
  155.0 3.8 %collective-permute-start.18 = (bf16[2,64,3584]{2,1,0:T(8,128)(2,1)}, bf16[2,64,3584]{2,1,0:T(8,128)(2,1)S(1)}, u32[]{:S(2)}, u32[]{:S(2)}) collective-permute-start(bf16[2,64,3584]{2,1,0:T(8,128)(2,1)} %get-tuple-element.65), channel_id=1, source_target_pairs={{0,1},{1,0},{2,3},{3,2},{4,5},{5,4},{6,7},{7,6},{8,9},{9,8},{10,11... | collective-permute-start | bytes 2752520 | tf_op jit(solution)/shard_map/ppermute | solution.py:353
  158.8 24.9 %copy-start.4 = (bf16[2,64,3584]{2,1,0:T(8,128)(2,1)S(1)}, bf16[2,64,3584]{2,1,0:T(8,128)(2,1)}, u32[]{:S(2)}) copy-start(bf16[2,64,3584]{2,1,0:T(8,128)(2,1)} %get-tuple-element.64.mine_ref) | copy-start | bytes 2752516
  160.7 22.9 %collective-permute-start.19 = (bf16[64,3584]{1,0:T(8,128)(2,1)}, bf16[64,3584]{1,0:T(8,128)(2,1)S(1)}, u32[]{:S(2)}, u32[]{:S(2)}) collective-permute-start(bf16[64,3584]{1,0:T(8,128)(2,1)} %fusion), channel_id=1, source_target_pairs={{0,2},{2,0},{1,3},{3,1},{4,6},{6,4},{5,7},{7,5},{8,10},{10,8},{9,1... | collective-permute-start | bytes 1376264 | tf_op jit(solution)/shard_map/ppermute | solution.py:355
  172.9 7.7 %collective-permute-start.20 = (bf16[64,896]{1,0:T(8,128)(2,1)S(1)}, bf16[64,896]{1,0:T(8,128)(2,1)S(1)}, u32[]{:S(2)}, u32[]{:S(2)}) collective-permute-start(bf16[64,896]{1,0:T(8,128)(2,1)S(1)} %get-tuple-element.68), channel_id=1, source_target_pairs={{0,2},{2,0},{1,3},{3,1},{4,6},{6,4},{5,7},{7,5},{8,10},{10,8},{9,1... | collective-permute-start | bytes 344072 | tf_op jit(solution)/shard_map/ppermute | solution.py:343
  173.0 7.6 %collective-permute-start.21 = (bf16[64,896]{1,0:T(8,128)(2,1)S(1)}, bf16[64,896]{1,0:T(8,128)(2,1)S(1)}, u32[]{:S(2)}, u32[]{:S(2)}) collective-permute-start(bf16[64,896]{1,0:T(8,128)(2,1)S(1)} %get-tuple-element.69), channel_id=1, source_target_pairs={{0,1},{1,0},{2,3},{3,2},{4,5},{5,4},{6,7},{7,6},{8,9},{9,8},{10,11... | collective-permute-start | bytes 344072 | tf_op jit(solution)/shard_map/ppermute | solution.py:343
  176.8 6.9 %collective-permute-start.22 = (bf16[64,896]{1,0:T(8,128)(2,1)S(1)}, bf16[64,896]{1,0:T(8,128)(2,1)S(1)}, u32[]{:S(2)}, u32[]{:S(2)}) collective-permute-start(bf16[64,896]{1,0:T(8,128)(2,1)S(1)} %get-tuple-element.70), channel_id=1, source_target_pairs={{0,3},{3,0},{1,2},{2,1},{4,7},{7,4},{5,6},{6,5},{8,11},{11,8},{9,1... | collective-permute-start | bytes 344072 | tf_op jit(solution)/shard_map/ppermute | solution.py:343
Sparse Core Ops, SparseCore 0:
  39.7 106.1 all-gather.1
